TPU v7x, 128 devices: a whole 4x4x4 slice. The times are simulated.
128 devices in a mesh: ctx: 2 (over y_hi), fsdp: 64 (over y_lo, x, z, core).
Axes of the slice: x: 4, y: 4 (y_hi: 2, y_lo: 2; y = y_hi * 2 + y_lo), z: 4, core: 2. Of those that a mesh axis runs over, the one named last changes fastest.
Arguments:
- layer_in: bfloat16 [64, 256, 2048], P('fsdp', 'ctx'), may hold values from -6 to 6
- segment: int32 [64, 256], P('fsdp'), may hold values from 0 to 4, as said below
- position: int32 [64, 256], P('fsdp'), may hold values from 0 to 159, as said below
- first_gain: bfloat16 [2048], P(('ctx', 'fsdp')), may hold values from 0.5 to 1.5
- first_shift: bfloat16 [2048], P(('ctx', 'fsdp')), may hold values from -1.5 to 1.5
- attend_weight: bfloat16 [2048, 6144], P(('ctx', 'fsdp')), may hold values from -0.125 to 0.125
- attend_bias: bfloat16 [6144], P(('ctx', 'fsdp')), may hold values from -2.5 to 2.5
- output_weight: bfloat16 [2048, 2048], P(('ctx', 'fsdp')), may hold values from -1 to 1
- second_gain: bfloat16 [2048], P(('ctx', 'fsdp')), may hold values from 0.5 to 1.5
- second_shift: bfloat16 [2048], P(('ctx', 'fsdp')), may hold values from -1.5 to 1.5
- gate_weight: bfloat16 [2048, 5632], P(('ctx', 'fsdp')), may hold values from -0.125 to 0.125
- up_weight: bfloat16 [2048, 5632], P(('ctx', 'fsdp')), may hold values from -0.125 to 0.125
- down_weight: bfloat16 [5632, 2048], P(('ctx', 'fsdp')), may hold values from -0.078125 to 0.078125
- cotangent: bfloat16 [64, 256, 2048], P('fsdp', 'ctx'), may hold values from -6 to 6
Outputs:
- layer_out: bfloat16 [64, 256, 2048], P('fsdp', 'ctx')
- input_grad: bfloat16 [64, 256, 2048], P('fsdp', 'ctx')
- first_gain_grad: float32 [2048], P(('ctx', 'fsdp'))
- first_shift_grad: float32 [2048], P(('ctx', 'fsdp'))
- attend_weight_grad: float32 [2048, 6144], P(('ctx', 'fsdp'))
- attend_bias_grad: float32 [6144], P(('ctx', 'fsdp'))
- output_weight_grad: float32 [2048, 2048], P(('ctx', 'fsdp'))
- second_gain_grad: float32 [2048], P(('ctx', 'fsdp'))
- second_shift_grad: float32 [2048], P(('ctx', 'fsdp'))
- gate_weight_grad: float32 [2048, 5632], P(('ctx', 'fsdp'))
- up_weight_grad: float32 [2048, 5632], P(('ctx', 'fsdp'))
- down_weight_grad: float32 [5632, 2048], P(('ctx', 'fsdp'))
Inputs may be any that keep to these rules, and one draw needn't show every extreme that they name: Within each group the tokens fall in aligned blocks of 32: segment 0 is the prompt of 128 tokens, segments 1 to 4 are continuations of 32 tokens each, one block each; each index of ctx holds an equal share of the prompt's blocks and of the continuations, in an order drawn from the seed. A prompt token's position is its place in the prompt; a continuation token's is 128 plus its place in its continuation; positions rise by one within a block.
All inputs are finite; a program needn't handle non-finite values.
Results may differ from a plain program's by a relative error of at most 0.015.
Values may be sent and summed in bfloat16 or wider, within the bound.
No kernel may reach another device: no remote copies, remote signals or barrier semaphores. Data moves between devices by JAX's collectives and lax.ppermute only.
A program may use at most 512 MiB of HBM per device.

v0:
```python
import math

import jax
import jax.numpy as jnp
from jax import lax
from jax.sharding import PartitionSpec as P

HEADS = 32
HD = 64
D = 2048
ROT = 16


EPS_NORM = 1e-05


def frequencies():
    index = jnp.arange(ROT // 2, dtype=jnp.float32)
    return jnp.exp(index * (-2.0 * math.log(10000.0) / ROT))


def rotate(tensor, cosine, sine):
    half_rot = ROT // 2
    first_part = tensor[..., :half_rot]
    second_part = tensor[..., half_rot:ROT]
    cos_wide = cosine[:, None, :]
    sin_wide = sine[:, None, :]
    return jnp.concatenate(
        [
            first_part * cos_wide - second_part * sin_wide,
            second_part * cos_wide + first_part * sin_wide,
            tensor[..., ROT:],
        ],
        axis=-1,
    )


def normalize(tok_rows, gain, shift):
    mean_val = jnp.mean(tok_rows, axis=-1, keepdims=True)
    centred = tok_rows - mean_val
    variance = jnp.mean(centred * centred, axis=-1, keepdims=True)
    inv_std = lax.rsqrt(variance + EPS_NORM)
    normed = centred * inv_std
    return (normed, inv_std, normed * gain + shift)


def norm_back(grad_h, normed, inv_std, gain):
    grad_n = grad_h * gain
    return inv_std * (
        grad_n
        - jnp.mean(grad_n, axis=-1, keepdims=True)
        - normed * jnp.mean(grad_n * normed, axis=-1, keepdims=True)
    )


def on_device(
    layer_in,
    segment,
    position,
    first_gain,
    first_shift,
    attend_weight,
    attend_bias,
    output_weight,
    second_gain,
    second_shift,
    gate_weight,
    up_weight,
    down_weight,
    cotangent,
):
    f32 = jnp.float32
    bf16 = jnp.bfloat16
    tok_count = layer_in.shape[1]
    offset = lax.axis_index("ctx") * tok_count
    seg_all = segment[0]
    pos_all = position[0]
    seg_mine = lax.dynamic_slice_in_dim(seg_all, offset, tok_count)
    pos_mine = lax.dynamic_slice_in_dim(pos_all, offset, tok_count)
    angles = pos_mine.astype(f32)[:, None] * frequencies()[None, :]
    cosine = jnp.cos(angles)
    sine = jnp.sin(angles)
    allowed = (pos_all[None, :] <= pos_mine[:, None]) & (
        (seg_all[None, :] == 0) | (seg_all[None, :] == seg_mine[:, None])
    )
    tokens_in = layer_in[0].astype(f32)
    joined_w, joined_b, out_w, gain_one, shift_one = (
        lax.all_gather(attend_weight, ("ctx", "fsdp"), axis=0, tiled=True),
        lax.all_gather(attend_bias, ("ctx", "fsdp"), axis=0, tiled=True),
        lax.all_gather(output_weight, ("ctx", "fsdp"), axis=0, tiled=True),
        lax.all_gather(first_gain, ("ctx", "fsdp"), axis=0, tiled=True),
        lax.all_gather(first_shift, ("ctx", "fsdp"), axis=0, tiled=True),
    )
    gain_one_f = gain_one.astype(f32)
    normed1, inv_std1, pre_one = normalize(tokens_in, gain_one_f, shift_one.astype(f32))
    hidden1 = pre_one.astype(bf16)
    projected = jnp.dot(hidden1, joined_w, preferred_element_type=f32) + joined_b.astype(f32)
    shaped = projected.reshape(tok_count, 3, HEADS, HD)
    queries = rotate(shaped[:, 0], cosine, sine).astype(bf16)
    keys_mine = rotate(shaped[:, 1], cosine, sine).astype(bf16)
    values_mine = shaped[:, 2].astype(bf16)
    keys_flat, values_flat = (
        lax.all_gather(keys_mine.reshape(tok_count, D), "ctx", axis=0, tiled=True),
        lax.all_gather(values_mine.reshape(tok_count, D), "ctx", axis=0, tiled=True),
    )
    group_rows = keys_flat.shape[0]
    keys_all = keys_flat.reshape(group_rows, HEADS, HD)
    values_all = values_flat.reshape(group_rows, HEADS, HD)
    scores = jnp.einsum("qhd,khd->hqk", queries, keys_all, preferred_element_type=f32) * 0.125
    scores = jnp.where(allowed[None], scores, -1e30)
    top_val = jnp.max(scores, axis=-1, keepdims=True)
    expo = jnp.exp(scores - top_val)
    probs = expo / jnp.sum(expo, axis=-1, keepdims=True)
    probs_low = probs.astype(bf16)
    attended = jnp.einsum("hqk,khd->qhd", probs_low, values_all, preferred_element_type=f32)
    mixed = attended.reshape(tok_count, D).astype(bf16)
    resid = tokens_in + jnp.dot(mixed, out_w, preferred_element_type=f32)
    gate_w, up_w, down_w, gain_two, shift_two = (
        lax.all_gather(gate_weight, ("ctx", "fsdp"), axis=0, tiled=True),
        lax.all_gather(up_weight, ("ctx", "fsdp"), axis=0, tiled=True),
        lax.all_gather(down_weight, ("ctx", "fsdp"), axis=0, tiled=True),
        lax.all_gather(second_gain, ("ctx", "fsdp"), axis=0, tiled=True),
        lax.all_gather(second_shift, ("ctx", "fsdp"), axis=0, tiled=True),
    )
    normed2, inv_std2, pre_two = normalize(resid, gain_two.astype(f32), shift_two.astype(f32))
    hidden2 = pre_two.astype(bf16)
    gate_val = jnp.dot(hidden2, gate_w, preferred_element_type=f32)
    up_val = jnp.dot(hidden2, up_w, preferred_element_type=f32)
    sigmoid_gate = jax.nn.sigmoid(gate_val)
    activated = gate_val * sigmoid_gate
    product = (activated * up_val).astype(bf16)
    result = resid + jnp.dot(product, down_w, preferred_element_type=f32)
    layer_out = result.astype(bf16)[None]
    gate_back, up_back, down_back, gain_two_back = (
        lax.all_gather(gate_weight, ("ctx", "fsdp"), axis=0, tiled=True),
        lax.all_gather(up_weight, ("ctx", "fsdp"), axis=0, tiled=True),
        lax.all_gather(down_weight, ("ctx", "fsdp"), axis=0, tiled=True),
        lax.all_gather(second_gain, ("ctx", "fsdp"), axis=0, tiled=True),
    )
    grad_top = cotangent[0]
    down_grad = jnp.einsum("tf,td->fd", product, grad_top, preferred_element_type=f32)
    grad_prod = jnp.einsum("td,fd->tf", grad_top, down_back, preferred_element_type=f32)
    grad_gate = (
        grad_prod * up_val * sigmoid_gate * (1.0 + gate_val * (1.0 - sigmoid_gate))
    ).astype(bf16)
    grad_up = (grad_prod * activated).astype(bf16)
    gate_grad = jnp.einsum("td,tf->df", hidden2, grad_gate, preferred_element_type=f32)
    up_grad = jnp.einsum("td,tf->df", hidden2, grad_up, preferred_element_type=f32)
    grad_h2 = jnp.einsum(
        "tf,df->td", grad_gate, gate_back, preferred_element_type=f32
    ) + jnp.einsum("tf,df->td", grad_up, up_back, preferred_element_type=f32)
    gain_two_grad = jnp.sum(grad_h2 * normed2, axis=0)
    shift_two_grad = jnp.sum(grad_h2, axis=0)
    grad_resid = grad_top.astype(f32) + norm_back(
        grad_h2, normed2, inv_std2, gain_two_back.astype(f32)
    )
    mlp_shares = (
        lax.psum_scatter(gate_grad, ("ctx", "fsdp"), scatter_dimension=0, tiled=True),
        lax.psum_scatter(up_grad, ("ctx", "fsdp"), scatter_dimension=0, tiled=True),
        lax.psum_scatter(down_grad, ("ctx", "fsdp"), scatter_dimension=0, tiled=True),
        lax.psum_scatter(gain_two_grad, ("ctx", "fsdp"), scatter_dimension=0, tiled=True),
        lax.psum_scatter(shift_two_grad, ("ctx", "fsdp"), scatter_dimension=0, tiled=True),
    )
    joined_back, out_back, gain_one_back = (
        lax.all_gather(attend_weight, ("ctx", "fsdp"), axis=0, tiled=True),
        lax.all_gather(output_weight, ("ctx", "fsdp"), axis=0, tiled=True),
        lax.all_gather(first_gain, ("ctx", "fsdp"), axis=0, tiled=True),
    )
    gain_one_back = gain_one_back.astype(f32)
    grad_branch = grad_resid.astype(bf16)
    out_grad = jnp.einsum("td,te->de", mixed, grad_branch, preferred_element_type=f32)
    grad_mixed = (
        jnp.einsum("te,de->td", grad_branch, out_back, preferred_element_type=f32)
        .astype(bf16)
        .reshape(tok_count, HEADS, HD)
    )
    grad_probs = jnp.einsum("qhd,khd->hqk", grad_mixed, values_all, preferred_element_type=f32)
    grad_values_all = jnp.einsum("hqk,qhd->khd", probs_low, grad_mixed, preferred_element_type=f32)
    row_dot = jnp.sum(probs * grad_probs, axis=-1, keepdims=True)
    grad_scores = (probs * (grad_probs - row_dot)).astype(bf16)
    grad_queries = (
        jnp.einsum("hqk,khd->qhd", grad_scores, keys_all, preferred_element_type=f32) * 0.125
    )
    grad_keys_all = (
        jnp.einsum("hqk,qhd->khd", grad_scores, queries, preferred_element_type=f32) * 0.125
    )
    grad_keys, grad_values = (
        lax.psum_scatter(
            grad_keys_all.reshape(group_rows, D).astype(jnp.bfloat16),
            "ctx",
            scatter_dimension=0,
            tiled=True,
        ).astype(jnp.float32),
        lax.psum_scatter(
            grad_values_all.reshape(group_rows, D).astype(jnp.bfloat16),
            "ctx",
            scatter_dimension=0,
            tiled=True,
        ).astype(jnp.float32),
    )
    grad_joined = jnp.concatenate(
        [
            rotate(grad_queries, cosine, -sine).reshape(tok_count, D),
            rotate(grad_keys.reshape(tok_count, HEADS, HD), cosine, -sine).reshape(tok_count, D),
            grad_values,
        ],
        axis=1,
    ).astype(bf16)
    joined_grad = jnp.einsum("td,te->de", hidden1, grad_joined, preferred_element_type=f32)
    bias_grad = jnp.sum(grad_joined.astype(f32), axis=0)
    grad_h1 = jnp.einsum("te,de->td", grad_joined, joined_back, preferred_element_type=f32)
    gain_one_grad = jnp.sum(grad_h1 * normed1, axis=0)
    shift_one_grad = jnp.sum(grad_h1, axis=0)
    input_grad = (grad_resid + norm_back(grad_h1, normed1, inv_std1, gain_one_back)).astype(bf16)[
        None
    ]
    attend_shares = (
        lax.psum_scatter(joined_grad, ("ctx", "fsdp"), scatter_dimension=0, tiled=True),
        lax.psum_scatter(bias_grad, ("ctx", "fsdp"), scatter_dimension=0, tiled=True),
        lax.psum_scatter(out_grad, ("ctx", "fsdp"), scatter_dimension=0, tiled=True),
        lax.psum_scatter(gain_one_grad, ("ctx", "fsdp"), scatter_dimension=0, tiled=True),
        lax.psum_scatter(shift_one_grad, ("ctx", "fsdp"), scatter_dimension=0, tiled=True),
    )
    return (
        layer_out,
        input_grad,
        attend_shares[3],
        attend_shares[4],
        attend_shares[0],
        attend_shares[1],
        attend_shares[2],
        mlp_shares[3],
        mlp_shares[4],
        mlp_shares[0],
        mlp_shares[1],
        mlp_shares[2],
    )


def solution(mesh):
    placed = (
        P("fsdp", "ctx", None),
        P("fsdp", None),
        P("fsdp", None),
        P(("ctx", "fsdp")),
        P(("ctx", "fsdp")),
        P(("ctx", "fsdp"), None),
        P(("ctx", "fsdp")),
        P(("ctx", "fsdp"), None),
        P(("ctx", "fsdp")),
        P(("ctx", "fsdp")),
        P(("ctx", "fsdp"), None),
        P(("ctx", "fsdp"), None),
        P(("ctx", "fsdp"), None),
        P("fsdp", "ctx", None),
    )
    return jax.shard_map(
        on_device,
        mesh=mesh,
        in_specs=placed,
        out_specs=(
            P("fsdp", "ctx", None),
            P("fsdp", "ctx", None),
            P(("ctx", "fsdp")),
            P(("ctx", "fsdp")),
            P(("ctx", "fsdp"), None),
            P(("ctx", "fsdp")),
            P(("ctx", "fsdp"), None),
            P(("ctx", "fsdp")),
            P(("ctx", "fsdp")),
            P(("ctx", "fsdp"), None),
            P(("ctx", "fsdp"), None),
            P(("ctx", "fsdp"), None),
        ),
        check_vma=False,
    )
```

profile of v0, /device:TPU:1, one launch (start us, length us, event | category | flops | bytes accessed | tf_op | source)
XLA Modules:
  0.0 3065.0 jit_solution(4728885240396829539)
XLA Ops:
  13.0 70.2 %all-reduce.13 = (bf16[6144]{0:T(1024)(128)(2,1)S(1)}, bf16[2048]{0:T(1024)(128)(2,1)S(1)}, bf16[2048]{0:T(1024)(128)(2,1)S(1)}, bf16[2048]{0:T(1024)(128)(2,1)S(1)}, bf16[2048]{0:T(1024)(128)(2,1)S(1)}) all-reduce(bf16[6144]{0:T(1024)(128)(2,1)S(1)} %dynamic-update-slice.2, ...), channel_id=1, replica_groups=mesh['ctx'=2,'fsdp'=64] {'ctx','fsdp'}, use_global_device_ids=true, to_apply=%add.2 | all-reduce | flops 14336 | bytes 57344
  87.2 21.4 all-gather.9.cloned.1.call-done
  108.6 10.3 convolution_add_fusion
  118.9 2.4 copy.33
  124.1 2.1 slice.103
  128.6 75.1 %all-gather.21.cloned.1.call-done = bf16[128,44,2048]{2,1,0:T(8,128)(2,1)} async-done(((bf16[1,44,2048]{2,1,0:T(8,128)(2,1)}), bf16[128,44,2048]{2,1,0:T(8,128)(2,1)}) %all-gather.21.cloned.1.call-update) | async-done | bytes 23068688 | tf_op jit(solution)/shard_map/all_gather | solution.py:121
  203.7 27.3 reshape.292
  231.1 4.7 fusion.46
  235.8 21.4 all-gather.11.cloned.1.call-done
  257.2 3.5 convolution_convert_fusion.2
  260.7 69.3 %all-gather.15.cloned.1.call-done = bf16[2048,2048]{1,0:T(8,128)(2,1)} async-done(((bf16[16,2048]{1,0:T(8,128)(2,1)}), bf16[2048,2048]{1,0:T(8,128)(2,1)}) %all-gather.15.cloned.1.call-update) | async-done | bytes 8388624 | tf_op jit(solution)/shard_map/all_gather | solution.py:90
  330.0 4.7 fusion.47
  335.3 85.0 %all-gather.19.cloned.1.call-done = bf16[2048,5632]{1,0:T(8,128)(2,1)} async-done(((bf16[16,5632]{1,0:T(8,128)(2,1)}), bf16[2048,5632]{1,0:T(8,128)(2,1)}) %all-gather.19.cloned.1.call-update) | async-done | bytes 23068688 | tf_op jit(solution)/shard_map/all_gather | solution.py:120
  420.3 12.4 fusion.49
  432.6 80.0 %all-gather.17.cloned.1.call-done = bf16[2048,5632]{1,0:T(8,128)(2,1)} async-done(((bf16[16,5632]{1,0:T(8,128)(2,1)}), bf16[2048,5632]{1,0:T(8,128)(2,1)}) %all-gather.17.cloned.1.call-update) | async-done | bytes 23068688 | tf_op jit(solution)/shard_map/all_gather | solution.py:119
  512.6 12.3 fusion.48
  525.0 15.2 multiply_convert_fusion.1
  540.1 12.3 fusion.50
  552.4 13.9 multiply_reduce_fusion.1
  568.3 6.6 convolution_convert_fusion
  575.2 4.3 multiply_reduce_fusion
  584.5 4.2 convolution_convert_fusion.1
  588.7 2.3 copy.37
  591.1 8.1 fusion.35
  600.5 2.4 fusion.9
  603.0 5.0 reduce-scatter.21.cloned.1.call-done
  611.2 23.1 reduce-scatter.23.cloned.1.call-done
  638.2 21.8 fusion.41
  660.0 19.5 fusion.52
  679.7 19.3 fusion.51
  700.5 17.9 fusion.29
  718.4 423.2 %fusion = f32[48,2048]{1,0:T(8,128)S(1)} fusion(f32[5632,2048]{1,0:T(8,128)} %fusion.29), kind=kCustom, calls=%all-reduce-scatter | all-reduce-scatter fusion | flops 12582913 | bytes 46530560
  1143.6 2.1 collective-permute-start.9
  1147.7 2.0 collective-permute-start.7
  1151.8 2.1 collective-permute-start.5
  1155.6 2.5 collective-permute-start.4
  1158.1 5.9 collective-permute-done.8
  1164.0 7.7 collective-permute-start.3
  1173.7 6.4 collective-permute-done.6
  1181.4 11.6 collective-permute-start
  1193.0 11.5 fusion.5
  1206.4 30.8 %concatenate.25 = f32[556,2048]{1,0:T(8,128)} concatenate(f32[28,2048]{1,0:T(8,128)} %collective-permute-done.10, f32[48,2048]{1,0:T(8,128)} %collective-permute-done.9, f32[48,2048]{1,0:T(8,128)} %collective-permute-done.8, f32[48,2048]{1,0:T(8,128)} %collective-permute-done.7, f32[48,2048]{1,0:T(8,128)} %collective-permute-done.6, f32[48,2048]{1,0:T(8,128)} %collective-permute-done.5, ...), dimensions={0} | concatenate | bytes 9109504
  1239.5 20.8 fusion.24
  1260.3 97.2 %all-reduce.12 = (f32[2048]{0:T(1024)S(1)}, f32[2048]{0:T(1024)S(1)}, f32[6144]{0:T(1024)S(1)}, f32[2048]{0:T(1024)S(1)}, f32[2048]{0:T(1024)S(1)}) all-reduce(f32[2048]{0:T(1024)S(1)} %get-tuple-element.14, f32[2048]{0:T(1024)S(1)} %get-tuple-element.19, ...), channel_id=4, replica_groups=mesh['ctx'=2,'fsdp'=64] {'ctx','fsdp'}, use_global_device_ids=true, to_apply=%region_14.15.clone | all-reduce | flops 14336 | bytes 114688
  1360.4 2.5 fusion.28
  1363.0 271.6 %reduce-scatter.13.cloned.1.call-done = f32[16,6144]{1,0:T(8,128)} async-done(((f32[2048,6144]{1,0:T(8,128)}), f32[16,6144]{1,0:T(8,128)}) %reduce-scatter.13.cloned.1.call-update) | async-done | bytes 393232 | tf_op jit(solution)/shard_map/reduce_scatter | solution.py:218
  1634.5 711.0 %reduce-scatter.19.cloned.1.call-done = f32[16,5632]{1,0:T(8,128)} async-done(((f32[2048,5632]{1,0:T(8,128)}), f32[16,5632]{1,0:T(8,128)}) %reduce-scatter.19.cloned.1.call-update) | async-done | bytes 360464 | tf_op jit(solution)/shard_map/reduce_scatter | solution.py:159
  2345.5 712.6 %reduce-scatter.17.cloned.1.call-done = f32[16,5632]{1,0:T(8,128)} async-done(((f32[2048,5632]{1,0:T(8,128)}), f32[16,5632]{1,0:T(8,128)}) %reduce-scatter.17.cloned.1.call-update) | async-done | bytes 360464 | tf_op jit(solution)/shard_map/reduce_scatter | solution.py:158
  (198 shorter events, 50.6 us)
Async XLA Ops:
  7.2 101.4 %all-gather.9.cloned.1.call-start = ((), (), s32[]{:S(2)}) async-start(), calls=%async_computation.6 | async-start | bytes 25362432 | tf_op jit(solution)/shard_map/all_gather | solution.py:88
  7.9 195.8 %all-gather.21.cloned.1.call-start = ((), (), s32[]{:S(2)}) async-start(), calls=%async_computation.16 | async-start | bytes 25362432 | tf_op jit(solution)/shard_map/all_gather | solution.py:121
  8.7 222.4 %all-gather.13.cloned.1.call-start = ((), (), s32[]{:S(2)}) async-start(), calls=%async_computation.8 | async-start | bytes 1572864 | tf_op jit(solution)/shard_map/all_gather | solution.py:103
  85.1 33.8 %copy-start.33 = (f32[128]{0:T(128)}, f32[128]{0:T(128)S(1)}, u32[]{:S(2)}) copy-start(f32[128]{0:T(128)S(1)} %broadcast_multiply_fusion.5) | copy-start | bytes 1540
  86.5 32.4 %copy-start.37 = (f32[128]{0:T(128)}, f32[128]{0:T(128)S(1)}, u32[]{:S(2)}) copy-start(f32[128]{0:T(128)S(1)} %add_rsqrt_fusion.1) | copy-start | bytes 1540
  87.2 35.9 %copy-start.31 = (f32[128,8]{0,1:T(8,128)}, f32[128,8]{0,1:T(8,128)S(1)}, u32[]{:S(2)}) copy-start(f32[128,8]{0,1:T(8,128)S(1)} %get-tuple-element.51) | copy-start | bytes 12292
  123.2 107.9 %copy-start.25 = (bf16[128,32,8]{0,2,1:T(8,128)(2,1)}, bf16[128,32,8]{0,2,1:T(8,128)(2,1)S(1)}, u32[]{:S(2)}) copy-start(bf16[128,32,8]{0,2,1:T(8,128)(2,1)S(1)} %get-tuple-element.41) | copy-start | bytes 196612
  123.2 107.9 %copy-start.27 = (bf16[128,32,8]{0,2,1:T(8,128)(2,1)}, bf16[128,32,8]{0,2,1:T(8,128)(2,1)S(1)}, u32[]{:S(2)}) copy-start(bf16[128,32,8]{0,2,1:T(8,128)(2,1)S(1)} %get-tuple-element.42) | copy-start | bytes 196612
  124.1 133.1 %all-gather.11.cloned.1.call-start = ((), (), s32[]{:S(2)}) async-start(), calls=%async_computation.7 | async-start | bytes 1572864 | tf_op jit(solution)/shard_map/all_gather | solution.py:104
  126.3 203.7 %all-gather.15.cloned.1.call-start = ((), (), s32[]{:S(2)}) async-start(), calls=%async_computation.9 | async-start | bytes 8454144 | tf_op jit(solution)/shard_map/all_gather | solution.py:90
  126.9 293.4 %all-gather.19.cloned.1.call-start = ((), (), s32[]{:S(2)}) async-start(), calls=%async_computation.11 | async-start | bytes 23248896 | tf_op jit(solution)/shard_map/all_gather | solution.py:120
  127.4 385.2 %all-gather.17.cloned.1.call-start = ((), (), s32[]{:S(2)}) async-start(), calls=%async_computation.10 | async-start | bytes 23248896 | tf_op jit(solution)/shard_map/all_gather | solution.py:119
  128.2 479.8 %reduce-scatter.21.cloned.1.call-start = ((), (), s32[]{:S(2)}) async-start(), calls=%async_computation.17 | async-start | bytes 1572864
  128.4 206.6 %copy-start.29 = (f32[2048]{0:T(1024)}, f32[2048]{0:T(1024)S(1)}, u32[]{:S(2)}) copy-start(f32[2048]{0:T(1024)S(1)} %convert_element_type.123) | copy-start | bytes 24580
  235.8 24.9 copy-start.39
  257.1 72.8 %copy-start.2 = (bf16[1,128,2048]{2,1,0:T(8,128)(2,1)S(1)}, bf16[1,128,2048]{2,1,0:T(8,128)(2,1)}, u32[]{:S(2)}) copy-start(bf16[1,128,2048]{2,1,0:T(8,128)(2,1)} %param.14) | copy-start | bytes 1572868
  260.7 74.0 %copy-start.14 = (bf16[32,64,128]{2,1,0:T(8,128)(2,1)}, bf16[32,64,128]{2,1,0:T(8,128)(2,1)S(1)}, u32[]{:S(2)}) copy-start(bf16[32,64,128]{2,1,0:T(8,128)(2,1)S(1)} %convolution_convert_fusion.2) | copy-start | bytes 1572868
  334.7 231.6 %copy-start = (f32[128,2048]{1,0:T(8,128)}, f32[128,2048]{1,0:T(8,128)S(1)}, u32[]{:S(2)}) copy-start(f32[128,2048]{1,0:T(8,128)S(1)} %get-tuple-element.55) | copy-start | bytes 3145732
  334.7 97.9 %copy-start.43 = (f32[128]{0:T(128)}, f32[128]{0:T(128)S(1)}, u32[]{:S(2)}) copy-start(f32[128]{0:T(128)S(1)} %broadcast_multiply_fusion.4) | copy-start | bytes 1540
  335.0 97.6 %copy-start.45 = (f32[128]{0:T(128)}, f32[128]{0:T(128)S(1)}, u32[]{:S(2)}) copy-start(f32[128]{0:T(128)S(1)} %add_rsqrt_fusion) | copy-start | bytes 1540
  432.6 92.3 %copy-start.17 = (bf16[1,128,2048]{2,1,0:T(8,128)(2,1)S(1)}, bf16[1,128,2048]{2,1,0:T(8,128)(2,1)}, u32[]{:S(2)}) copy-start(bf16[1,128,2048]{2,1,0:T(8,128)(2,1)} %param.27) | copy-start | bytes 1572868
  584.5 49.8 %reduce-scatter.23.cloned.1.call-start = ((), (), s32[]{:S(2)}) async-start(), calls=%async_computation.18 | async-start | bytes 1572864
  591.1 771.9 %reduce-scatter.15.cloned.1.call-start = ((), (), s32[]{:S(2)}) async-start(), calls=%async_computation.13 | async-start | bytes 16908288 | tf_op jit(solution)/shard_map/reduce_scatter | solution.py:220
  599.3 1035.2 %reduce-scatter.13.cloned.1.call-start = ((), (), s32[]{:S(2)}) async-start(), calls=%async_computation.12 | async-start | bytes 50724864 | tf_op jit(solution)/shard_map/reduce_scatter | solution.py:218
  602.9 32.7 %copy-start.32 = (f32[128,8]{0,1:T(8,128)S(1)}, f32[128,8]{0,1:T(8,128)}, u32[]{:S(2)}) copy-start(f32[128,8]{0,1:T(8,128)} %copy-done.31) | copy-start | bytes 12292
  602.9 32.7 %copy-start.42 = (f32[128,8]{0,1:T(8,128)S(1)}, f32[128,8]{0,1:T(8,128)}, u32[]{:S(2)}) copy-start(f32[128,8]{0,1:T(8,128)} %get-tuple-element.49) | copy-start | bytes 12292
  635.6 24.4 copy-start.8
  636.9 23.1 copy-start.10
  660.0 1685.5 %reduce-scatter.19.cloned.1.call-start = ((), (), s32[]{:S(2)}) async-start(), calls=%async_computation.15 | async-start | bytes 46497792 | tf_op jit(solution)/shard_map/reduce_scatter | solution.py:159
  679.6 2378.4 %reduce-scatter.17.cloned.1.call-start = ((), (), s32[]{:S(2)}) async-start(), calls=%async_computation.14 | async-start | bytes 46497792 | tf_op jit(solution)/shard_map/reduce_scatter | solution.py:158
  718.4 474.6 %copy-start.1 = (f32[128,2048]{1,0:T(8,128)S(1)}, f32[128,2048]{1,0:T(8,128)}, u32[]{:S(2)}) copy-start(f32[128,2048]{1,0:T(8,128)} %copy-done) | copy-start | bytes 3145732
  1141.6 10.2 collective-permute-start.10
  1143.6 12.0 collective-permute-start.9
  1145.7 18.3 collective-permute-start.8
  1147.7 24.7 collective-permute-start.7
  1149.8 30.3 collective-permute-start.6
  1151.8 29.6 collective-permute-start.5
  1155.6 49.0 %collective-permute-start.4 = (f32[48,2048]{1,0:T(8,128)S(1)}, f32[48,2048]{1,0:T(8,128)S(1)}, u32[]{:S(2)}, u32[]{:S(2)}) collective-permute-start(f32[48,2048]{1,0:T(8,128)S(1)} %fusion), channel_id=1, source_target_pairs={{0,5},{1,6},{2,7},{3,8},{4,9},{5,10},{6,11},{7,12},{8,13},{9,14},{... | collective-permute-start | bytes 1179656
  1164.0 40.6 %collective-permute-start.3 = (f32[48,2048]{1,0:T(8,128)S(1)}, f32[48,2048]{1,0:T(8,128)S(1)}, u32[]{:S(2)}, u32[]{:S(2)}) collective-permute-start(f32[48,2048]{1,0:T(8,128)S(1)} %fusion), channel_id=1, source_target_pairs={{0,4},{1,5},{2,6},{3,7},{4,8},{5,9},{6,10},{7,11},{8,12},{9,13},{1... | collective-permute-start | bytes 1179656
  1172.4 32.2 %collective-permute-start.2 = (f32[48,2048]{1,0:T(8,128)S(1)}, f32[48,2048]{1,0:T(8,128)S(1)}, u32[]{:S(2)}, u32[]{:S(2)}) collective-permute-start(f32[48,2048]{1,0:T(8,128)S(1)} %fusion), channel_id=1, source_target_pairs={{0,3},{1,4},{2,5},{3,6},{4,7},{5,8},{6,9},{7,10},{8,11},{9,12},{10... | collective-permute-start | bytes 1179656
  1180.1 24.5 collective-permute-start.1
  1181.4 24.9 collective-permute-start
  1204.5 34.4 %copy-start.9 = (bf16[128,2048]{0,1:T(8,128)(2,1)S(1)}, bf16[128,2048]{0,1:T(8,128)(2,1)}, u32[]{:S(2)}) copy-start(bf16[128,2048]{0,1:T(8,128)(2,1)} %copy-done.8) | copy-start | bytes 1572868
  1204.6 34.4 %copy-start.11 = (bf16[128,32,64]{0,2,1:T(8,128)(2,1)S(1)}, bf16[128,32,64]{0,2,1:T(8,128)(2,1)}, u32[]{:S(2)}) copy-start(bf16[128,32,64]{0,2,1:T(8,128)(2,1)} %copy-done.10) | copy-start | bytes 1572868
  1204.6 34.4 %copy-start.13 = (bf16[128,32,64]{0,2,1:T(8,128)(2,1)S(1)}, bf16[128,32,64]{0,2,1:T(8,128)(2,1)}, u32[]{:S(2)}) copy-start(bf16[128,32,64]{0,2,1:T(8,128)(2,1)} %copy-done.12) | copy-start | bytes 1572868
  1204.6 34.9 %copy-start.34 = (f32[128]{0:T(128)S(1)}, f32[128]{0:T(128)}, u32[]{:S(2)}) copy-start(f32[128]{0:T(128)} %copy-done.33) | copy-start | bytes 1540
  1204.6 34.9 %copy-start.38 = (f32[128]{0:T(128)S(1)}, f32[128]{0:T(128)}, u32[]{:S(2)}) copy-start(f32[128]{0:T(128)} %copy-done.37) | copy-start | bytes 1540
  1239.5 121.0 %copy-start.5 = (f32[128,2048]{1,0:T(8,128)S(1)}, f32[128,2048]{1,0:T(8,128)}, u32[]{:S(2)}) copy-start(f32[128,2048]{1,0:T(8,128)} %copy-done.4) | copy-start | bytes 3145732
  (25 other events, 178.0 us)
Sparse Core Ops, SparseCore 0:
  11.0 97.5 all-gather.8
  111.6 92.1 all-gather.20
  206.0 24.2 all-gather.12
  232.4 24.7 all-gather.10
  260.0 69.9 all-gather.14
  332.8 87.4 all-gather.18
  423.2 89.3 all-gather.16
  584.6 23.3 reduce-scatter.20
  610.5 23.7 reduce-scatter.22
  637.1 682.7 reduce-scatter.14
  1325.9 308.5 reduce-scatter.12
  1637.4 708.0 reduce-scatter.18
  2348.5 709.5 reduce-scatter.16
where the time goes:
time: 3080 us; the launch traced here: 3070 us
  waiting for transfers between devices  2090 us (68%)
  blocking collectives  591 us (19%)
  matrix products  226 us (7%)
  local copies, waits for them, and re-layouts  86.9 us (3%)
  starting transfers between devices  37.4 us (1%)
    reduce_scatter x1, waiting for transfers between devices, on_device(): lax.psum_scatter(gate_grad, ('ctx', 'fsdp'), scatter_dimension=0, tiled=T...  713 us
    reduce_scatter x1, waiting for transfers between devices, on_device(): lax.psum_scatter(up_grad, ('ctx', 'fsdp'), scatter_dimension=0, tiled=True)  711 us
    unnamed x3, blocking collectives  591 us
    reduce_scatter x1, waiting for transfers between devices, on_device(): lax.psum_scatter(joined_grad, ('ctx', 'fsdp'), scatter_dimension=0, tiled...  272 us
    all_gather x1, waiting for transfers between devices, on_device(): lax.all_gather(up_weight, ('ctx', 'fsdp'), axis=0, tiled=True)  85 us
    all_gather x1, waiting for transfers between devices, on_device(): lax.all_gather(gate_weight, ('ctx', 'fsdp'), axis=0, tiled=True)  80 us
    unnamed x121, local copies, waits for them, and re-layouts  79.4 us
    all_gather x1, waiting for transfers between devices, on_device(): lax.all_gather(down_weight, ('ctx', 'fsdp'), axis=0, tiled=True)  75.1 us
  transfers between devices with their start and end apart: 24, of which 15 were waited for; matrix products, arithmetic and copies ran while one was open for 22% of the time, Pallas kernels for 0%

commit v1 on v0

v1 whole, which is shorter than its diff:
```python
import functools
import math

import jax
import jax.numpy as jnp
import numpy as np
from jax import lax
from jax.experimental import pallas as pl
from jax.experimental.pallas import tpu as pltpu
from jax.sharding import Mesh, PartitionSpec as P

HEADS = 32
HD = 64
D = 2048
FF = 5632
ROT = 16
EPS = 1e-05
TOK = 128
NY, NC, NX, NZ = 4, 2, 4, 4
NT = NY * NC
NXZ = NX * NZ
ROWS = D // (NT * NXZ)
FROWS = FF // (NT * NXZ)
FPAD = 48
FT = FPAD * NXZ
HC = D // NT
LH = HC // HD
EXTRA = 128
SIZES = {"yh": 2, "yl": 2, "x": NX, "z": NZ, "c": NC}
AXES = ("yh", "yl", "x", "z", "c")
YC = ("yh", "yl", "c")
XZ = ("x", "z")

f32 = jnp.float32
bf16 = jnp.bfloat16


def shift_perm(axes, deltas):
    sizes = [SIZES[a] for a in axes]
    pairs = []
    for src in range(math.prod(sizes)):
        coord = dict(zip(axes, np.unravel_index(src, sizes)))
        for key, delta in deltas.items():
            if key == "y":
                y = (2 * coord["yh"] + coord["yl"] + delta) % NY
                coord["yh"], coord["yl"] = y // 2, y % 2
            else:
                coord[key] = (coord[key] + delta) % SIZES[key]
        pairs.append((src, int(np.ravel_multi_index([coord[a] for a in axes], sizes))))
    return pairs


def send(value, **deltas):
    axes = tuple(a for a in AXES if a in deltas or (a in ("yh", "yl") and "y" in deltas))
    return lax.ppermute(value, axes, shift_perm(axes, deltas))


class Place:
    def __init__(self):
        yh, yl = lax.axis_index("yh"), lax.axis_index("yl")
        self.c, self.x, self.z = (lax.axis_index(a) for a in ("c", "x", "z"))
        self.y = 2 * yh + yl

    def tensor(self, ry, rc):
        return (self.y + ry) % NY * NC + (self.c ^ rc)

    def row(self, ry, rc):
        y = (self.y + ry) % NY
        return ((y % 2 * NC + (self.c ^ rc)) * 2 + y // 2) * TOK

    def whole(self):
        return ((self.y * NX + self.x) * NZ + self.z) * NC + self.c


EVERY = tuple((r, k) for r in range(NY) for k in range(NC))


def gather_y(own, half):
    from_prev = send(own, y=1)
    from_next = send(own, y=-1)
    top = send(from_prev[:half], y=1)
    bottom = send(from_next[half:], y=-1)
    blocks = {(0, 0): (own,), (1, 0): (from_next,), (3, 0): (from_prev,), (2, 0): (top, bottom)}
    for r in (0, 1, 3, 2):
        blocks[(r, 1)] = tuple(send(b, c=1) for b in blocks[(r, 0)])
    return blocks


def put(blocks, start, shape, axis=0):
    whole = jnp.zeros(shape, bf16)
    for s in EVERY:
        at = 0
        for b in blocks[s]:
            where = [at, 0]
            where[axis] = where[axis] + start(*s)
            whole = lax.dynamic_update_slice(whole, b, tuple(where))
            at += b.shape[0]
    return whole


def gather_rows(own, place):
    return put(gather_y(own, TOK // 2), place.row, (NT * TOK, own.shape[1]))


def reduce_y(total, place):
    part = lambda r, k: lax.dynamic_slice_in_dim(total, place.row(r, k), TOK)
    sums = {}
    half = TOK // 2
    for r in (2, 1, 3, 0):
        other = send(part(r, 1), c=1)
        sums[r] = part(r, 0).astype(f32) + other.astype(f32)
    far = sums[2].astype(bf16)
    top = send(far[:half], y=1)
    bottom = send(far[half:], y=-1)
    one = jnp.concatenate([sums[1][:half] + top.astype(f32), sums[1][half:]], axis=0).astype(bf16)
    three = jnp.concatenate([sums[3][:half], sums[3][half:] + bottom.astype(f32)], axis=0).astype(bf16)
    from_prev = send(one, y=1)
    from_next = send(three, y=-1)
    return sums[0] + from_prev.astype(f32) + from_next.astype(f32)


def all_to_all_y(piece):
    mine = [piece(r, 0) for r in range(NY)]
    other = send(jnp.stack([piece(r, 1) for r in range(NY)]), c=1)
    got = {}
    for r in range(NY):
        pair = jnp.stack([mine[r], other[r]])
        if r:
            pair = send(pair, y=r if r < 3 else -1)
        got[((-r) % NY, 0)] = (pair[0],)
        got[((-r) % NY, 1)] = (pair[1],)
    return got


def to_pi(a):
    n = a.shape[0]
    return a.reshape(n, NY, NXZ, D // NY // NXZ).transpose(0, 2, 1, 3).reshape(n, D)


def from_pi(a):
    n = a.shape[0]
    return a.reshape(n, NXZ, NY, D // NY // NXZ).transpose(0, 2, 1, 3).reshape(n, D)


def norm_stats(rows):
    mean = jnp.mean(rows, axis=-1, keepdims=True)
    centred = rows - mean
    var = jnp.mean(centred * centred, axis=-1, keepdims=True)
    return mean, lax.rsqrt(var + EPS)


def norm_back(grad_h, normed, inv_std, gain):
    grad_n = grad_h * gain
    return inv_std * (
        grad_n
        - jnp.mean(grad_n, axis=-1, keepdims=True)
        - normed * jnp.mean(grad_n * normed, axis=-1, keepdims=True)
    )


GR = 256


def lane_tables(pos):
    lane = lax.broadcasted_iota(jnp.int32, (1, HC), 1) % HD
    index = (lane % (ROT // 2)).astype(f32)
    freq = jnp.exp(index * (-2.0 * math.log(10000.0) / ROT))
    angles = pos * freq
    turned = lane < ROT
    cosine = jnp.where(turned, jnp.cos(angles), 1.0)
    sine = jnp.where(turned, jnp.sin(angles), 0.0)
    return lane < ROT // 2, cosine, sine


def turn(x, first, cosine, sine):
    ahead = pltpu.roll(x, HC - ROT // 2, 1)
    behind = pltpu.roll(x, ROT // 2, 1)
    return x * cosine + jnp.where(first, -ahead, behind) * sine


def dot_t(a, b):
    return lax.dot_general(a, b, (((1,), (1,)), ((), ())), preferred_element_type=f32)


def dot_n(a, b):
    return lax.dot_general(a, b, (((1,), (0,)), ((), ())), preferred_element_type=f32)


def dot_tn(a, b):
    return lax.dot_general(a, b, (((0,), (0,)), ((), ())), preferred_element_type=f32)


def readable(seg_q, pos_q, seg_k, pos_k):
    return (pos_k <= pos_q) & ((seg_k == 0.0) | (seg_k == seg_q))


def softmax_rows(scores):
    top = jnp.max(scores, axis=-1, keepdims=True)
    expo = jnp.exp(scores - top)
    return expo / jnp.sum(expo, axis=-1, keepdims=True)


def attend_kernel(proj_ref, bias_ref, cos_ref, sin_ref, colq_ref, rowk_ref, qkv_ref, mixed_ref):
    lane = lax.broadcasted_iota(jnp.int32, (1, HC), 1)
    first = (lane % HD) < ROT // 2
    cosine, sine = cos_ref[...], sin_ref[...]
    q = turn(proj_ref[:, :HC] + bias_ref[:, :HC], first, cosine, sine).astype(bf16)
    k = turn(proj_ref[:, HC : 2 * HC] + bias_ref[:, HC : 2 * HC], first, cosine, sine).astype(bf16)
    v = (proj_ref[:, 2 * HC :] + bias_ref[:, 2 * HC :]).astype(bf16)
    qkv_ref[:, :HC] = q.astype(f32)
    qkv_ref[:, HC : 2 * HC] = k.astype(f32)
    qkv_ref[:, 2 * HC :] = v.astype(f32)
    allowed = readable(colq_ref[:, 0:1], colq_ref[:, 1:2], rowk_ref[0:1, :], rowk_ref[1:2, :])
    out = jnp.zeros((GR, HC), f32)
    for h in range(LH):
        mine = (lane // HD) == h
        scores = dot_t(jnp.where(mine, q, 0), k) * 0.125
        probs = softmax_rows(jnp.where(allowed, scores, -1e30)).astype(bf16)
        out = jnp.where(mine, dot_n(probs, v), out)
    mixed_ref[...] = out


def attend_back_kernel(qkv_ref, grad_ref, cos_ref, sin_ref, colq_ref, rowk_ref, out_ref, bias_ref):
    lane = lax.broadcasted_iota(jnp.int32, (1, HC), 1)
    first = (lane % HD) < ROT // 2
    cosine, sine = cos_ref[...], sin_ref[...]
    q = qkv_ref[:, :HC].astype(bf16)
    k = qkv_ref[:, HC : 2 * HC].astype(bf16)
    v = qkv_ref[:, 2 * HC :].astype(bf16)
    gm = grad_ref[...].astype(bf16)
    allowed = readable(colq_ref[:, 0:1], colq_ref[:, 1:2], rowk_ref[0:1, :], rowk_ref[1:2, :])
    gq = jnp.zeros((GR, HC), f32)
    gk = jnp.zeros((GR, HC), f32)
    gv = jnp.zeros((GR, HC), f32)
    for h in range(LH):
        mine = (lane // HD) == h
        scores = dot_t(jnp.where(mine, q, 0), k) * 0.125
        probs = softmax_rows(jnp.where(allowed, scores, -1e30))
        gp = dot_t(jnp.where(mine, gm, 0), v)
        gv = jnp.where(mine, dot_tn(probs.astype(bf16), gm), gv)
        row = jnp.sum(probs * gp, axis=-1, keepdims=True)
        gs = (probs * (gp - row)).astype(bf16)
        gq = jnp.where(mine, dot_n(gs, k), gq)
        gk = jnp.where(mine, dot_tn(gs, q), gk)
    gq = turn(gq * 0.125, first, cosine, -sine).astype(bf16)
    gk = turn(gk * 0.125, first, cosine, -sine).astype(bf16)
    gv = gv.astype(bf16)
    out_ref[:, :HC] = gq.astype(f32)
    out_ref[:, HC : 2 * HC] = gk.astype(f32)
    out_ref[:, 2 * HC :] = gv.astype(f32)

    @pl.when(pl.program_id(0) == 0)
    def _():
        bias_ref[...] = jnp.zeros_like(bias_ref)

    for i, g in enumerate((gq, gk, gv)):
        bias_ref[:, i * HC : (i + 1) * HC] += jnp.sum(g.astype(f32), axis=0, keepdims=True)


def group_specs():
    rows = lambda width: pl.BlockSpec((GR, width), lambda g: (g, 0))
    return dict(
        wide=rows(3 * HC),
        narrow=rows(HC),
        cols=rows(2),
        keys=pl.BlockSpec((None, 2, GR), lambda g: (g, 0, 0)),
        bias=pl.BlockSpec((1, 3 * HC), lambda g: (0, 0)),
    )


def attention(projected, bias, cosine, sine, colq, rowk):
    s = group_specs()
    n = projected.shape[0]
    return pl.pallas_call(
        attend_kernel,
        grid=(n // GR,),
        in_specs=[s["wide"], s["bias"], s["narrow"], s["narrow"], s["cols"], s["keys"]],
        out_specs=[s["wide"], s["narrow"]],
        out_shape=[jax.ShapeDtypeStruct((n, 3 * HC), f32), jax.ShapeDtypeStruct((n, HC), f32)],
        compiler_params=pltpu.CompilerParams(vmem_limit_bytes=32 << 20),
        cost_estimate=pl.CostEstimate(flops=4 * n * GR * HC * LH, bytes_accessed=n * HC * 28, transcendentals=n * GR * LH),
        name="attention",
    )(projected, bias, cosine, sine, colq, rowk)


def attention_back(qkv, grad, cosine, sine, colq, rowk):
    s = group_specs()
    n = qkv.shape[0]
    return pl.pallas_call(
        attend_back_kernel,
        grid=(n // GR,),
        in_specs=[s["wide"], s["narrow"], s["narrow"], s["narrow"], s["cols"], s["keys"]],
        out_specs=[s["wide"], s["bias"]],
        out_shape=[jax.ShapeDtypeStruct((n, 3 * HC), f32), jax.ShapeDtypeStruct((1, 3 * HC), f32)],
        compiler_params=pltpu.CompilerParams(vmem_limit_bytes=32 << 20),
        cost_estimate=pl.CostEstimate(flops=10 * n * GR * HC * LH, bytes_accessed=n * HC * 24, transcendentals=n * GR * LH),
        name="attention_back",
    )(qkv, grad, cosine, sine, colq, rowk)


def mm(spec, a, b):
    return jnp.einsum(spec, a, b, preferred_element_type=f32)


def pair_of(own, axis):
    other = send(own, **{axis: 1})
    first = lax.axis_index(axis) == 0
    return jnp.stack([jnp.where(first, own, other), jnp.where(first, other, own)])


def on_device(
    layer_in,
    segment,
    position,
    first_gain,
    first_shift,
    attend_weight,
    attend_bias,
    output_weight,
    second_gain,
    second_shift,
    gate_weight,
    up_weight,
    down_weight,
    cotangent,
):
    place = Place()
    own_row = place.row(0, 0)
    own_rows = lambda a: lax.dynamic_slice_in_dim(a, own_row, TOK)

    joined = attend_weight.reshape(ROWS, 3, NT, HC).transpose(2, 0, 1, 3).reshape(NT, ROWS, 3 * HC)
    small = jnp.concatenate(
        [v.reshape(ROWS, 1) for v in (first_gain, first_shift, second_gain, second_shift)]
        + [attend_bias.reshape(ROWS, 3), jnp.zeros((ROWS, EXTRA - 7), bf16)],
        axis=1,
    )
    joined = jnp.concatenate([joined, jnp.broadcast_to(small[None], (NT, ROWS, EXTRA))], axis=2)
    joined = lax.all_to_all(joined, YC, 0, 0, tiled=True).reshape(NT * ROWS, 3 * HC + EXTRA)
    first_w = lax.all_gather(joined, XZ, axis=0, tiled=True)
    out_w = lax.all_gather(to_pi(output_weight), AXES, axis=0, tiled=True)

    tokens = gather_rows(to_pi(layer_in[0]), place)
    here = jnp.concatenate([segment, position], axis=0).astype(f32)
    rowk = pair_of(here, "yl")
    rowk = pair_of(rowk, "c").transpose(1, 0, 2, 3).reshape(4, 2, GR)
    colq = rowk.transpose(0, 2, 1).reshape(NT * TOK, 2)
    _, cosine, sine = lane_tables(colq[:, 1:2])

    def hidden_cols(w):
        w = w.reshape(ROWS, NY, NXZ, NC, FROWS)
        w = jnp.pad(w, ((0, 0),) * 4 + ((0, FPAD - FROWS),))
        return w.transpose(1, 3, 0, 2, 4).reshape(NT, ROWS, FT)

    gate_up = jnp.concatenate([hidden_cols(gate_weight), hidden_cols(up_weight)], axis=2)
    gate_up = lax.all_to_all(gate_up, YC, 0, 0, tiled=True).reshape(NT * ROWS, 2 * FT)
    down_own = jnp.pad(to_pi(down_weight), ((0, FPAD - FROWS), (0, 0)))

    def pack_down(a):
        rest = jnp.concatenate([a[..., 16 * i : 16 * i + 16, 2 * FT :] for i in range(3)], axis=-1)
        return jnp.concatenate([a[..., : 2 * FT], rest], axis=-2)

    def unpack_down(a):
        w = D - 2 * FT
        rest = jnp.concatenate([a[..., FPAD:, w * i : w * i + w] for i in range(3)], axis=-2)
        return jnp.concatenate([a[..., :FPAD, :], rest], axis=-1)

    second_w = lax.all_gather(jnp.concatenate([gate_up, pack_down(down_own)], axis=0), XZ, axis=0)
    gate_up_w = second_w[:, : NT * ROWS].reshape(D, 2 * FT)
    down_w = unpack_down(second_w[:, NT * ROWS :]).reshape(FT, D)

    joined_w = first_w[:, : 3 * HC]
    small_all = first_w[:, 3 * HC : 3 * HC + 8]
    vectors = small_all[:, :4].astype(f32).T
    gain_one, shift_one, gain_two, shift_two = (vectors[i : i + 1] for i in range(4))
    bias_all = small_all[:, 4:7].reshape(NXZ, NY, NC * ROWS * 3).transpose(1, 0, 2).reshape(3, NT, HC)
    bias = lax.dynamic_index_in_dim(bias_all, place.tensor(0, 0), axis=1, keepdims=False)
    bias = bias.reshape(1, 3 * HC).astype(f32)

    tokens_f = tokens.astype(f32)
    mean_one, inv_one = norm_stats(tokens_f)
    hidden1 = ((tokens_f - mean_one) * inv_one * gain_one + shift_one).astype(bf16)
    projected = mm("td,de->te", hidden1, joined_w)
    qkv, mixed = attention(projected, bias, cosine, sine, colq, rowk)
    mixed = mixed.astype(bf16)
    mixed_all = put(gather_y(mixed, NT * TOK // 2), lambda r, k: place.tensor(r, k) * HC, (NT * TOK, D), axis=1)
    resid = tokens_f + mm("td,de->te", mixed_all, out_w)

    mean_two, inv_two = norm_stats(resid)
    normed2 = (resid - mean_two) * inv_two
    hidden2 = (normed2 * gain_two + shift_two).astype(bf16)
    gate_up_val = mm("td,de->te", hidden2, gate_up_w)
    gate_val, up_val = gate_up_val[:, :FT], gate_up_val[:, FT:]
    sig = jax.nn.sigmoid(gate_val)
    activated = gate_val * sig
    product = (activated * up_val).astype(bf16)
    out_part = mm("tf,fd->td", product, down_w).astype(bf16)
    layer_out = from_pi((own_rows(resid) + reduce_y(out_part, place)).astype(bf16))[None]

    cot = to_pi(cotangent[0])
    grad_top = gather_rows(cot, place)
    grad_prod = mm("td,fd->tf", grad_top, down_w)
    grad_gate = (grad_prod * up_val * sig * (1.0 + gate_val * (1.0 - sig))).astype(bf16)
    grad_up = (grad_prod * activated).astype(bf16)
    grad_gu = jnp.concatenate([grad_gate, grad_up], axis=1)
    h2_part = mm("tf,df->td", grad_gu, gate_up_w)
    gain_two_part = jnp.sum(h2_part * normed2, axis=0)
    shift_two_part = jnp.sum(h2_part, axis=0)
    grad_h2 = reduce_y(h2_part.astype(bf16), place)
    grad_resid = cot.astype(f32) + norm_back(grad_h2, own_rows(normed2), own_rows(inv_two), gain_two)

    down_grad = mm("tf,td->fd", product, grad_top)
    gate_up_grad = mm("td,tf->df", hidden2, grad_gu)
    lane = lax.broadcasted_iota(jnp.int32, (1, 2 * FT), 1)
    gate_up_grad = gate_up_grad + (
        jnp.where(lane == FROWS, gain_two_part[:, None], 0.0) + jnp.where(lane == FROWS + 1, shift_two_part[:, None], 0.0)
    )
    second_chunks = jnp.concatenate(
        [gate_up_grad.astype(bf16).reshape(NXZ, NT * ROWS, 2 * FT), pack_down(down_grad.astype(bf16).reshape(NXZ, FPAD, D))],
        axis=1,
    )
    second_sum = lax.psum_scatter(second_chunks.reshape(-1, 2 * FT), XZ, scatter_dimension=0, tiled=True)
    down_sum = from_pi(unpack_down(second_sum[NT * ROWS :])[:FROWS].astype(f32))
    gate_up_sum = second_sum[: NT * ROWS].reshape(NT, ROWS, 2 * FT)
    gate_up_sum = lax.all_to_all(gate_up_sum, YC, 0, 0, tiled=True).astype(f32)
    gain_two_grad = jnp.sum(gate_up_sum[:, :, FROWS], axis=0)
    shift_two_grad = jnp.sum(gate_up_sum[:, :, FROWS + 1], axis=0)

    def weight_cols(a):
        a = a.reshape(NY, NC, ROWS, NXZ, FPAD)[..., :FROWS]
        return a.transpose(2, 0, 3, 1, 4).reshape(ROWS, FF)

    gate_sum = weight_cols(gate_up_sum[:, :, :FT])
    up_sum = weight_cols(gate_up_sum[:, :, FT:])

    grad_branch = grad_resid.astype(bf16)
    grad_mixed_own = mm("te,de->td", grad_branch, out_w).astype(bf16)
    got = all_to_all_y(lambda r, k: lax.dynamic_slice_in_dim(grad_mixed_own, place.tensor(r, k) * HC, HC, axis=1))
    grad_mixed = put(got, place.row, (NT * TOK, HC))
    grad_proj, bias_part = attention_back(qkv, grad_mixed.astype(f32), cosine, sine, colq, rowk)
    grad_proj = grad_proj.astype(bf16)
    h1_part = mm("te,de->td", grad_proj, joined_w)
    normed1 = (tokens_f - mean_one) * inv_one
    gain_one_part = jnp.sum(h1_part * normed1, axis=0)
    shift_one_part = jnp.sum(h1_part, axis=0)
    grad_h1 = reduce_y(h1_part.astype(bf16), place)
    input_grad = grad_resid + norm_back(grad_h1, own_rows(normed1), own_rows(inv_one), gain_one)
    input_grad = from_pi(input_grad.astype(bf16))[None]

    branch_all = gather_rows(grad_branch, place)
    out_grad = mm("td,te->de", mixed, branch_all).astype(bf16).reshape(NXZ, ROWS, D)
    joined_grad = mm("td,te->de", hidden1, grad_proj)
    bias_block = jnp.broadcast_to(bias_part.reshape(1, ROWS, 3 * HC // ROWS), (D // ROWS, ROWS, 3 * HC // ROWS))
    extra = jnp.concatenate(
        [
            gain_one_part[:, None],
            shift_one_part[:, None],
            bias_block.reshape(D, 3 * HC // ROWS),
            jnp.zeros((D, EXTRA - 2 - 3 * HC // ROWS), f32),
        ],
        axis=1,
    )
    joined_chunks = jnp.concatenate([joined_grad, extra], axis=1).astype(bf16).reshape(NXZ, NT * ROWS, 3 * HC + EXTRA)
    out_chunks = out_grad.reshape(NXZ, ROWS, NT, HC).transpose(0, 2, 1, 3).reshape(NXZ, NT * ROWS, HC)
    first_sum = lax.psum_scatter(jnp.concatenate([joined_chunks, out_chunks], axis=2), XZ, scatter_dimension=0)
    out_mine = first_sum[:, 3 * HC + EXTRA :].reshape(NT, ROWS, HC).transpose(1, 0, 2).reshape(ROWS, D)
    pairs = [(xz * NC + cc, (8 * cc + xz // 2) * NC + xz % 2) for xz in range(NXZ) for cc in range(NC)]
    out_sum = from_pi(lax.ppermute(out_mine, ("x", "z", "c"), pairs)).astype(f32)
    joined_sum = first_sum[:, : 3 * HC + EXTRA].reshape(NT, ROWS, 3 * HC + EXTRA)
    joined_sum = lax.all_to_all(joined_sum, YC, 0, 0, tiled=True).astype(f32)
    attend_sum = joined_sum[:, :, : 3 * HC].reshape(NT, ROWS, 3, HC).transpose(1, 2, 0, 3).reshape(ROWS, 3 * D)
    gain_one_grad = jnp.sum(joined_sum[:, :, 3 * HC], axis=0)
    shift_one_grad = jnp.sum(joined_sum[:, :, 3 * HC + 1], axis=0)
    bias_sum = joined_sum[:, :, 3 * HC + 2 : 3 * HC + 2 + 3 * HC // ROWS].reshape(NT, 3, HC)
    bias_sum = bias_sum.transpose(1, 0, 2).reshape(3 * D)
    bias_grad = lax.dynamic_slice_in_dim(bias_sum, place.whole() * (3 * D // 128), 3 * D // 128)

    return (
        layer_out,
        input_grad,
        gain_one_grad,
        shift_one_grad,
        attend_sum,
        bias_grad,
        out_sum,
        gain_two_grad,
        shift_two_grad,
        gate_sum,
        up_sum,
        down_sum,
    )


def solution(mesh):
    fine = Mesh(np.asarray(mesh.devices).reshape([SIZES[a] for a in AXES]), AXES)
    group, every = ("yl", "x", "z", "c"), AXES
    tokens, whole = P(group, "yh", None), P(every)
    rows = P(every, None)
    return jax.shard_map(
        on_device,
        mesh=fine,
        in_specs=(
            tokens,
            P(group, None),
            P(group, None),
            whole,
            whole,
            rows,
            whole,
            rows,
            whole,
            whole,
            rows,
            rows,
            rows,
            tokens,
        ),
        out_specs=(tokens, tokens, whole, whole, rows, whole, rows, whole, whole, rows, rows, rows),
        check_vma=False,
    )
```

time: 3080 us -> 627 us (0.20)
  waiting for transfers between devices: 2090 us -> 217 us
  blocking collectives: 591 us -> 12 us
  matrix products: 226 us -> 93.7 us
  local copies, waits for them, and re-layouts: 86.9 us -> 137 us
  starting transfers between devices: 37.4 us -> 79.8 us
    reduce_scatter x4 -> x1, waiting for transfers between devices: 1700 us -> 70.5 us  [on_device(): lax.psum_scatter(second_chunks.reshape(-1, 2 * FT), XZ, scatter_dimension...]
    unnamed x3 -> x0, blocking collectives: 591 us -> none
    all_gather x7 -> x3, waiting for transfers between devices: 352 us -> 29.6 us  [the longest x1 29.6 us: on_device(): lax.all_gather(jnp.concatenate([gate_up, pack_down(down_own)], axis=0), X...]
    dot_general x20 -> x12, matrix products: 222 us -> 93.7 us  [mm(): return jnp.einsum(spec, a, b, preferred_element_type=f32)]
    ppermute x0 -> x67, waiting for transfers between devices: none -> 95.6 us  [the longest x66 95.6 us: send(): return lax.ppermute(value, axes, shift_perm(axes, deltas))]
    unnamed x121 -> x66, local copies, waits for them, and re-layouts: 79.4 us -> 14.1 us
    ppermute x0 -> x67, starting transfers between devices: none -> 62.8 us  [the longest x66 58.7 us: send(): return lax.ppermute(value, axes, shift_perm(axes, deltas))]
    dynamic_update_slice x0 -> x45, local copies, waits for them, and re-layouts: none -> 44.8 us  [put(): whole = lax.dynamic_update_slice(whole, b, tuple(where))]
  transfers between devices with their start and end apart: 24 -> 75, of which waited for: 15 -> 25; matrix products, arithmetic and copies ran while one was open for 22% -> 31% of each run, Pallas kernels for 0% -> 3%
where the time goes in v1:
time: 627 us; the launch traced here: 617 us
  waiting for transfers between devices  217 us (35%)
  local copies, waits for them, and re-layouts  137 us (22%)
  matrix products  93.7 us (15%)
  starting transfers between devices  79.8 us (13%)
  other arithmetic  44.9 us (7%)
  Pallas kernels  16.7 us (3%)
  between operations  15.8 us (3%)
  blocking collectives  12 us (2%)
    ppermute x66, waiting for transfers between devices, send(): return lax.ppermute(value, axes, shift_perm(axes, deltas))  95.6 us
    dot_general x12, matrix products, mm(): return jnp.einsum(spec, a, b, preferred_element_type=f32)  93.7 us
    reduce_scatter x1, waiting for transfers between devices, on_device(): lax.psum_scatter(second_chunks.reshape(-1, 2 * FT), XZ, scatter_dimension...  70.5 us
    ppermute x66, starting transfers between devices, send(): return lax.ppermute(value, axes, shift_perm(axes, deltas))  58.7 us
    dynamic_update_slice x45, local copies, waits for them, and re-layouts, put(): whole = lax.dynamic_update_slice(whole, b, tuple(where))  44.8 us
    all_gather x1, waiting for transfers between devices, on_device(): lax.all_gather(jnp.concatenate([gate_up, pack_down(down_own)], axis=0), X...  29.6 us
    unnamed x66, local copies, waits for them, and re-layouts  14.1 us
  transfers between devices with their start and end apart: 75, of which 25 were waited for; matrix products, arithmetic and copies ran while one was open for 31% of the time, Pallas kernels for 3%

profile of v1, /device:TPU:1, one launch (start us, length us, event | category | flops | bytes accessed | tf_op | source)
XLA Modules:
  0.0 617.0 jit_solution(5180091679338603054)
XLA Ops:
  12.5 12.0 %all_to_all.20 = bf16[8,16,896]{2,1,0:T(8,128)(2,1)S(1)} all-to-all(bf16[8,16,896]{2,1,0:T(8,128)(2,1)S(1)} %pad_maximum_fusion.11), channel_id=1, replica_groups=mesh['yh'=2,'yl'=2,'x'=4,'z'=4,'c'=2] {'yh','yl','c'}, dimensions={0} | all-to-all | bytes 458752 | tf_op jit(solution)/shard_map/all_to_all | solution.py:338
  32.6 4.4 all-to-all-start.1
  39.7 5.3 all-to-all-done.1
  60.6 11.9 %collective-permute-done.9 = f32[2,256]{1,0:T(2,128)S(1)} collective-permute-done((f32[2,256]{1,0:T(2,128)S(1)}, f32[2,256]{1,0:T(2,128)S(1)}, u32[]{:S(2)}, u32[]{:S(2)}) %collective-permute-start.9) | collective-permute-done | bytes 2080 | tf_op jit(solution)/shard_map/ppermute | solution.py:55
  74.9 3.8 fusion.11
  81.5 7.4 %collective-permute-done.3 = bf16[128,2048]{1,0:T(8,128)(2,1)} collective-permute-done((bf16[128,2048]{1,0:T(8,128)(2,1)}, bf16[128,2048]{1,0:T(8,128)(2,1)}, u32[]{:S(2)}, u32[]{:S(2)}) %collective-permute-start.3) | collective-permute-done | bytes 524320 | tf_op jit(solution)/shard_map/ppermute | solution.py:55
  103.7 3.3 collective-permute-done.5
  115.8 2.8 convert_reduce_fusion
  118.6 3.5 fusion.2
  129.2 6.8 %fusion.6.proj_ref = f32[1024,768]{1,0:T(8,128)S(1)} fusion(bf16[2048,896]{0,1:T(8,128)(2,1)} %all-gather.5.cloned.1.call-done, f32[2048]{0:T(1024)S(1)} %bitcast.233, f32[2048]{0:T(1024)S(1)} %bitcast.222, bf16[1024,2048]{1,0:T(8,128)(2,1)} %constant_dynamic-update-slice_fusion.28, f32[1024]{0:T(1024)S(1)} %add_rsqrt_fusion.1, ...), kind=kOutput, calls=%fused_computation.26 | convolution fusion | flops 3233808384 | bytes 10510336 | tf_op jit(solution)/shard_map/td,de->te/dot_general | solution.py:302
  136.1 6.3 %attention.1 = (f32[1024,768]{1,0:T(8,128)S(1)}, f32[1024,256]{1,0:T(8,128)S(1)}) custom-call(f32[1024,768]{1,0:T(8,128)S(1)} %fusion.6.proj_ref, f32[1,768]{1,0:T(1,128)S(1)} %convert.86.bias_ref, f32[1024,256]{1,0:T(8,128)S(1)} %get-tuple-element.140.cos_ref, f32[1024,256]{1,0:T(8,128)S(1)} %get-tuple-element.139.sin_ref, f32[1024,2]{1,0:T(8,128)S(1)} %copy.140.colq_ref, ...), custom_call_target="tpu_custom_call" | custom-call | flops 1073741824 | bytes 7340032 | tf_op jit(solution)/shard_map/attention/pallas_call | solution.py:274
  142.4 2.9 broadcast.205.clone
  153.0 9.5 %collective-permute-done.12 = bf16[1024,256]{1,0:T(8,128)(2,1)S(1)} collective-permute-done((bf16[1024,256]{1,0:T(8,128)(2,1)S(1)}, bf16[1024,256]{1,0:T(8,128)(2,1)S(1)}, u32[]{:S(2)}, u32[]{:S(2)}) %collective-permute-start.12) | collective-permute-done | bytes 524320 | tf_op jit(solution)/shard_map/ppermute | solution.py:55
  180.8 13.2 %fusion.49 = (f32[1024]{0:T(1024)S(1)}, f32[1024,2048]{1,0:T(8,128)S(1)}) fusion(bf16[1024,2048]{1,0:T(8,128)(2,1)} %constant_dynamic-update-slice_fusion.20, bf16[2048,2048]{1,0:T(8,128)(2,1)} %all-gather.7.cloned.1.call-done, bf16[1024,2048]{1,0:T(8,128)(2,1)} %constant_dynamic-update-slice_fusion.28), kind=kOutput, calls=%fused_computation.223 | convolution fusion | flops 8596225024 | bytes 25169920 | tf_op jit(solution)/shard_map/td,de->te/dot_general | solution.py:302
  197.4 4.1 subtract_multiply_fusion
  201.5 29.6 %all-gather.9.cloned.1.call-done = bf16[3072,1536]{1,0:T(8,128)(2,1)} async-done(((bf16[192,1536]{1,0:T(8,128)(2,1)}), bf16[3072,1536]{1,0:T(8,128)(2,1)}) %all-gather.9.cloned.1.call-update) | async-done | bytes 9437200 | tf_op jit(solution)/shard_map/all_gather | solution.py:367
  231.2 6.4 %slice.343 = bf16[16,128,1536]{2,1,0:T(8,128)(2,1)} slice(bf16[16,192,1536]{2,1,0:T(8,128)(2,1)} %bitcast.176), slice={[0:16], [0:128], [0:1536]} | slice | bytes 12582912 | tf_op jit(solution)/shard_map/slice | solution.py:368
  241.4 8.6 %fusion.9 = f32[1024,1536]{1,0:T(8,128)} fusion(bf16[2048,1536]{1,0:T(8,128)(2,1)S(1)} %bitcast.181, f32[1024,2048]{1,0:T(8,128)S(1)} %copy-done.3, f32[2048]{0:T(1024)S(1)} %bitcast.231, f32[2048]{0:T(1024)S(1)} %bitcast.225), kind=kOutput, calls=%fused_computation.33 | convolution fusion | flops 6448742400 | bytes 20987904 | tf_op jit(solution)/shard_map/td,de->te/dot_general | solution.py:302
  250.5 10.3 %multiply_convert_fusion.1 = (bf16[1024,768]{1,0:T(8,128)(2,1)}, bf16[1024,768]{1,0:T(8,128)(2,1)}, bf16[1024,768]{1,0:T(8,128)(2,1)S(1)}) fusion(f32[1024,1536]{1,0:T(8,128)} %fusion.9, bf16[1024,2048]{1,0:T(8,128)(2,1)} %constant_dynamic-update-slice_fusion.10, bf16[768,2048]{1,0:T(8,128)(2,1)S(1)} %bitcast.189), kind=kOutput, calls=%fused_computation.20 | convolution fusion | flops 3233021952 | bytes 18350080 | tf_op jit(solution)/shard_map/td,fd->tf/dot_general | solution.py:302
  260.8 4.0 convolution_convert_fusion
  269.5 10.3 %multiply_reduce_fusion = (f32[2048]{0:T(1024)S(1)}, f32[2048]{0:T(1024)S(1)}, bf16[1024,2048]{1,0:T(8,128)(2,1)}) fusion(f32[1024,2048]{1,0:T(8,128)S(1)} %copy-done.3, bf16[2048,1536]{1,0:T(8,128)(2,1)S(1)} %bitcast.184, bf16[1024,768]{1,0:T(8,128)(2,1)} %get-tuple-element.76, bf16[1024,768]{1,0:T(8,128)(2,1)} %get-tuple-element.75), kind=kOutput, calls=%fused_computation.8 | convolution fusion | flops 6457126912 | bytes 22036480 | tf_op jit(solution)/shard_map/tf,df->td/dot_general | solution.py:302
  288.1 5.1 collective-permute-done.23
  295.0 3.9 collective-permute-done.40
  303.2 6.0 collective-permute-done.24
  310.0 10.4 %collective-permute-done.41 = bf16[128,2048]{1,0:T(8,128)(2,1)S(1)} collective-permute-done((bf16[128,2048]{1,0:T(8,128)(2,1)S(1)}, bf16[128,2048]{1,0:T(8,128)(2,1)S(1)}, u32[]{:S(2)}, u32[]{:S(2)}) %collective-permute-start.41) | collective-permute-done | bytes 524320 | tf_op jit(solution)/shard_map/ppermute | solution.py:55
  321.2 3.1 fusion.38
  327.0 4.3 convolution_convert_fusion.4
  331.6 3.3 collective-permute-start.45
  337.6 2.7 collective-permute-start.46
  340.3 11.0 %collective-permute-done.46 = bf16[2,128,256]{2,1,0:T(8,128)(2,1)S(1)} collective-permute-done((bf16[2,128,256]{2,1,0:T(8,128)(2,1)S(1)}, bf16[2,128,256]{2,1,0:T(8,128)(2,1)S(1)}, u32[]{:S(2)}, u32[]{:S(2)}) %collective-permute-start.46) | collective-permute-done | bytes 131104 | tf_op jit(solution)/shard_map/ppermute | solution.py:55
  353.7 3.1 collective-permute-done.47
  357.0 10.3 %attention_back.1 = (f32[1024,768]{1,0:T(8,128)S(1)}, f32[1,768]{1,0:T(1,128)S(1)}) custom-call(f32[1024,768]{1,0:T(8,128)S(1)} %copy-done.1, f32[1024,256]{1,0:T(8,128)S(1)} %convert_element_type.269.grad_ref, f32[1024,256]{1,0:T(8,128)S(1)} %get-tuple-element.140.cos_ref, f32[1024,256]{1,0:T(8,128)S(1)} %get-tuple-element.139.sin_ref, ...), custom_call_target="tpu_custom_call" | custom-call | flops 2684354560 | bytes 6291456 | tf_op jit(solution)/shard_map/attention_back/pallas_call | solution.py:289
  367.3 8.5 %fusion.36 = (bf16[2048]{0:T(1024)(128)(2,1)S(1)}, bf16[2048]{0:T(1024)(128)(2,1)S(1)}, bf16[1024,2048]{1,0:T(8,128)(2,1)}, f32[1024,2048]{1,0:T(8,128)}) fusion(f32[1024]{0:T(1024)S(1)} %add_rsqrt_fusion.1, f32[1024]{0:T(1024)S(1)} %broadcast_multiply_fusion.1, bf16[1024,2048]{1,0:T(8,128)(2,1)} %constant_dynamic-update-slice_fusion.28, ...), kind=kOutput, calls=%fused_computation.210 | convolution fusion | flops 3236687872 | bytes 23085056 | tf_op jit(solution)/shard_map/te,de->td/dot_general | solution.py:302
  375.8 8.1 %convolution_convert_fusion.2 = bf16[2048,768]{1,0:T(8,128)(2,1)} fusion(f32[2048]{0:T(1024)S(1)} %bitcast.234, f32[2048]{0:T(1024)S(1)} %bitcast.223, f32[1024,768]{1,0:T(8,128)S(1)} %get-tuple-element.18, bf16[1024,2048]{1,0:T(8,128)(2,1)} %constant_dynamic-update-slice_fusion.28, f32[1024]{0:T(1024)S(1)} %add_rsqrt_fusion.1, ...), kind=kOutput, calls=%fused_computation.16 | convolution fusion | flops 3236167680 | bytes 10510336 | tf_op jit(solution)/shard_map/td,te->de/dot_general | solution.py:302
  389.9 2.8 collective-permute-start.62
  405.8 3.5 convolution_convert_fusion.3
  410.1 8.1 %concatenate.97 = bf16[16,128,1152]{2,1,0:T(8,128)(2,1)} concatenate(bf16[16,128,768]{2,1,0:T(8,128)(2,1)} %bitcast.193, bf16[16,128,1]{2,1,0:T(8,128)(2,1)S(1)} %copy.160, bf16[16,128,1]{2,1,0:T(8,128)(2,1)S(1)} %copy.161, bf16[16,128,48]{2,1,0:T(8,128)(2,1)S(1)} %bitcast.205, bf16[16,128,78]{2,1,0:T(8,128)(2,1)S(1)} %broadcast_in_dim.93, bf16[16,128,256]{2,1,0:T(8,128)(2,1)S(1)} %bitcast.188), dimensions={2} | concatenate | bytes 9437184 | tf_op jit(solution)/shard_map/concatenate | solution.py:464
  419.6 5.9 convolution_convert_fusion.1
  427.4 10.2 %add_convert_fusion = bf16[2048,1536]{1,0:T(8,128)(2,1)S(1)} fusion(f32[2048]{0:T(1024)S(1)} %get-tuple-element.57, f32[2048]{0:T(1024)S(1)} %get-tuple-element.56, pred[1536]{0:T(1024)(128)(4,1)S(1)} %get-tuple-element.148, pred[1536]{0:T(1024)(128)(4,1)S(1)} %get-tuple-element.149, bf16[1024,768]{1,0:T(8,128)(2,1)S(1)} %copy-done.24, ...), kind=kOutput, calls=%fused_computation | convolution fusion | flops 6470762496 | bytes 17861632 | tf_op jit(solution)/shard_map/td,tf->df/dot_general | solution.py:302
  437.6 9.5 %maximum_maximum_fusion = bf16[16,192,1536]{2,1,0:T(8,128)(2,1)} fusion(bf16[16,16,512]{2,1,0:T(8,128)(2,1)S(1)} %get-tuple-element.106, bf16[16,16,512]{2,1,0:T(8,128)(2,1)S(1)} %get-tuple-element.107, bf16[16,16,512]{2,1,0:T(8,128)(2,1)S(1)} %get-tuple-element.105, bf16[16,48,1536]{2,1,0:T(8,128)(2,1)S(1)} %slice.388, bf16[16,128,1536]{2,1,0:T(8,128)(2,1)S(1)} %bitcast.185), kind=kLoop, calls=%fused_computation.6 | loop fusion | flops 47185920 | bytes 18874368 | tf_op jit(solution)/shard_map/concatenate | solution.py:417
  459.3 5.9 collective-permute-done.52
  471.2 9.2 %collective-permute-done.53 = bf16[128,2048]{1,0:T(8,128)(2,1)S(1)} collective-permute-done((bf16[128,2048]{1,0:T(8,128)(2,1)}, bf16[128,2048]{1,0:T(8,128)(2,1)S(1)}, u32[]{:S(2)}, u32[]{:S(2)}) %collective-permute-start.53) | collective-permute-done | bytes 524320 | tf_op jit(solution)/shard_map/ppermute | solution.py:55
  483.3 12.0 %reduce-scatter.7.cloned.1.call-done = bf16[1,128,1152]{2,1,0:T(8,128)(2,1)} async-done(((bf16[16,128,1152]{2,1,0:T(8,128)(2,1)}), bf16[1,128,1152]{2,1,0:T(8,128)(2,1)}) %reduce-scatter.7.cloned.1.call-update) | async-done | bytes 294928
  497.7 6.5 %all-to-all-start.2 = ((bf16[8,16,896]{2,1,0:T(8,128)(2,1)}), bf16[8,16,896]{2,1,0:T(8,128)(2,1)S(1)}, u32[]{:S(2)}, u32[]{:S(2)}) async-start(bf16[8,16,896]{2,1,0:T(8,128)(2,1)} %bitcast.65), calls=%async_computation.2 | async-start | bytes 458752 | tf_op jit(solution)/shard_map/all_to_all | solution.py:469
  504.3 4.2 collective-permute-start.66
  515.6 70.5 %reduce-scatter.5.cloned.1.call-done = bf16[192,1536]{1,0:T(8,128)(2,1)} async-done(((bf16[3072,1536]{1,0:T(8,128)(2,1)}), bf16[192,1536]{1,0:T(8,128)(2,1)}) %reduce-scatter.5.cloned.1.call-update) | async-done | bytes 589840 | tf_op jit(solution)/shard_map/reduce_scatter | solution.py:421
  587.9 5.9 all-to-all-start.3
  597.9 4.0 all-to-all-done.3
  (409 shorter events, 196.9 us)
Async XLA Ops:
  7.2 117.5 %all-gather.5.cloned.1.call-start = ((), (), s32[]{:S(2)}) async-start(), calls=%async_computation.6 | async-start | bytes 3899392 | tf_op jit(solution)/shard_map/all_gather | solution.py:339
  25.3 155.5 %all-gather.7.cloned.1.call-start = ((), (), s32[]{:S(2)}) async-start(), calls=%async_computation.7 | async-start | bytes 8454144 | tf_op jit(solution)/shard_map/all_gather | solution.py:340
  32.6 12.5 %all-to-all-start.1 = ((bf16[8,16,1536]{2,1,0:T(8,128)(2,1)}), bf16[8,16,1536]{2,1,0:T(8,128)(2,1)S(1)}, u32[]{:S(2)}, u32[]{:S(2)}) async-start(bf16[8,16,1536]{2,1,0:T(8,128)(2,1)} %pad_maximum_fusion.9), calls=%async_computation.1 | async-start | bytes 786432 | tf_op jit(solution)/shard_map/all_to_all | solution.py:355
  37.0 194.2 %all-gather.9.cloned.1.call-start = ((), (), s32[]{:S(2)}) async-start(), calls=%async_computation.9 | async-start | bytes 10027008 | tf_op jit(solution)/shard_map/all_gather | solution.py:367
  46.0 449.3 %reduce-scatter.7.cloned.1.call-start = ((), (), s32[]{:S(2)}) async-start(), calls=%async_computation.10 | async-start | bytes 5013504
  46.6 43.3 %collective-permute-start.28 = (bf16[128,2048]{1,0:T(8,128)(2,1)S(1)}, bf16[128,2048]{1,0:T(8,128)(2,1)}, u32[]{:S(2)}, u32[]{:S(2)}) collective-permute-start(bf16[128,2048]{1,0:T(8,128)(2,1)S(1)} %copy.149), channel_id=1, source_target_pairs={{0,1},{1,0},{2,3},{3,2},{4,5},{5,4},{6,7},{7,6},{8,9},{9,8},{10,11... | collective-permute-start | bytes 1572872 | tf_op jit(solution)/shard_map/ppermute | solution.py:55
  47.6 32.3 %collective-permute-start.29 = (bf16[128,2048]{1,0:T(8,128)(2,1)S(1)}, bf16[128,2048]{1,0:T(8,128)(2,1)}, u32[]{:S(2)}, u32[]{:S(2)}) collective-permute-start(bf16[128,2048]{1,0:T(8,128)(2,1)S(1)} %copy.149), channel_id=1, source_target_pairs={{0,96},{32,0},{64,32},{96,64},{1,97},{33,1},{65,33},{97,65},{2,98}... | collective-permute-start | bytes 1572872 | tf_op jit(solution)/shard_map/ppermute | solution.py:55
  48.4 25.8 %collective-permute-start.31 = (bf16[128,2048]{1,0:T(8,128)(2,1)S(1)}, bf16[128,2048]{1,0:T(8,128)(2,1)}, u32[]{:S(2)}, u32[]{:S(2)}) collective-permute-start(bf16[128,2048]{1,0:T(8,128)(2,1)S(1)} %copy.149), channel_id=1, source_target_pairs={{0,32},{32,64},{64,96},{96,0},{1,33},{33,65},{65,97},{97,1},{2,34}... | collective-permute-start | bytes 1572872 | tf_op jit(solution)/shard_map/ppermute | solution.py:55
  50.4 41.0 %collective-permute-start.1 = (bf16[128,2048]{1,0:T(8,128)(2,1)}, bf16[128,2048]{1,0:T(8,128)(2,1)}, u32[]{:S(2)}, u32[]{:S(2)}) collective-permute-start(bf16[128,2048]{1,0:T(8,128)(2,1)} %copy.127), channel_id=1, source_target_pairs={{0,96},{32,0},{64,32},{96,64},{1,97},{33,1},{65,33},{97,65},{2,98}... | collective-permute-start | bytes 1572872 | tf_op jit(solution)/shard_map/ppermute | solution.py:55
  52.5 19.9 %collective-permute-start.9 = (f32[2,256]{1,0:T(2,128)S(1)}, f32[2,256]{1,0:T(2,128)S(1)}, u32[]{:S(2)}, u32[]{:S(2)}) collective-permute-start(f32[2,256]{1,0:T(2,128)S(1)} %add_convert_fusion.12), channel_id=1, source_target_pairs={{0,32},{32,0},{1,33},{33,1},{2,34},{34,2},{3,35},{35,3},{4,36},{36... | collective-permute-start | bytes 6152 | tf_op jit(solution)/shard_map/ppermute | solution.py:55
  74.2 14.7 %collective-permute-start.3 = (bf16[128,2048]{1,0:T(8,128)(2,1)}, bf16[128,2048]{1,0:T(8,128)(2,1)}, u32[]{:S(2)}, u32[]{:S(2)}) collective-permute-start(bf16[128,2048]{1,0:T(8,128)(2,1)} %copy.127), channel_id=1, source_target_pairs={{0,32},{32,64},{64,96},{96,0},{1,33},{33,65},{65,97},{97,1},{2,34}... | collective-permute-start | bytes 1572872 | tf_op jit(solution)/shard_map/ppermute | solution.py:55
  74.3 24.4 %collective-permute-start = (bf16[128,2048]{1,0:T(8,128)(2,1)}, bf16[128,2048]{1,0:T(8,128)(2,1)}, u32[]{:S(2)}, u32[]{:S(2)}) collective-permute-start(bf16[128,2048]{1,0:T(8,128)(2,1)} %copy.127), channel_id=1, source_target_pairs={{0,1},{1,0},{2,3},{3,2},{4,5},{5,4},{6,7},{7,6},{8,9},{9,8},{10,11... | collective-permute-start | bytes 1572872 | tf_op jit(solution)/shard_map/ppermute | solution.py:55
  79.9 31.4 %collective-permute-start.32 = (bf16[64,2048]{1,0:T(8,128)(2,1)S(1)}, bf16[64,2048]{1,0:T(8,128)(2,1)}, u32[]{:S(2)}, u32[]{:S(2)}) collective-permute-start(bf16[64,2048]{1,0:T(8,128)(2,1)S(1)} %slice.356), channel_id=1, source_target_pairs={{0,32},{32,64},{64,96},{96,0},{1,33},{33,65},{65,97},{97,1},{2,34}... | collective-permute-start | bytes 786440 | tf_op jit(solution)/shard_map/ppermute | solution.py:55
  88.9 22.5 %collective-permute-start.33 = (bf16[64,2048]{1,0:T(8,128)(2,1)S(1)}, bf16[64,2048]{1,0:T(8,128)(2,1)S(1)}, u32[]{:S(2)}, u32[]{:S(2)}) collective-permute-start(bf16[64,2048]{1,0:T(8,128)(2,1)S(1)} %slice.357), channel_id=1, source_target_pairs={{0,96},{32,0},{64,32},{96,64},{1,97},{33,1},{65,33},{97,65},{2,98}... | collective-permute-start | bytes 786440 | tf_op jit(solution)/shard_map/ppermute | solution.py:55
  89.9 13.6 %collective-permute-start.4 = (bf16[64,2048]{1,0:T(8,128)(2,1)S(1)}, bf16[64,2048]{1,0:T(8,128)(2,1)S(1)}, u32[]{:S(2)}, u32[]{:S(2)}) collective-permute-start(bf16[64,2048]{1,0:T(8,128)(2,1)S(1)} %slice.329), channel_id=1, source_target_pairs={{0,32},{32,64},{64,96},{96,0},{1,33},{33,65},{65,97},{97,1},{2,34}... | collective-permute-start | bytes 786440 | tf_op jit(solution)/shard_map/ppermute | solution.py:55
  91.4 16.4 %collective-permute-start.2 = (bf16[128,2048]{1,0:T(8,128)(2,1)}, bf16[128,2048]{1,0:T(8,128)(2,1)S(1)}, u32[]{:S(2)}, u32[]{:S(2)}) collective-permute-start(bf16[128,2048]{1,0:T(8,128)(2,1)} %collective-permute-done.1), channel_id=1, source_target_pairs={{0,1},{1,0},{2,3},{3,2},{4,5},{5,4},{6,7},{7,6},{8,9},{9,8},{10,11... | collective-permute-start | bytes 1572872 | tf_op jit(solution)/shard_map/ppermute | solution.py:55
  103.5 18.7 %collective-permute-start.30 = (bf16[128,2048]{1,0:T(8,128)(2,1)}, bf16[128,2048]{1,0:T(8,128)(2,1)S(1)}, u32[]{:S(2)}, u32[]{:S(2)}) collective-permute-start(bf16[128,2048]{1,0:T(8,128)(2,1)} %collective-permute-done.29), channel_id=1, source_target_pairs={{0,1},{1,0},{2,3},{3,2},{4,5},{5,4},{6,7},{7,6},{8,9},{9,8},{10,11... | collective-permute-start | bytes 1572872 | tf_op jit(solution)/shard_map/ppermute | solution.py:55
  111.3 56.5 %collective-permute-start.36 = (bf16[128,2048]{1,0:T(8,128)(2,1)}, bf16[128,2048]{1,0:T(8,128)(2,1)}, u32[]{:S(2)}, u32[]{:S(2)}) collective-permute-start(bf16[128,2048]{1,0:T(8,128)(2,1)} %collective-permute-done.31), channel_id=1, source_target_pairs={{0,1},{1,0},{2,3},{3,2},{4,5},{5,4},{6,7},{7,6},{8,9},{9,8},{10,11... | collective-permute-start | bytes 1572872 | tf_op jit(solution)/shard_map/ppermute | solution.py:55
  111.4 37.7 %collective-permute-start.34 = (bf16[64,2048]{1,0:T(8,128)(2,1)}, bf16[64,2048]{1,0:T(8,128)(2,1)}, u32[]{:S(2)}, u32[]{:S(2)}) collective-permute-start(bf16[64,2048]{1,0:T(8,128)(2,1)} %collective-permute-done.32), channel_id=1, source_target_pairs={{0,1},{1,0},{2,3},{3,2},{4,5},{5,4},{6,7},{7,6},{8,9},{9,8},{10,11... | collective-permute-start | bytes 786440 | tf_op jit(solution)/shard_map/ppermute | solution.py:55
  111.9 39.5 %collective-permute-start.35 = (bf16[64,2048]{1,0:T(8,128)(2,1)S(1)}, bf16[64,2048]{1,0:T(8,128)(2,1)}, u32[]{:S(2)}, u32[]{:S(2)}) collective-permute-start(bf16[64,2048]{1,0:T(8,128)(2,1)S(1)} %collective-permute-done.33), channel_id=1, source_target_pairs={{0,1},{1,0},{2,3},{3,2},{4,5},{5,4},{6,7},{7,6},{8,9},{9,8},{10,11... | collective-permute-start | bytes 786440 | tf_op jit(solution)/shard_map/ppermute | solution.py:55
  146.2 16.3 %collective-permute-start.12 = (bf16[1024,256]{1,0:T(8,128)(2,1)S(1)}, bf16[1024,256]{1,0:T(8,128)(2,1)S(1)}, u32[]{:S(2)}, u32[]{:S(2)}) collective-permute-start(bf16[1024,256]{1,0:T(8,128)(2,1)S(1)} %get-tuple-element.74), channel_id=1, source_target_pairs={{0,96},{32,0},{64,32},{96,64},{1,97},{33,1},{65,33},{97,65},{2,98}... | collective-permute-start | bytes 1572872 | tf_op jit(solution)/shard_map/ppermute | solution.py:55
  149.1 15.9 %collective-permute-start.14 = (bf16[1024,256]{1,0:T(8,128)(2,1)S(1)}, bf16[1024,256]{1,0:T(8,128)(2,1)S(1)}, u32[]{:S(2)}, u32[]{:S(2)}) collective-permute-start(bf16[1024,256]{1,0:T(8,128)(2,1)S(1)} %get-tuple-element.74), channel_id=1, source_target_pairs={{0,32},{32,64},{64,96},{96,0},{1,33},{33,65},{65,97},{97,1},{2,34}... | collective-permute-start | bytes 1572872 | tf_op jit(solution)/shard_map/ppermute | solution.py:55
  150.8 19.5 %collective-permute-start.11 = (bf16[1024,256]{1,0:T(8,128)(2,1)S(1)}, bf16[1024,256]{1,0:T(8,128)(2,1)S(1)}, u32[]{:S(2)}, u32[]{:S(2)}) collective-permute-start(bf16[1024,256]{1,0:T(8,128)(2,1)S(1)} %get-tuple-element.74), channel_id=1, source_target_pairs={{0,1},{1,0},{2,3},{3,2},{4,5},{5,4},{6,7},{7,6},{8,9},{9,8},{10,11... | collective-permute-start | bytes 1572872 | tf_op jit(solution)/shard_map/ppermute | solution.py:55
  162.5 12.7 %collective-permute-start.13 = (bf16[1024,256]{1,0:T(8,128)(2,1)S(1)}, bf16[1024,256]{1,0:T(8,128)(2,1)S(1)}, u32[]{:S(2)}, u32[]{:S(2)}) collective-permute-start(bf16[1024,256]{1,0:T(8,128)(2,1)S(1)} %collective-permute-done.12), channel_id=1, source_target_pairs={{0,1},{1,0},{2,3},{3,2},{4,5},{5,4},{6,7},{7,6},{8,9},{9,8},{10,11... | collective-permute-start | bytes 1572872 | tf_op jit(solution)/shard_map/ppermute | solution.py:55
  169.7 10.2 %collective-permute-start.19 = (bf16[1024,256]{1,0:T(8,128)(2,1)S(1)}, bf16[1024,256]{1,0:T(8,128)(2,1)S(1)}, u32[]{:S(2)}, u32[]{:S(2)}) collective-permute-start(bf16[1024,256]{1,0:T(8,128)(2,1)S(1)} %collective-permute-done.14), channel_id=1, source_target_pairs={{0,1},{1,0},{2,3},{3,2},{4,5},{5,4},{6,7},{7,6},{8,9},{9,8},{10,11... | collective-permute-start | bytes 1572872 | tf_op jit(solution)/shard_map/ppermute | solution.py:55
  268.3 13.9 %collective-permute-start.21 = (bf16[128,2048]{1,0:T(8,128)(2,1)}, bf16[128,2048]{1,0:T(8,128)(2,1)S(1)}, u32[]{:S(2)}, u32[]{:S(2)}) collective-permute-start(bf16[128,2048]{1,0:T(8,128)(2,1)} %get-tuple-element.101), channel_id=1, source_target_pairs={{0,1},{1,0},{2,3},{3,2},{4,5},{5,4},{6,7},{7,6},{8,9},{9,8},{10,11... | collective-permute-start | bytes 1572872 | tf_op jit(solution)/shard_map/ppermute | solution.py:55
  269.0 13.3 %collective-permute-start.22 = (bf16[128,2048]{1,0:T(8,128)(2,1)}, bf16[128,2048]{1,0:T(8,128)(2,1)S(1)}, u32[]{:S(2)}, u32[]{:S(2)}) collective-permute-start(bf16[128,2048]{1,0:T(8,128)(2,1)} %get-tuple-element.100), channel_id=1, source_target_pairs={{0,1},{1,0},{2,3},{3,2},{4,5},{5,4},{6,7},{7,6},{8,9},{9,8},{10,11... | collective-permute-start | bytes 1572872 | tf_op jit(solution)/shard_map/ppermute | solution.py:55
  269.0 13.7 %collective-permute-start.25 = (bf16[128,2048]{1,0:T(8,128)(2,1)}, bf16[128,2048]{1,0:T(8,128)(2,1)}, u32[]{:S(2)}, u32[]{:S(2)}) collective-permute-start(bf16[128,2048]{1,0:T(8,128)(2,1)} %get-tuple-element.99), channel_id=1, source_target_pairs={{0,1},{1,0},{2,3},{3,2},{4,5},{5,4},{6,7},{7,6},{8,9},{9,8},{10,11... | collective-permute-start | bytes 1572872 | tf_op jit(solution)/shard_map/ppermute | solution.py:55
  269.5 31.1 %collective-permute-start.20 = (bf16[128,2048]{1,0:T(8,128)(2,1)}, bf16[128,2048]{1,0:T(8,128)(2,1)}, u32[]{:S(2)}, u32[]{:S(2)}) collective-permute-start(bf16[128,2048]{1,0:T(8,128)(2,1)} %get-tuple-element.98), channel_id=1, source_target_pairs={{0,1},{1,0},{2,3},{3,2},{4,5},{5,4},{6,7},{7,6},{8,9},{9,8},{10,11... | collective-permute-start | bytes 1572872 | tf_op jit(solution)/shard_map/ppermute | solution.py:55
  282.7 20.5 %collective-permute-start.37 = (bf16[128,2048]{1,0:T(8,128)(2,1)S(1)}, bf16[128,2048]{1,0:T(8,128)(2,1)S(1)}, u32[]{:S(2)}, u32[]{:S(2)}) collective-permute-start(bf16[128,2048]{1,0:T(8,128)(2,1)S(1)} %get-tuple-element.91), channel_id=1, source_target_pairs={{0,1},{1,0},{2,3},{3,2},{4,5},{5,4},{6,7},{7,6},{8,9},{9,8},{10,11... | collective-permute-start | bytes 1572872 | tf_op jit(solution)/shard_map/ppermute | solution.py:55
  287.9 10.9 %collective-permute-start.40 = (bf16[64,2048]{1,0:T(8,128)(2,1)S(1)}, bf16[64,2048]{1,0:T(8,128)(2,1)S(1)}, u32[]{:S(2)}, u32[]{:S(2)}) collective-permute-start(bf16[64,2048]{1,0:T(8,128)(2,1)S(1)} %get-tuple-element.121), channel_id=1, source_target_pairs={{0,32},{32,64},{64,96},{96,0},{1,33},{33,65},{65,97},{97,1},{2,34}... | collective-permute-start | bytes 786440 | tf_op jit(solution)/shard_map/ppermute | solution.py:55
  294.6 14.6 %collective-permute-start.24 = (bf16[128,2048]{1,0:T(8,128)(2,1)S(1)}, bf16[128,2048]{1,0:T(8,128)(2,1)S(1)}, u32[]{:S(2)}, u32[]{:S(2)}) collective-permute-start(bf16[128,2048]{1,0:T(8,128)(2,1)S(1)} %pad_maximum_fusion.3), channel_id=1, source_target_pairs={{0,32},{32,64},{64,96},{96,0},{1,33},{33,65},{65,97},{97,1},{2,34}... | collective-permute-start | bytes 1572872 | tf_op jit(solution)/shard_map/ppermute | solution.py:55
  298.8 11.1 %collective-permute-start.27 = (bf16[128,2048]{1,0:T(8,128)(2,1)S(1)}, bf16[128,2048]{1,0:T(8,128)(2,1)S(1)}, u32[]{:S(2)}, u32[]{:S(2)}) collective-permute-start(bf16[128,2048]{1,0:T(8,128)(2,1)S(1)} %pad_maximum_fusion.4), channel_id=1, source_target_pairs={{0,96},{32,0},{64,32},{96,64},{1,97},{33,1},{65,33},{97,65},{2,98}... | collective-permute-start | bytes 1572872 | tf_op jit(solution)/shard_map/ppermute | solution.py:55
  300.2 20.2 %collective-permute-start.41 = (bf16[128,2048]{1,0:T(8,128)(2,1)S(1)}, bf16[128,2048]{1,0:T(8,128)(2,1)S(1)}, u32[]{:S(2)}, u32[]{:S(2)}) collective-permute-start(bf16[128,2048]{1,0:T(8,128)(2,1)S(1)} %pad_maximum_fusion.5), channel_id=1, source_target_pairs={{0,32},{32,64},{64,96},{96,0},{1,33},{33,65},{65,97},{97,1},{2,34}... | collective-permute-start | bytes 1572872 | tf_op jit(solution)/shard_map/ppermute | solution.py:55
  300.6 20.6 %collective-permute-start.44 = (bf16[128,2048]{1,0:T(8,128)(2,1)S(1)}, bf16[128,2048]{1,0:T(8,128)(2,1)S(1)}, u32[]{:S(2)}, u32[]{:S(2)}) collective-permute-start(bf16[128,2048]{1,0:T(8,128)(2,1)S(1)} %pad_maximum_fusion.6), channel_id=1, source_target_pairs={{0,96},{32,0},{64,32},{96,64},{1,97},{33,1},{65,33},{97,65},{2,98}... | collective-permute-start | bytes 1572872 | tf_op jit(solution)/shard_map/ppermute | solution.py:55
  334.8 58.1 %collective-permute-start.57 = (bf16[128,2048]{1,0:T(8,128)(2,1)}, bf16[128,2048]{1,0:T(8,128)(2,1)}, u32[]{:S(2)}, u32[]{:S(2)}) collective-permute-start(bf16[128,2048]{1,0:T(8,128)(2,1)} %get-tuple-element.69), channel_id=1, source_target_pairs={{0,1},{1,0},{2,3},{3,2},{4,5},{5,4},{6,7},{7,6},{8,9},{9,8},{10,11... | collective-permute-start | bytes 1572872 | tf_op jit(solution)/shard_map/ppermute | solution.py:55
  334.9 48.9 %collective-permute-start.58 = (bf16[128,2048]{1,0:T(8,128)(2,1)}, bf16[128,2048]{1,0:T(8,128)(2,1)}, u32[]{:S(2)}, u32[]{:S(2)}) collective-permute-start(bf16[128,2048]{1,0:T(8,128)(2,1)} %get-tuple-element.69), channel_id=1, source_target_pairs={{0,96},{32,0},{64,32},{96,64},{1,97},{33,1},{65,33},{97,65},{2,98}... | collective-permute-start | bytes 1572872 | tf_op jit(solution)/shard_map/ppermute | solution.py:55
  337.4 49.6 %collective-permute-start.60 = (bf16[128,2048]{1,0:T(8,128)(2,1)}, bf16[128,2048]{1,0:T(8,128)(2,1)}, u32[]{:S(2)}, u32[]{:S(2)}) collective-permute-start(bf16[128,2048]{1,0:T(8,128)(2,1)} %get-tuple-element.69), channel_id=1, source_target_pairs={{0,32},{32,64},{64,96},{96,0},{1,33},{33,65},{65,97},{97,1},{2,34}... | collective-permute-start | bytes 1572872 | tf_op jit(solution)/shard_map/ppermute | solution.py:55
  337.5 19.4 %collective-permute-start.48 = (bf16[2,128,256]{2,1,0:T(8,128)(2,1)S(1)}, bf16[2,128,256]{2,1,0:T(8,128)(2,1)S(1)}, u32[]{:S(2)}, u32[]{:S(2)}) collective-permute-start(bf16[2,128,256]{2,1,0:T(8,128)(2,1)S(1)} %pad_maximum_fusion.17), channel_id=1, source_target_pairs={{0,32},{32,64},{64,96},{96,0},{1,33},{33,65},{65,97},{97,1},{2,34}... | collective-permute-start | bytes 393224 | tf_op jit(solution)/shard_map/ppermute | solution.py:55
  337.6 13.8 %collective-permute-start.46 = (bf16[2,128,256]{2,1,0:T(8,128)(2,1)S(1)}, bf16[2,128,256]{2,1,0:T(8,128)(2,1)S(1)}, u32[]{:S(2)}, u32[]{:S(2)}) collective-permute-start(bf16[2,128,256]{2,1,0:T(8,128)(2,1)S(1)} %pad_maximum_fusion.15), channel_id=1, source_target_pairs={{0,96},{32,0},{64,32},{96,64},{1,97},{33,1},{65,33},{97,65},{2,98}... | collective-permute-start | bytes 393224 | tf_op jit(solution)/shard_map/ppermute | solution.py:55
  383.9 15.4 %collective-permute-start.59 = (bf16[128,2048]{1,0:T(8,128)(2,1)}, bf16[128,2048]{1,0:T(8,128)(2,1)S(1)}, u32[]{:S(2)}, u32[]{:S(2)}) collective-permute-start(bf16[128,2048]{1,0:T(8,128)(2,1)} %collective-permute-done.58), channel_id=1, source_target_pairs={{0,1},{1,0},{2,3},{3,2},{4,5},{5,4},{6,7},{7,6},{8,9},{9,8},{10,11... | collective-permute-start | bytes 1572872 | tf_op jit(solution)/shard_map/ppermute | solution.py:55
  392.6 12.3 %collective-permute-start.65 = (bf16[128,2048]{1,0:T(8,128)(2,1)}, bf16[128,2048]{1,0:T(8,128)(2,1)S(1)}, u32[]{:S(2)}, u32[]{:S(2)}) collective-permute-start(bf16[128,2048]{1,0:T(8,128)(2,1)} %collective-permute-done.60), channel_id=1, source_target_pairs={{0,1},{1,0},{2,3},{3,2},{4,5},{5,4},{6,7},{7,6},{8,9},{9,8},{10,11... | collective-permute-start | bytes 1572872 | tf_op jit(solution)/shard_map/ppermute | solution.py:55
  418.3 167.9 %reduce-scatter.5.cloned.1.call-start = ((), (), s32[]{:S(2)}) async-start(), calls=%async_computation.8 | async-start | bytes 10027008 | tf_op jit(solution)/shard_map/reduce_scatter | solution.py:421
  456.7 14.5 %collective-permute-start.49 = (bf16[128,2048]{1,0:T(8,128)(2,1)}, bf16[128,2048]{1,0:T(8,128)(2,1)S(1)}, u32[]{:S(2)}, u32[]{:S(2)}) collective-permute-start(bf16[128,2048]{1,0:T(8,128)(2,1)} %get-tuple-element.84), channel_id=1, source_target_pairs={{0,1},{1,0},{2,3},{3,2},{4,5},{5,4},{6,7},{7,6},{8,9},{9,8},{10,11... | collective-permute-start | bytes 1572872 | tf_op jit(solution)/shard_map/ppermute | solution.py:55
  466.2 14.2 %collective-permute-start.53 = (bf16[128,2048]{1,0:T(8,128)(2,1)}, bf16[128,2048]{1,0:T(8,128)(2,1)S(1)}, u32[]{:S(2)}, u32[]{:S(2)}) collective-permute-start(bf16[128,2048]{1,0:T(8,128)(2,1)} %pad_maximum_fusion.7), channel_id=1, source_target_pairs={{0,32},{32,64},{64,96},{96,0},{1,33},{33,65},{65,97},{97,1},{2,34}... | collective-permute-start | bytes 1572872 | tf_op jit(solution)/shard_map/ppermute | solution.py:55
  467.1 13.3 %collective-permute-start.56 = (bf16[128,2048]{1,0:T(8,128)(2,1)}, bf16[128,2048]{1,0:T(8,128)(2,1)}, u32[]{:S(2)}, u32[]{:S(2)}) collective-permute-start(bf16[128,2048]{1,0:T(8,128)(2,1)} %pad_maximum_fusion.8), channel_id=1, source_target_pairs={{0,96},{32,0},{64,32},{96,64},{1,97},{33,1},{65,33},{97,65},{2,98}... | collective-permute-start | bytes 1572872 | tf_op jit(solution)/shard_map/ppermute | solution.py:55
  497.7 15.0 %all-to-all-start.2 = ((bf16[8,16,896]{2,1,0:T(8,128)(2,1)}), bf16[8,16,896]{2,1,0:T(8,128)(2,1)S(1)}, u32[]{:S(2)}, u32[]{:S(2)}) async-start(bf16[8,16,896]{2,1,0:T(8,128)(2,1)} %bitcast.65), calls=%async_computation.2 | async-start | bytes 458752 | tf_op jit(solution)/shard_map/all_to_all | solution.py:469
  587.9 14.0 %all-to-all-start.3 = ((bf16[8,16,1536]{2,1,0:T(8,128)(2,1)}), bf16[8,16,1536]{2,1,0:T(8,128)(2,1)S(1)}, u32[]{:S(2)}, u32[]{:S(2)}) async-start(bf16[8,16,1536]{2,1,0:T(8,128)(2,1)} %bitcast.74), calls=%async_computation.4 | async-start | bytes 786432 | tf_op jit(solution)/shard_map/all_to_all | solution.py:424
  (56 other events, 499.6 us)
Sparse Core Ops, SparseCore 0:
  25.4 54.9 all-gather.4
  84.0 72.5 all-gather.6
  158.9 72.2 all-gather.8
  418.4 76.8 reduce-scatter.6
  498.6 87.4 reduce-scatter.4

commit v2 on v1

--- a/solution.py
+++ b/solution.py
@@ -7,6 +7,7 @@
 from jax import lax
 from jax.experimental import pallas as pl
 from jax.experimental.pallas import tpu as pltpu
+from jax.experimental.layout import Layout, with_layout_constraint
 from jax.sharding import Mesh, PartitionSpec as P
 
 HEADS = 32
@@ -50,9 +51,13 @@
     return pairs
 
 
+def plain(value):
+    return with_layout_constraint(value, Layout(major_to_minor=tuple(range(value.ndim))))
+
+
 def send(value, **deltas):
     axes = tuple(a for a in AXES if a in deltas or (a in ("yh", "yl") and "y" in deltas))
-    return lax.ppermute(value, axes, shift_perm(axes, deltas))
+    return plain(lax.ppermute(plain(value), axes, shift_perm(axes, deltas)))
 
 
 class Place:
@@ -64,9 +69,9 @@
     def tensor(self, ry, rc):
         return (self.y + ry) % NY * NC + (self.c ^ rc)
 
-    def row(self, ry, rc):
+    def block(self, ry, rc):
         y = (self.y + ry) % NY
-        return ((y % 2 * NC + (self.c ^ rc)) * 2 + y // 2) * TOK
+        return (y % 2 * NC + (self.c ^ rc)) * 2 + y // 2
 
     def whole(self):
         return ((self.y * NX + self.x) * NZ + self.z) * NC + self.c
@@ -75,71 +80,57 @@
 EVERY = tuple((r, k) for r in range(NY) for k in range(NC))
 
 
-def gather_y(own, half):
+def gather_y(own, half, hold):
     from_prev = send(own, y=1)
     from_next = send(own, y=-1)
+    from_prev, from_next, hold = lax.optimization_barrier((from_prev, from_next, hold))
     top = send(from_prev[:half], y=1)
     bottom = send(from_next[half:], y=-1)
     blocks = {(0, 0): (own,), (1, 0): (from_next,), (3, 0): (from_prev,), (2, 0): (top, bottom)}
     for r in (0, 1, 3, 2):
         blocks[(r, 1)] = tuple(send(b, c=1) for b in blocks[(r, 0)])
-    return blocks
-
-
-def put(blocks, start, shape, axis=0):
-    whole = jnp.zeros(shape, bf16)
+    return blocks, hold
+
+
+def gather_rows(own, place, hold=()):
+    blocks, hold = gather_y(own, TOK // 2, hold)
+    whole = jnp.zeros((NT,) + own.shape, own.dtype)
     for s in EVERY:
         at = 0
         for b in blocks[s]:
-            where = [at, 0]
-            where[axis] = where[axis] + start(*s)
-            whole = lax.dynamic_update_slice(whole, b, tuple(where))
+            whole = lax.dynamic_update_slice(whole, b[None], (place.block(*s), at, 0))
             at += b.shape[0]
-    return whole
-
-
-def gather_rows(own, place):
-    return put(gather_y(own, TOK // 2), place.row, (NT * TOK, own.shape[1]))
-
-
-def reduce_y(total, place):
-    part = lambda r, k: lax.dynamic_slice_in_dim(total, place.row(r, k), TOK)
+    whole = whole.reshape(NT * TOK, own.shape[1])
+    return (whole, hold) if hold else whole
+
+
+def reduce_y(total, place, hold=()):
+    total = total.reshape(NT, TOK, D)
+    part = lambda r, k: lax.dynamic_index_in_dim(total, place.block(r, k), keepdims=False)
     sums = {}
     half = TOK // 2
     for r in (2, 1, 3, 0):
         other = send(part(r, 1), c=1)
         sums[r] = part(r, 0).astype(f32) + other.astype(f32)
-    far = sums[2].astype(bf16)
+    far, hold = lax.optimization_barrier((sums[2].astype(bf16), hold))
     top = send(far[:half], y=1)
     bottom = send(far[half:], y=-1)
     one = jnp.concatenate([sums[1][:half] + top.astype(f32), sums[1][half:]], axis=0).astype(bf16)
     three = jnp.concatenate([sums[3][:half], sums[3][half:] + bottom.astype(f32)], axis=0).astype(bf16)
     from_prev = send(one, y=1)
     from_next = send(three, y=-1)
-    return sums[0] + from_prev.astype(f32) + from_next.astype(f32)
-
-
-def all_to_all_y(piece):
-    mine = [piece(r, 0) for r in range(NY)]
-    other = send(jnp.stack([piece(r, 1) for r in range(NY)]), c=1)
-    got = {}
-    for r in range(NY):
-        pair = jnp.stack([mine[r], other[r]])
-        if r:
-            pair = send(pair, y=r if r < 3 else -1)
-        got[((-r) % NY, 0)] = (pair[0],)
-        got[((-r) % NY, 1)] = (pair[1],)
-    return got
+    out = sums[0] + from_prev.astype(f32) + from_next.astype(f32)
+    return (out, hold) if hold else out
 
 
 def to_pi(a):
     n = a.shape[0]
-    return a.reshape(n, NY, NXZ, D // NY // NXZ).transpose(0, 2, 1, 3).reshape(n, D)
+    return plain(plain(a).reshape(n, NY, NXZ, D // NY // NXZ).transpose(0, 2, 1, 3).reshape(n, D))
 
 
 def from_pi(a):
     n = a.shape[0]
-    return a.reshape(n, NXZ, NY, D // NY // NXZ).transpose(0, 2, 1, 3).reshape(n, D)
+    return plain(plain(a).reshape(n, NXZ, NY, D // NY // NXZ).transpose(0, 2, 1, 3).reshape(n, D))
 
 
 def norm_stats(rows):
@@ -325,8 +316,8 @@
     cotangent,
 ):
     place = Place()
-    own_row = place.row(0, 0)
-    own_rows = lambda a: lax.dynamic_slice_in_dim(a, own_row, TOK)
+    own_block = place.block(0, 0)
+    own_rows = lambda a: lax.dynamic_index_in_dim(a.reshape((NT, TOK) + a.shape[1:]), own_block, keepdims=False)
 
     joined = attend_weight.reshape(ROWS, 3, NT, HC).transpose(2, 0, 1, 3).reshape(NT, ROWS, 3 * HC)
     small = jnp.concatenate(
@@ -336,24 +327,37 @@
     )
     joined = jnp.concatenate([joined, jnp.broadcast_to(small[None], (NT, ROWS, EXTRA))], axis=2)
     joined = lax.all_to_all(joined, YC, 0, 0, tiled=True).reshape(NT * ROWS, 3 * HC + EXTRA)
-    first_w = lax.all_gather(joined, XZ, axis=0, tiled=True)
-    out_w = lax.all_gather(to_pi(output_weight), AXES, axis=0, tiled=True)
-
-    tokens = gather_rows(to_pi(layer_in[0]), place)
+    pairs = [(xz * NC + cc, (8 * cc + xz // 2) * NC + xz % 2) for xz in range(NXZ) for cc in range(NC)]
+    out_own = lax.ppermute(to_pi(output_weight), ("x", "z", "c"), [(b, a) for a, b in pairs])
+    out_own = out_own.reshape(ROWS, NT, HC).transpose(1, 0, 2).reshape(NT * ROWS, HC)
+    first_own = jnp.concatenate([joined, out_own], axis=1)
+
+    layer_pi = to_pi(layer_in[0])
+    tokens = gather_rows(layer_pi, place)
+    cot = to_pi(cotangent[0])
     here = jnp.concatenate([segment, position], axis=0).astype(f32)
     rowk = pair_of(here, "yl")
     rowk = pair_of(rowk, "c").transpose(1, 0, 2, 3).reshape(4, 2, GR)
     colq = rowk.transpose(0, 2, 1).reshape(NT * TOK, 2)
     _, cosine, sine = lane_tables(colq[:, 1:2])
 
+    first_w = lax.all_gather(first_own, XZ, axis=0)
+    hold = (tokens, gate_weight, up_weight, down_weight)
+    tokens, gate_weight, up_weight, down_weight = lax.optimization_barrier(hold)
+
+    spread = np.zeros((NXZ, FROWS, NXZ, FPAD), np.float32)
+    for k in range(NXZ):
+        spread[k, :, k, :FROWS] = np.eye(FROWS)
+    spread = jnp.asarray(spread.reshape(NXZ * FROWS, FT), bf16)
+
     def hidden_cols(w):
-        w = w.reshape(ROWS, NY, NXZ, NC, FROWS)
-        w = jnp.pad(w, ((0, 0),) * 4 + ((0, FPAD - FROWS),))
-        return w.transpose(1, 3, 0, 2, 4).reshape(NT, ROWS, FT)
+        w = plain(w).reshape(ROWS, NT, NXZ * FROWS).transpose(1, 0, 2)
+        return mm("trf,fg->trg", w, spread).astype(bf16)
 
     gate_up = jnp.concatenate([hidden_cols(gate_weight), hidden_cols(up_weight)], axis=2)
     gate_up = lax.all_to_all(gate_up, YC, 0, 0, tiled=True).reshape(NT * ROWS, 2 * FT)
-    down_own = jnp.pad(to_pi(down_weight), ((0, FPAD - FROWS), (0, 0)))
+    down_own = lax.ppermute(plain(down_weight), ("x", "z", "c"), [(b, a) for a, b in pairs])
+    down_own = jnp.pad(to_pi(down_own), ((0, FPAD - FROWS), (0, 0)))
 
     def pack_down(a):
         rest = jnp.concatenate([a[..., 16 * i : 16 * i + 16, 2 * FT :] for i in range(3)], axis=-1)
@@ -364,10 +368,15 @@
         rest = jnp.concatenate([a[..., FPAD:, w * i : w * i + w] for i in range(3)], axis=-2)
         return jnp.concatenate([a[..., :FPAD, :], rest], axis=-1)
 
-    second_w = lax.all_gather(jnp.concatenate([gate_up, pack_down(down_own)], axis=0), XZ, axis=0)
+    second_own = jnp.concatenate([gate_up, pack_down(down_own)], axis=0)
+    second_w = lax.all_gather(second_own, XZ, axis=0)
     gate_up_w = second_w[:, : NT * ROWS].reshape(D, 2 * FT)
     down_w = unpack_down(second_w[:, NT * ROWS :]).reshape(FT, D)
 
+    cot_later, first_w = lax.optimization_barrier((cot, first_w))
+    grad_top = gather_rows(cot_later, place)
+    out_w = first_w[:, :, 3 * HC + EXTRA :].reshape(NXZ, NT, ROWS, HC).transpose(0, 2, 1, 3).reshape(HC, D)
+    first_w = first_w[:, :, : 3 * HC + EXTRA].reshape(D, 3 * HC + EXTRA)
     joined_w = first_w[:, : 3 * HC]
     small_all = first_w[:, 3 * HC : 3 * HC + 8]
     vectors = small_all[:, :4].astype(f32).T
@@ -382,71 +391,55 @@
     projected = mm("td,de->te", hidden1, joined_w)
     qkv, mixed = attention(projected, bias, cosine, sine, colq, rowk)
     mixed = mixed.astype(bf16)
-    mixed_all = put(gather_y(mixed, NT * TOK // 2), lambda r, k: place.tensor(r, k) * HC, (NT * TOK, D), axis=1)
-    resid = tokens_f + mm("td,de->te", mixed_all, out_w)
+    attended = mm("td,de->te", mixed, out_w).astype(bf16)
+    resid = layer_pi.astype(f32) + reduce_y(attended, place)
 
     mean_two, inv_two = norm_stats(resid)
     normed2 = (resid - mean_two) * inv_two
     hidden2 = (normed2 * gain_two + shift_two).astype(bf16)
+    hidden2, (gate_up_w, down_w) = gather_rows(hidden2, place, (gate_up_w, down_w))
     gate_up_val = mm("td,de->te", hidden2, gate_up_w)
     gate_val, up_val = gate_up_val[:, :FT], gate_up_val[:, FT:]
     sig = jax.nn.sigmoid(gate_val)
     activated = gate_val * sig
     product = (activated * up_val).astype(bf16)
-    out_part = mm("tf,fd->td", product, down_w).astype(bf16)
-    layer_out = from_pi((own_rows(resid) + reduce_y(out_part, place)).astype(bf16))[None]
-
-    cot = to_pi(cotangent[0])
-    grad_top = gather_rows(cot, place)
+
     grad_prod = mm("td,fd->tf", grad_top, down_w)
     grad_gate = (grad_prod * up_val * sig * (1.0 + gate_val * (1.0 - sig))).astype(bf16)
     grad_up = (grad_prod * activated).astype(bf16)
     grad_gu = jnp.concatenate([grad_gate, grad_up], axis=1)
     h2_part = mm("tf,df->td", grad_gu, gate_up_w)
-    gain_two_part = jnp.sum(h2_part * normed2, axis=0)
-    shift_two_part = jnp.sum(h2_part, axis=0)
-    grad_h2 = reduce_y(h2_part.astype(bf16), place)
-    grad_resid = cot.astype(f32) + norm_back(grad_h2, own_rows(normed2), own_rows(inv_two), gain_two)
+    later = (product, grad_top, hidden2, grad_gu)
+    grad_h2, (product, grad_top, hidden2, grad_gu) = reduce_y(h2_part.astype(bf16), place, later)
 
     down_grad = mm("tf,td->fd", product, grad_top)
     gate_up_grad = mm("td,tf->df", hidden2, grad_gu)
-    lane = lax.broadcasted_iota(jnp.int32, (1, 2 * FT), 1)
-    gate_up_grad = gate_up_grad + (
-        jnp.where(lane == FROWS, gain_two_part[:, None], 0.0) + jnp.where(lane == FROWS + 1, shift_two_part[:, None], 0.0)
-    )
     second_chunks = jnp.concatenate(
         [gate_up_grad.astype(bf16).reshape(NXZ, NT * ROWS, 2 * FT), pack_down(down_grad.astype(bf16).reshape(NXZ, FPAD, D))],
         axis=1,
     )
+    grad_h2, second_chunks = lax.optimization_barrier((grad_h2, second_chunks))
+    gain_two_part = jnp.sum(grad_h2 * normed2, axis=0)
+    shift_two_part = jnp.sum(grad_h2, axis=0)
+    grad_resid = cot.astype(f32) + norm_back(grad_h2, normed2, inv_two, gain_two)
     second_sum = lax.psum_scatter(second_chunks.reshape(-1, 2 * FT), XZ, scatter_dimension=0, tiled=True)
-    down_sum = from_pi(unpack_down(second_sum[NT * ROWS :])[:FROWS].astype(f32))
-    gate_up_sum = second_sum[: NT * ROWS].reshape(NT, ROWS, 2 * FT)
-    gate_up_sum = lax.all_to_all(gate_up_sum, YC, 0, 0, tiled=True).astype(f32)
-    gain_two_grad = jnp.sum(gate_up_sum[:, :, FROWS], axis=0)
-    shift_two_grad = jnp.sum(gate_up_sum[:, :, FROWS + 1], axis=0)
-
-    def weight_cols(a):
-        a = a.reshape(NY, NC, ROWS, NXZ, FPAD)[..., :FROWS]
-        return a.transpose(2, 0, 3, 1, 4).reshape(ROWS, FF)
-
-    gate_sum = weight_cols(gate_up_sum[:, :, :FT])
-    up_sum = weight_cols(gate_up_sum[:, :, FT:])
-
     grad_branch = grad_resid.astype(bf16)
-    grad_mixed_own = mm("te,de->td", grad_branch, out_w).astype(bf16)
-    got = all_to_all_y(lambda r, k: lax.dynamic_slice_in_dim(grad_mixed_own, place.tensor(r, k) * HC, HC, axis=1))
-    grad_mixed = put(got, place.row, (NT * TOK, HC))
-    grad_proj, bias_part = attention_back(qkv, grad_mixed.astype(f32), cosine, sine, colq, rowk)
+    branch_all = gather_rows(grad_branch, place)
+    grad_mixed = mm("te,de->td", branch_all, out_w)
+    grad_proj, bias_part = attention_back(qkv, grad_mixed, cosine, sine, colq, rowk)
     grad_proj = grad_proj.astype(bf16)
     h1_part = mm("te,de->td", grad_proj, joined_w)
     normed1 = (tokens_f - mean_one) * inv_one
     gain_one_part = jnp.sum(h1_part * normed1, axis=0)
     shift_one_part = jnp.sum(h1_part, axis=0)
-    grad_h1 = reduce_y(h1_part.astype(bf16), place)
+    later = (hidden1, mixed, branch_all)
+    grad_h1, (hidden1, mixed, branch_all) = reduce_y(h1_part.astype(bf16), place, later)
+    grad_h1, product = lax.optimization_barrier((grad_h1, product))
+    out_part = mm("tf,fd->td", product, down_w).astype(bf16)
+    layer_out = from_pi((resid + reduce_y(out_part, place)).astype(bf16))[None]
     input_grad = grad_resid + norm_back(grad_h1, own_rows(normed1), own_rows(inv_one), gain_one)
     input_grad = from_pi(input_grad.astype(bf16))[None]
 
-    branch_all = gather_rows(grad_branch, place)
     out_grad = mm("td,te->de", mixed, branch_all).astype(bf16).reshape(NXZ, ROWS, D)
     joined_grad = mm("td,te->de", hidden1, grad_proj)
     bias_block = jnp.broadcast_to(bias_part.reshape(1, ROWS, 3 * HC // ROWS), (D // ROWS, ROWS, 3 * HC // ROWS))
@@ -454,23 +447,38 @@
         [
             gain_one_part[:, None],
             shift_one_part[:, None],
+            gain_two_part[:, None],
+            shift_two_part[:, None],
             bias_block.reshape(D, 3 * HC // ROWS),
-            jnp.zeros((D, EXTRA - 2 - 3 * HC // ROWS), f32),
+            jnp.zeros((D, EXTRA - 4 - 3 * HC // ROWS), f32),
         ],
         axis=1,
     )
     joined_chunks = jnp.concatenate([joined_grad, extra], axis=1).astype(bf16).reshape(NXZ, NT * ROWS, 3 * HC + EXTRA)
     out_chunks = out_grad.reshape(NXZ, ROWS, NT, HC).transpose(0, 2, 1, 3).reshape(NXZ, NT * ROWS, HC)
-    first_sum = lax.psum_scatter(jnp.concatenate([joined_chunks, out_chunks], axis=2), XZ, scatter_dimension=0)
+    first_chunks = jnp.concatenate([joined_chunks, out_chunks], axis=2)
+    first_chunks, second_sum = lax.optimization_barrier((first_chunks, second_sum))
+    first_sum = lax.psum_scatter(first_chunks, XZ, scatter_dimension=0)
+    down_sum = unpack_down(second_sum[NT * ROWS :])[:FROWS]
+    down_sum = from_pi(lax.ppermute(plain(down_sum), ("x", "z", "c"), pairs)).astype(f32)
+    gate_up_sum = second_sum[: NT * ROWS].reshape(NT, ROWS, 2 * FT)
+    gate_up_sum = lax.all_to_all(gate_up_sum, YC, 0, 0, tiled=True)
+
+    def weight_cols(a):
+        a = mm("trg,fg->trf", a, spread)
+        return a.transpose(1, 0, 2).reshape(ROWS, FF)
+
+    gate_sum = weight_cols(gate_up_sum[:, :, :FT])
+    up_sum = weight_cols(gate_up_sum[:, :, FT:])
+
     out_mine = first_sum[:, 3 * HC + EXTRA :].reshape(NT, ROWS, HC).transpose(1, 0, 2).reshape(ROWS, D)
-    pairs = [(xz * NC + cc, (8 * cc + xz // 2) * NC + xz % 2) for xz in range(NXZ) for cc in range(NC)]
     out_sum = from_pi(lax.ppermute(out_mine, ("x", "z", "c"), pairs)).astype(f32)
     joined_sum = first_sum[:, : 3 * HC + EXTRA].reshape(NT, ROWS, 3 * HC + EXTRA)
     joined_sum = lax.all_to_all(joined_sum, YC, 0, 0, tiled=True).astype(f32)
     attend_sum = joined_sum[:, :, : 3 * HC].reshape(NT, ROWS, 3, HC).transpose(1, 2, 0, 3).reshape(ROWS, 3 * D)
-    gain_one_grad = jnp.sum(joined_sum[:, :, 3 * HC], axis=0)
-    shift_one_grad = jnp.sum(joined_sum[:, :, 3 * HC + 1], axis=0)
-    bias_sum = joined_sum[:, :, 3 * HC + 2 : 3 * HC + 2 + 3 * HC // ROWS].reshape(NT, 3, HC)
+    summed = jnp.sum(joined_sum[:, :, 3 * HC : 3 * HC + 4], axis=0)
+    gain_one_grad, shift_one_grad, gain_two_grad, shift_two_grad = (summed[:, i] for i in range(4))
+    bias_sum = joined_sum[:, :, 3 * HC + 4 : 3 * HC + 4 + 3 * HC // ROWS].reshape(NT, 3, HC)
     bias_sum = bias_sum.transpose(1, 0, 2).reshape(3 * D)
     bias_grad = lax.dynamic_slice_in_dim(bias_sum, place.whole() * (3 * D // 128), 3 * D // 128)
 

time: 627 us -> 473 us (0.75)
  waiting for transfers between devices: 217 us -> 112 us
  local copies, waits for them, and re-layouts: 137 us -> 97.2 us
  matrix products: 93.7 us -> 60.5 us
  starting transfers between devices: 79.8 us -> 109 us
  blocking collectives: 12 us -> 0 us
  other arithmetic: 44.9 us -> 53 us
    reduce_scatter x1, waiting for transfers between devices: 70.5 us -> 4.75 us  [on_device(): lax.psum_scatter(second_chunks.reshape(-1, 2 * FT), XZ, scatter_dimension...]
    dot_general x12 -> x16, matrix products: 93.7 us -> 60.5 us  [mm(): return jnp.einsum(spec, a, b, preferred_element_type=f32)]
    dynamic_update_slice x45 -> x38, local copies, waits for them, and re-layouts: 44.8 us -> 14.1 us  [gather_rows(): whole = lax.dynamic_update_slice(whole, b[None], (place.block(*s), at, 0))]
    all_gather x3 -> x2, waiting for transfers between devices: 29.6 us -> 0.02 us  [the longest x1 0.02 us: on_device(): first_w = lax.all_gather(first_own, XZ, axis=0)]
    ppermute x66 -> x73, starting transfers between devices: 58.7 us -> 84.5 us  [the longest x70 71.1 us: send(): return plain(lax.ppermute(plain(value), axes, shift_perm(axes, deltas)))]
    all_to_all x1 -> x0, blocking collectives: 12 us -> none  [on_device(): lax.all_to_all(joined, YC, 0, 0, tiled=True)]
    unnamed x6 -> x5, waiting for transfers between devices: 12.1 us -> 1.86 us
    reshape x22 -> x20, local copies, waits for them, and re-layouts: 18.3 us -> 10.2 us  [the longest x7 4.78 us: from_pi(): plain(a).reshape(n, NXZ, NY, D // NY // NXZ).transpose(0, 2, 1, 3)]
  transfers between devices with their start and end apart: 75 -> 82, of which waited for: 25 -> 35; matrix products, arithmetic and copies ran while one was open for 31% -> 35% of each run, Pallas kernels for 3% -> 4%
where the time goes in v2:
time: 473 us; the launch traced here: 464 us
  waiting for transfers between devices  112 us (24%)
  starting transfers between devices  109 us (23%)
  local copies, waits for them, and re-layouts  97.2 us (21%)
  matrix products  60.5 us (13%)
  other arithmetic  53 us (11%)
  Pallas kernels  16.6 us (4%)
  between operations  15.8 us (3%)
    ppermute x70, waiting for transfers between devices, send(): return plain(lax.ppermute(plain(value), axes, shift_perm(axes, deltas)))  95.9 us
    ppermute x70, starting transfers between devices, send(): return plain(lax.ppermute(plain(value), axes, shift_perm(axes, deltas)))  71.1 us
    dot_general x16, matrix products, mm(): return jnp.einsum(spec, a, b, preferred_element_type=f32)  60.5 us
    unnamed x104, local copies, waits for them, and re-layouts  16.6 us
    dynamic_update_slice x38, local copies, waits for them, and re-layouts, gather_rows(): whole = lax.dynamic_update_slice(whole, b[None], (place.block(*s), at, 0))  14.1 us
    pallas_call x1, Pallas kernels, attention_back(): pl.pallas_call(attend_back_kernel, grid=(n // GR,), in_specs=[s['wide'],...  10.3 us
    concatenate x1, other arithmetic, on_device(): jnp.concatenate([gate_up_grad.astype(bf16).reshape(NXZ, NT * ROWS, 2 * FT...  9.51 us
  transfers between devices with their start and end apart: 82, of which 35 were waited for; matrix products, arithmetic and copies ran while one was open for 35% of the time, Pallas kernels for 4%

profile of v2, /device:TPU:1, one launch (start us, length us, event | category | flops | bytes accessed | tf_op | source)
XLA Modules:
  0.0 464.3 jit_solution(3623682901374526099)
XLA Ops:
  13.1 6.0 %all-to-all-start = ((bf16[8,16,896]{2,1,0:T(8,128)(2,1)}), bf16[8,16,896]{2,1,0:T(8,128)(2,1)S(1)}, u32[]{:S(2)}, u32[]{:S(2)}) async-start(bf16[8,16,896]{2,1,0:T(8,128)(2,1)} %pad_maximum_fusion.11), calls=%async_computation | async-start | bytes 458752 | tf_op jit(solution)/shard_map/all_to_all | solution.py:329
  20.6 3.5 collective-permute-start.9
  24.0 3.6 collective-permute-done.9
  35.1 7.9 %collective-permute-done.1 = bf16[128,2048]{1,0:T(8,128)(2,1)S(1)} collective-permute-done((bf16[128,2048]{1,0:T(8,128)(2,1)S(1)}, bf16[128,2048]{1,0:T(8,128)(2,1)S(1)}, u32[]{:S(2)}, u32[]{:S(2)}) %collective-permute-start.1) | collective-permute-done | bytes 524320 | tf_op jit(solution)/shard_map/ppermute | solution.py:60
  43.7 3.0 collective-permute-start.5
  48.3 5.0 %collective-permute-done.4 = bf16[64,2048]{1,0:T(8,128)(2,1)S(1)} collective-permute-done((bf16[64,2048]{1,0:T(8,128)(2,1)S(1)}, bf16[64,2048]{1,0:T(8,128)(2,1)S(1)}, u32[]{:S(2)}, u32[]{:S(2)}) %collective-permute-start.4) | collective-permute-done | bytes 262176 | tf_op jit(solution)/shard_map/ppermute | solution.py:60
  59.7 4.5 collective-permute-start.31
  65.7 3.8 all-to-all-start.1
  69.5 3.9 collective-permute-done.31
  84.8 3.8 fusion.9
  88.6 2.8 convert_reduce_fusion
  91.4 3.4 fusion.2
  100.2 3.2 slice.254
  109.0 3.5 add_convert_fusion
  112.6 3.4 fusion.6.proj_ref
  116.0 6.3 %attention.1 = (f32[1024,768]{1,0:T(8,128)S(1)}, f32[1024,256]{1,0:T(8,128)S(1)}) custom-call(f32[1024,768]{1,0:T(8,128)S(1)} %fusion.6.proj_ref, f32[1,768]{1,0:T(1,128)S(1)} %convert.124.bias_ref, f32[1024,256]{1,0:T(8,128)S(1)} %get-tuple-element.161.cos_ref, f32[1024,256]{1,0:T(8,128)S(1)} %get-tuple-element.160.sin_ref, f32[1024,2]{1,0:T(8,128)S(1)} %copy.186.colq_ref, ...), custom_call_target="tpu_custom_call" | custom-call | flops 1073741824 | bytes 7340032 | tf_op jit(solution)/shard_map/attention/pallas_call | solution.py:265
  132.1 12.7 %collective-permute-done.15 = bf16[64,2048]{1,0:T(8,128)(2,1)S(1)} collective-permute-done((bf16[64,2048]{1,0:T(8,128)(2,1)S(1)}, bf16[64,2048]{1,0:T(8,128)(2,1)S(1)}, u32[]{:S(2)}, u32[]{:S(2)}) %collective-permute-start.15) | collective-permute-done | bytes 262176 | tf_op jit(solution)/shard_map/ppermute | solution.py:60
  144.8 7.1 %collective-permute-done.18 = bf16[64,2048]{1,0:T(8,128)(2,1)S(1)} collective-permute-done((bf16[64,2048]{1,0:T(8,128)(2,1)S(1)}, bf16[64,2048]{1,0:T(8,128)(2,1)S(1)}, u32[]{:S(2)}, u32[]{:S(2)}) %collective-permute-start.18) | collective-permute-done | bytes 262176 | tf_op jit(solution)/shard_map/ppermute | solution.py:60
  158.3 4.4 collective-permute-start.26
  181.0 3.4 slice.335
  186.3 5.4 %collective-permute-done.29 = bf16[128,2048]{1,0:T(8,128)(2,1)} collective-permute-done((bf16[128,2048]{1,0:T(8,128)(2,1)}, bf16[128,2048]{1,0:T(8,128)(2,1)}, u32[]{:S(2)}, u32[]{:S(2)}) %collective-permute-start.29) | collective-permute-done | bytes 524320 | tf_op jit(solution)/shard_map/ppermute | solution.py:60
  199.4 4.8 %collective-permute-done.34 = bf16[64,2048]{1,0:T(8,128)(2,1)S(1)} collective-permute-done((bf16[64,2048]{1,0:T(8,128)(2,1)S(1)}, bf16[64,2048]{1,0:T(8,128)(2,1)S(1)}, u32[]{:S(2)}, u32[]{:S(2)}) %collective-permute-start.34) | collective-permute-done | bytes 262176 | tf_op jit(solution)/shard_map/ppermute | solution.py:60
  208.7 8.7 %fusion.59 = f32[1024,1536]{0,1:T(8,128)} fusion(bf16[1024,2048]{1,0:T(8,128)(2,1)S(1)} %bitcast.372, bf16[2048,1536]{1,0:T(8,128)(2,1)S(1)} %bitcast.360), kind=kOutput, calls=%fused_computation.238 | convolution fusion | flops 6442450944 | bytes 16777216 | tf_op jit(solution)/shard_map/td,de->te/dot_general | solution.py:293
  217.4 7.5 %multiply_convert_fusion.2 = (bf16[1024,768]{0,1:T(8,128)(2,1)S(1)}, bf16[1024,768]{0,1:T(8,128)(2,1)S(1)}, bf16[1024,768]{0,1:T(8,128)(2,1)}) fusion(f32[1024,1536]{0,1:T(8,128)} %fusion.59, bf16[1024,2048]{1,0:T(8,128)(2,1)S(1)} %bitcast.374, bf16[768,2048]{1,0:T(8,128)(2,1)S(1)} %bitcast.390), kind=kOutput, calls=%fused_computation.18 | convolution fusion | flops 3233021952 | bytes 18350080 | tf_op jit(solution)/shard_map/td,fd->tf/dot_general | solution.py:293
  224.9 6.9 %convolution_convert_fusion.1 = bf16[1024,2048]{1,0:T(8,128)(2,1)S(1)} fusion(bf16[2048,1536]{1,0:T(8,128)(2,1)S(1)} %bitcast.361, bf16[1024,768]{0,1:T(8,128)(2,1)S(1)} %get-tuple-element.102, bf16[1024,768]{0,1:T(8,128)(2,1)S(1)} %get-tuple-element.101), kind=kOutput, calls=%fused_computation.9 | convolution fusion | flops 6450839552 | bytes 13631488 | tf_op jit(solution)/shard_map/tf,df->td/dot_general | solution.py:293
  239.0 7.2 %convolution_convert_fusion = bf16[2048,1536]{1,0:T(8,128)(2,1)S(1)} fusion(bf16[1024,2048]{1,0:T(8,128)(2,1)S(1)} %bitcast.373, bf16[1024,1536]{0,1:T(8,128)(2,1)S(1)} %pad_maximum_fusion), kind=kOutput, calls=%fused_computation.8 | convolution fusion | flops 6445596672 | bytes 13631488 | tf_op jit(solution)/shard_map/td,tf->df/dot_general | solution.py:293
  246.3 3.7 convolution_convert_fusion.5
  253.4 9.5 %maximum_maximum_fusion = bf16[16,192,1536]{2,1,0:T(8,128)(2,1)} fusion(bf16[16,16,512]{2,1,0:T(8,128)(2,1)S(1)} %get-tuple-element.138, bf16[16,16,512]{2,1,0:T(8,128)(2,1)S(1)} %get-tuple-element.139, bf16[16,16,512]{2,1,0:T(8,128)(2,1)S(1)} %get-tuple-element.137, bf16[16,48,1536]{2,1,0:T(8,128)(2,1)S(1)} %slice.346, bf16[16,128,1536]{2,1,0:T(8,128)(2,1)S(1)} %bitcast.362), kind=kLoop, calls=%fused_computation.4 | loop fusion | flops 47185920 | bytes 18874368 | tf_op jit(solution)/shard_map/concatenate | solution.py:417
  274.9 8.2 %collective-permute-done.48 = bf16[128,2048]{1,0:T(8,128)(2,1)S(1)} collective-permute-done((bf16[128,2048]{1,0:T(8,128)(2,1)S(1)}, bf16[128,2048]{1,0:T(8,128)(2,1)S(1)}, u32[]{:S(2)}, u32[]{:S(2)}) %collective-permute-start.48) | collective-permute-done | bytes 524320 | tf_op jit(solution)/shard_map/ppermute | solution.py:60
  288.7 5.9 %collective-permute-done.51 = bf16[64,2048]{1,0:T(8,128)(2,1)S(1)} collective-permute-done((bf16[64,2048]{1,0:T(8,128)(2,1)S(1)}, bf16[64,2048]{1,0:T(8,128)(2,1)S(1)}, u32[]{:S(2)}, u32[]{:S(2)}) %collective-permute-start.51) | collective-permute-done | bytes 262176 | tf_op jit(solution)/shard_map/ppermute | solution.py:60
  301.0 10.3 %attention_back.1 = (f32[1024,768]{1,0:T(8,128)S(1)}, f32[1,768]{1,0:T(1,128)S(1)}) custom-call(f32[1024,768]{1,0:T(8,128)S(1)} %copy-done.1, f32[1024,256]{1,0:T(8,128)S(1)} %fusion.60.grad_ref, f32[1024,256]{1,0:T(8,128)S(1)} %get-tuple-element.161.cos_ref, f32[1024,256]{1,0:T(8,128)S(1)} %get-tuple-element.160.sin_ref, f32[1024,2]{1,0:T(8,128)S(1)} %copy.186.colq_ref, ...), custom_call_target="tpu_custom_call" | custom-call | flops 2684354560 | bytes 6291456 | tf_op jit(solution)/shard_map/attention_back/pallas_call | solution.py:280
  311.4 8.7 %fusion.47 = (bf16[2048]{0:T(1024)(128)(2,1)S(1)}, bf16[2048]{0:T(1024)(128)(2,1)S(1)}, bf16[1024,2048]{1,0:T(8,128)(2,1)S(1)}, f32[1024,2048]{1,0:T(8,128)}) fusion(f32[1024]{0:T(1024)S(1)} %add_rsqrt_fusion, f32[1024]{0:T(1024)S(1)} %broadcast_multiply_fusion, bf16[1024,2048]{1,0:T(8,128)(2,1)} %bitcast.14, bf16[2048,896]{1,0:T(8,128)(2,1)S(1)} %bitcast.366, ...), kind=kOutput, calls=%fused_computation.227 | convolution fusion | flops 3236687872 | bytes 23085056 | tf_op jit(solution)/shard_map/te,de->td/dot_general | solution.py:293
  329.0 3.6 convert_add_fusion.6
  336.0 5.2 %convolution_convert_fusion.4 = bf16[2048,768]{1,0:T(8,128)(2,1)} fusion(bf16[1024,2048]{1,0:T(8,128)(2,1)S(1)} %copy-done.16, f32[1024,768]{1,0:T(8,128)S(1)} %copy-done.3), kind=kOutput, calls=%fused_computation.12 | convolution fusion | flops 3223584768 | bytes 10485760 | tf_op jit(solution)/shard_map/td,te->de/dot_general | solution.py:293
  342.9 9.0 %concatenate.119 = bf16[16,128,1152]{2,1,0:T(8,128)(2,1)} concatenate(bf16[16,128,768]{2,1,0:T(8,128)(2,1)} %bitcast.394, bf16[16,128,1]{2,1,0:T(8,128)(2,1)} %copy.201, bf16[16,128,1]{2,1,0:T(8,128)(2,1)} %copy.202, bf16[16,128,1]{2,1,0:T(8,128)(2,1)} %copy.203, bf16[16,128,1]{2,1,0:T(8,128)(2,1)} %copy.204, bf16[16,128,48]{2,1,0:T(8,128)(2,1)} %bitcast.397, ...), dimensions={2} | concatenate | bytes 9437184 | tf_op jit(solution)/shard_map/concatenate | solution.py:459
  352.0 4.8 %reduce-scatter.5.cloned.1.call-done = bf16[192,1536]{1,0:T(8,128)(2,1)} async-done(((bf16[3072,1536]{1,0:T(8,128)(2,1)}), bf16[192,1536]{1,0:T(8,128)(2,1)}) %reduce-scatter.5.cloned.1.call-update) | async-done | bytes 589840 | tf_op jit(solution)/shard_map/reduce_scatter | solution.py:425
  364.8 3.7 collective-permute-done.62
  368.6 2.8 collective-permute-start.63
  371.4 5.4 %collective-permute-done.60 = bf16[128,2048]{1,0:T(8,128)(2,1)S(1)} collective-permute-done((bf16[128,2048]{1,0:T(8,128)(2,1)S(1)}, bf16[128,2048]{1,0:T(8,128)(2,1)S(1)}, u32[]{:S(2)}, u32[]{:S(2)}) %collective-permute-start.60) | collective-permute-done | bytes 524320 | tf_op jit(solution)/shard_map/ppermute | solution.py:60
  376.7 5.1 %collective-permute-done.63 = bf16[128,2048]{1,0:T(8,128)(2,1)S(1)} collective-permute-done((bf16[128,2048]{1,0:T(8,128)(2,1)S(1)}, bf16[128,2048]{1,0:T(8,128)(2,1)S(1)}, u32[]{:S(2)}, u32[]{:S(2)}) %collective-permute-start.63) | collective-permute-done | bytes 524320 | tf_op jit(solution)/shard_map/ppermute | solution.py:60
  383.2 3.7 convolution_convert_fusion.3
  403.1 4.6 collective-permute-done.67
  409.5 3.2 collective-permute-start.71
  414.7 5.4 %collective-permute-start.73 = (bf16[44,2048]{1,0:T(8,128)(2,1)}, bf16[44,2048]{1,0:T(8,128)(2,1)}, u32[]{:S(2)}, u32[]{:S(2)}) collective-permute-start(bf16[44,2048]{1,0:T(8,128)(2,1)} %pad_maximum_fusion.12), channel_id=1, source_target_pairs={{0,0},{1,16},{2,1},{3,17},{4,2},{5,18},{6,3},{7,19},{8,4},{9,20},{... | collective-permute-start | bytes 540680 | tf_op jit(solution)/shard_map/ppermute | solution.py:463
  420.2 3.4 all-to-all-start.3
  423.6 3.5 fusion.14
  439.8 6.6 %all-to-all-start.2 = ((bf16[8,16,896]{2,1,0:T(8,128)(2,1)}), bf16[8,16,896]{2,1,0:T(8,128)(2,1)S(1)}, u32[]{:S(2)}, u32[]{:S(2)}) async-start(bf16[8,16,896]{2,1,0:T(8,128)(2,1)} %bitcast.151), calls=%async_computation.3 | async-start | bytes 458752 | tf_op jit(solution)/shard_map/all_to_all | solution.py:477
  446.4 4.3 collective-permute-start.72
  (458 shorter events, 192.2 us)
Async XLA Ops:
  13.1 14.5 %all-to-all-start = ((bf16[8,16,896]{2,1,0:T(8,128)(2,1)}), bf16[8,16,896]{2,1,0:T(8,128)(2,1)S(1)}, u32[]{:S(2)}, u32[]{:S(2)}) async-start(bf16[8,16,896]{2,1,0:T(8,128)(2,1)} %pad_maximum_fusion.11), calls=%async_computation | async-start | bytes 458752 | tf_op jit(solution)/shard_map/all_to_all | solution.py:329
  19.1 75.8 %all-gather.5.cloned.1.call-start = ((), (), s32[]{:S(2)}) async-start(), calls=%async_computation.7 | async-start | bytes 5013504 | tf_op jit(solution)/shard_map/all_gather | solution.py:344
  29.0 14.0 %collective-permute-start.1 = (bf16[128,2048]{1,0:T(8,128)(2,1)S(1)}, bf16[128,2048]{1,0:T(8,128)(2,1)S(1)}, u32[]{:S(2)}, u32[]{:S(2)}) collective-permute-start(bf16[128,2048]{1,0:T(8,128)(2,1)S(1)} %copy.172), channel_id=1, source_target_pairs={{0,32},{32,64},{64,96},{96,0},{1,33},{33,65},{65,97},{97,1},{2,34}... | collective-permute-start | bytes 1572872 | tf_op jit(solution)/shard_map/ppermute | solution.py:60
  30.5 12.6 %collective-permute-start.2 = (bf16[128,2048]{1,0:T(8,128)(2,1)S(1)}, bf16[128,2048]{1,0:T(8,128)(2,1)S(1)}, u32[]{:S(2)}, u32[]{:S(2)}) collective-permute-start(bf16[128,2048]{1,0:T(8,128)(2,1)S(1)} %copy.172), channel_id=1, source_target_pairs={{0,96},{32,0},{64,32},{96,64},{1,97},{33,1},{65,33},{97,65},{2,98}... | collective-permute-start | bytes 1572872 | tf_op jit(solution)/shard_map/ppermute | solution.py:60
  31.7 14.9 %collective-permute-start = (bf16[128,2048]{1,0:T(8,128)(2,1)S(1)}, bf16[128,2048]{1,0:T(8,128)(2,1)S(1)}, u32[]{:S(2)}, u32[]{:S(2)}) collective-permute-start(bf16[128,2048]{1,0:T(8,128)(2,1)S(1)} %copy.172), channel_id=1, source_target_pairs={{0,1},{1,0},{2,3},{3,2},{4,5},{5,4},{6,7},{7,6},{8,9},{9,8},{10,11... | collective-permute-start | bytes 1572872 | tf_op jit(solution)/shard_map/ppermute | solution.py:60
  43.0 10.9 %collective-permute-start.3 = (bf16[128,2048]{1,0:T(8,128)(2,1)S(1)}, bf16[128,2048]{1,0:T(8,128)(2,1)S(1)}, u32[]{:S(2)}, u32[]{:S(2)}) collective-permute-start(bf16[128,2048]{1,0:T(8,128)(2,1)S(1)} %collective-permute-done.2), channel_id=1, source_target_pairs={{0,1},{1,0},{2,3},{3,2},{4,5},{5,4},{6,7},{7,6},{8,9},{9,8},{10,11... | collective-permute-start | bytes 1572872 | tf_op jit(solution)/shard_map/ppermute | solution.py:60
  43.1 15.4 %collective-permute-start.8 = (bf16[128,2048]{1,0:T(8,128)(2,1)S(1)}, bf16[128,2048]{1,0:T(8,128)(2,1)S(1)}, u32[]{:S(2)}, u32[]{:S(2)}) collective-permute-start(bf16[128,2048]{1,0:T(8,128)(2,1)S(1)} %collective-permute-done.1), channel_id=1, source_target_pairs={{0,1},{1,0},{2,3},{3,2},{4,5},{5,4},{6,7},{7,6},{8,9},{9,8},{10,11... | collective-permute-start | bytes 1572872 | tf_op jit(solution)/shard_map/ppermute | solution.py:60
  43.7 9.7 %collective-permute-start.4 = (bf16[64,2048]{1,0:T(8,128)(2,1)S(1)}, bf16[64,2048]{1,0:T(8,128)(2,1)S(1)}, u32[]{:S(2)}, u32[]{:S(2)}) collective-permute-start(bf16[64,2048]{1,0:T(8,128)(2,1)S(1)} %slice.245), channel_id=1, source_target_pairs={{0,32},{32,64},{64,96},{96,0},{1,33},{33,65},{65,97},{97,1},{2,34}... | collective-permute-start | bytes 786440 | tf_op jit(solution)/shard_map/ppermute | solution.py:60
  43.7 10.2 %collective-permute-start.5 = (bf16[64,2048]{1,0:T(8,128)(2,1)S(1)}, bf16[64,2048]{1,0:T(8,128)(2,1)S(1)}, u32[]{:S(2)}, u32[]{:S(2)}) collective-permute-start(bf16[64,2048]{1,0:T(8,128)(2,1)S(1)} %slice.246), channel_id=1, source_target_pairs={{0,96},{32,0},{64,32},{96,64},{1,97},{33,1},{65,33},{97,65},{2,98}... | collective-permute-start | bytes 786440 | tf_op jit(solution)/shard_map/ppermute | solution.py:60
  59.7 13.7 %collective-permute-start.31 = (bf16[44,2048]{1,0:T(8,128)(2,1)}, bf16[44,2048]{1,0:T(8,128)(2,1)S(1)}, u32[]{:S(2)}, u32[]{:S(2)}) collective-permute-start(bf16[44,2048]{1,0:T(8,128)(2,1)} %param.27), channel_id=1, source_target_pairs={{0,0},{16,1},{1,2},{17,3},{2,4},{18,5},{3,6},{19,7},{4,8},{20,9},{... | collective-permute-start | bytes 540680 | tf_op jit(solution)/shard_map/ppermute | solution.py:359
  65.7 11.9 %all-to-all-start.1 = ((bf16[8,16,1536]{2,1,0:T(8,128)(2,1)}), bf16[8,16,1536]{2,1,0:T(8,128)(2,1)S(1)}, u32[]{:S(2)}, u32[]{:S(2)}) async-start(bf16[8,16,1536]{2,1,0:T(8,128)(2,1)} %pad_maximum_fusion.9), calls=%async_computation.1 | async-start | bytes 786432 | tf_op jit(solution)/shard_map/all_to_all | solution.py:358
  69.5 109.7 %all-gather.7.cloned.1.call-start = ((), (), s32[]{:S(2)}) async-start(), calls=%async_computation.8 | async-start | bytes 10027008 | tf_op jit(solution)/shard_map/all_gather | solution.py:372
  78.5 278.3 %reduce-scatter.5.cloned.1.call-start = ((), (), s32[]{:S(2)}) async-start(), calls=%async_computation.6 | async-start | bytes 10027008 | tf_op jit(solution)/shard_map/reduce_scatter | solution.py:425
  94.9 32.0 %collective-permute-start.21 = (bf16[128,2048]{1,0:T(8,128)(2,1)S(1)}, bf16[128,2048]{1,0:T(8,128)(2,1)}, u32[]{:S(2)}, u32[]{:S(2)}) collective-permute-start(bf16[128,2048]{1,0:T(8,128)(2,1)S(1)} %copy.175), channel_id=1, source_target_pairs={{0,32},{32,64},{64,96},{96,0},{1,33},{33,65},{65,97},{97,1},{2,34}... | collective-permute-start | bytes 1572872 | tf_op jit(solution)/shard_map/ppermute | solution.py:60
  95.2 31.8 %collective-permute-start.22 = (bf16[128,2048]{1,0:T(8,128)(2,1)S(1)}, bf16[128,2048]{1,0:T(8,128)(2,1)}, u32[]{:S(2)}, u32[]{:S(2)}) collective-permute-start(bf16[128,2048]{1,0:T(8,128)(2,1)S(1)} %copy.175), channel_id=1, source_target_pairs={{0,96},{32,0},{64,32},{96,64},{1,97},{33,1},{65,33},{97,65},{2,98}... | collective-permute-start | bytes 1572872 | tf_op jit(solution)/shard_map/ppermute | solution.py:60
  127.0 39.6 %collective-permute-start.12 = (bf16[128,2048]{1,0:T(8,128)(2,1)S(1)}, bf16[128,2048]{1,0:T(8,128)(2,1)S(1)}, u32[]{:S(2)}, u32[]{:S(2)}) collective-permute-start(bf16[128,2048]{1,0:T(8,128)(2,1)S(1)} %get-tuple-element.130), channel_id=1, source_target_pairs={{0,1},{1,0},{2,3},{3,2},{4,5},{5,4},{6,7},{7,6},{8,9},{9,8},{10,11... | collective-permute-start | bytes 1572872 | tf_op jit(solution)/shard_map/ppermute | solution.py:60
  129.4 24.3 %collective-permute-start.23 = (bf16[128,2048]{1,0:T(8,128)(2,1)}, bf16[128,2048]{1,0:T(8,128)(2,1)S(1)}, u32[]{:S(2)}, u32[]{:S(2)}) collective-permute-start(bf16[128,2048]{1,0:T(8,128)(2,1)} %collective-permute-done.22), channel_id=1, source_target_pairs={{0,1},{1,0},{2,3},{3,2},{4,5},{5,4},{6,7},{7,6},{8,9},{9,8},{10,11... | collective-permute-start | bytes 1572872 | tf_op jit(solution)/shard_map/ppermute | solution.py:60
  129.6 37.0 %collective-permute-start.28 = (bf16[128,2048]{1,0:T(8,128)(2,1)}, bf16[128,2048]{1,0:T(8,128)(2,1)S(1)}, u32[]{:S(2)}, u32[]{:S(2)}) collective-permute-start(bf16[128,2048]{1,0:T(8,128)(2,1)} %collective-permute-done.21), channel_id=1, source_target_pairs={{0,1},{1,0},{2,3},{3,2},{4,5},{5,4},{6,7},{7,6},{8,9},{9,8},{10,11... | collective-permute-start | bytes 1572872 | tf_op jit(solution)/shard_map/ppermute | solution.py:60
  130.0 23.8 %collective-permute-start.24 = (bf16[64,2048]{1,0:T(8,128)(2,1)S(1)}, bf16[64,2048]{1,0:T(8,128)(2,1)S(1)}, u32[]{:S(2)}, u32[]{:S(2)}) collective-permute-start(bf16[64,2048]{1,0:T(8,128)(2,1)S(1)} %slice.261), channel_id=1, source_target_pairs={{0,32},{32,64},{64,96},{96,0},{1,33},{33,65},{65,97},{97,1},{2,34}... | collective-permute-start | bytes 786440 | tf_op jit(solution)/shard_map/ppermute | solution.py:60
  130.7 14.1 %collective-permute-start.15 = (bf16[64,2048]{1,0:T(8,128)(2,1)S(1)}, bf16[64,2048]{1,0:T(8,128)(2,1)S(1)}, u32[]{:S(2)}, u32[]{:S(2)}) collective-permute-start(bf16[64,2048]{1,0:T(8,128)(2,1)S(1)} %get-tuple-element.149), channel_id=1, source_target_pairs={{0,32},{32,64},{64,96},{96,0},{1,33},{33,65},{65,97},{97,1},{2,34}... | collective-permute-start | bytes 786440 | tf_op jit(solution)/shard_map/ppermute | solution.py:60
  153.7 13.3 %collective-permute-start.16 = (bf16[128,2048]{1,0:T(8,128)(2,1)S(1)}, bf16[128,2048]{1,0:T(8,128)(2,1)S(1)}, u32[]{:S(2)}, u32[]{:S(2)}) collective-permute-start(bf16[128,2048]{1,0:T(8,128)(2,1)S(1)} %pad_maximum_fusion.1), channel_id=1, source_target_pairs={{0,32},{32,64},{64,96},{96,0},{1,33},{33,65},{65,97},{97,1},{2,34}... | collective-permute-start | bytes 1572872 | tf_op jit(solution)/shard_map/ppermute | solution.py:60
  153.8 15.6 %collective-permute-start.19 = (bf16[128,2048]{1,0:T(8,128)(2,1)S(1)}, bf16[128,2048]{1,0:T(8,128)(2,1)S(1)}, u32[]{:S(2)}, u32[]{:S(2)}) collective-permute-start(bf16[128,2048]{1,0:T(8,128)(2,1)S(1)} %pad_maximum_fusion.2), channel_id=1, source_target_pairs={{0,96},{32,0},{64,32},{96,64},{1,97},{33,1},{65,33},{97,65},{2,98}... | collective-permute-start | bytes 1572872 | tf_op jit(solution)/shard_map/ppermute | solution.py:60
  174.0 18.4 %collective-permute-start.32 = (bf16[128,2048]{1,0:T(8,128)(2,1)}, bf16[128,2048]{1,0:T(8,128)(2,1)}, u32[]{:S(2)}, u32[]{:S(2)}) collective-permute-start(bf16[128,2048]{1,0:T(8,128)(2,1)} %get-tuple-element.98), channel_id=1, source_target_pairs={{0,1},{1,0},{2,3},{3,2},{4,5},{5,4},{6,7},{7,6},{8,9},{9,8},{10,11... | collective-permute-start | bytes 1572872 | tf_op jit(solution)/shard_map/ppermute | solution.py:60
  176.5 15.2 %collective-permute-start.29 = (bf16[128,2048]{1,0:T(8,128)(2,1)}, bf16[128,2048]{1,0:T(8,128)(2,1)}, u32[]{:S(2)}, u32[]{:S(2)}) collective-permute-start(bf16[128,2048]{1,0:T(8,128)(2,1)} %get-tuple-element.98), channel_id=1, source_target_pairs={{0,32},{32,64},{64,96},{96,0},{1,33},{33,65},{65,97},{97,1},{2,34}... | collective-permute-start | bytes 1572872 | tf_op jit(solution)/shard_map/ppermute | solution.py:60
  176.5 15.2 %collective-permute-start.30 = (bf16[128,2048]{1,0:T(8,128)(2,1)}, bf16[128,2048]{1,0:T(8,128)(2,1)}, u32[]{:S(2)}, u32[]{:S(2)}) collective-permute-start(bf16[128,2048]{1,0:T(8,128)(2,1)} %get-tuple-element.98), channel_id=1, source_target_pairs={{0,96},{32,0},{64,32},{96,64},{1,97},{33,1},{65,33},{97,65},{2,98}... | collective-permute-start | bytes 1572872 | tf_op jit(solution)/shard_map/ppermute | solution.py:60
  191.7 14.2 %collective-permute-start.33 = (bf16[128,2048]{1,0:T(8,128)(2,1)}, bf16[128,2048]{1,0:T(8,128)(2,1)S(1)}, u32[]{:S(2)}, u32[]{:S(2)}) collective-permute-start(bf16[128,2048]{1,0:T(8,128)(2,1)} %collective-permute-done.30), channel_id=1, source_target_pairs={{0,1},{1,0},{2,3},{3,2},{4,5},{5,4},{6,7},{7,6},{8,9},{9,8},{10,11... | collective-permute-start | bytes 1572872 | tf_op jit(solution)/shard_map/ppermute | solution.py:60
  195.4 13.1 %collective-permute-start.38 = (bf16[128,2048]{1,0:T(8,128)(2,1)}, bf16[128,2048]{1,0:T(8,128)(2,1)S(1)}, u32[]{:S(2)}, u32[]{:S(2)}) collective-permute-start(bf16[128,2048]{1,0:T(8,128)(2,1)} %collective-permute-done.29), channel_id=1, source_target_pairs={{0,1},{1,0},{2,3},{3,2},{4,5},{5,4},{6,7},{7,6},{8,9},{9,8},{10,11... | collective-permute-start | bytes 1572872 | tf_op jit(solution)/shard_map/ppermute | solution.py:60
  232.8 30.1 %collective-permute-start.39 = (bf16[128,2048]{1,0:T(8,128)(2,1)S(1)}, bf16[128,2048]{1,0:T(8,128)(2,1)S(1)}, u32[]{:S(2)}, u32[]{:S(2)}) collective-permute-start(bf16[128,2048]{1,0:T(8,128)(2,1)S(1)} %get-tuple-element.123), channel_id=1, source_target_pairs={{0,1},{1,0},{2,3},{3,2},{4,5},{5,4},{6,7},{7,6},{8,9},{9,8},{10,11... | collective-permute-start | bytes 1572872 | tf_op jit(solution)/shard_map/ppermute | solution.py:60
  236.1 14.2 %collective-permute-start.42 = (bf16[64,2048]{1,0:T(8,128)(2,1)S(1)}, bf16[64,2048]{1,0:T(8,128)(2,1)S(1)}, u32[]{:S(2)}, u32[]{:S(2)}) collective-permute-start(bf16[64,2048]{1,0:T(8,128)(2,1)S(1)} %get-tuple-element.147), channel_id=1, source_target_pairs={{0,32},{32,64},{64,96},{96,0},{1,33},{33,65},{65,97},{97,1},{2,34}... | collective-permute-start | bytes 786440 | tf_op jit(solution)/shard_map/ppermute | solution.py:60
  236.9 13.6 %collective-permute-start.45 = (bf16[64,2048]{1,0:T(8,128)(2,1)S(1)}, bf16[64,2048]{1,0:T(8,128)(2,1)S(1)}, u32[]{:S(2)}, u32[]{:S(2)}) collective-permute-start(bf16[64,2048]{1,0:T(8,128)(2,1)S(1)} %get-tuple-element.148), channel_id=1, source_target_pairs={{0,96},{32,0},{64,32},{96,64},{1,97},{33,1},{65,33},{97,65},{2,98}... | collective-permute-start | bytes 786440 | tf_op jit(solution)/shard_map/ppermute | solution.py:60
  250.4 14.0 %collective-permute-start.43 = (bf16[128,2048]{1,0:T(8,128)(2,1)S(1)}, bf16[128,2048]{1,0:T(8,128)(2,1)S(1)}, u32[]{:S(2)}, u32[]{:S(2)}) collective-permute-start(bf16[128,2048]{1,0:T(8,128)(2,1)S(1)} %pad_maximum_fusion.3), channel_id=1, source_target_pairs={{0,32},{32,64},{64,96},{96,0},{1,33},{33,65},{65,97},{97,1},{2,34}... | collective-permute-start | bytes 1572872 | tf_op jit(solution)/shard_map/ppermute | solution.py:60
  250.6 13.8 %collective-permute-start.46 = (bf16[128,2048]{1,0:T(8,128)(2,1)S(1)}, bf16[128,2048]{1,0:T(8,128)(2,1)S(1)}, u32[]{:S(2)}, u32[]{:S(2)}) collective-permute-start(bf16[128,2048]{1,0:T(8,128)(2,1)S(1)} %pad_maximum_fusion.4), channel_id=1, source_target_pairs={{0,96},{32,0},{64,32},{96,64},{1,97},{33,1},{65,33},{97,65},{2,98}... | collective-permute-start | bytes 1572872 | tf_op jit(solution)/shard_map/ppermute | solution.py:60
  265.8 171.6 %reduce-scatter.7.cloned.1.call-start = ((), (), s32[]{:S(2)}) async-start(), calls=%async_computation.9 | async-start | bytes 5013504
  270.1 13.0 %collective-permute-start.48 = (bf16[128,2048]{1,0:T(8,128)(2,1)S(1)}, bf16[128,2048]{1,0:T(8,128)(2,1)S(1)}, u32[]{:S(2)}, u32[]{:S(2)}) collective-permute-start(bf16[128,2048]{1,0:T(8,128)(2,1)S(1)} %get-tuple-element.95), channel_id=1, source_target_pairs={{0,32},{32,64},{64,96},{96,0},{1,33},{33,65},{65,97},{97,1},{2,34}... | collective-permute-start | bytes 1572872 | tf_op jit(solution)/shard_map/ppermute | solution.py:60
  270.1 13.0 %collective-permute-start.49 = (bf16[128,2048]{1,0:T(8,128)(2,1)S(1)}, bf16[128,2048]{1,0:T(8,128)(2,1)S(1)}, u32[]{:S(2)}, u32[]{:S(2)}) collective-permute-start(bf16[128,2048]{1,0:T(8,128)(2,1)S(1)} %get-tuple-element.95), channel_id=1, source_target_pairs={{0,96},{32,0},{64,32},{96,64},{1,97},{33,1},{65,33},{97,65},{2,98}... | collective-permute-start | bytes 1572872 | tf_op jit(solution)/shard_map/ppermute | solution.py:60
  272.7 15.8 %collective-permute-start.47 = (bf16[128,2048]{1,0:T(8,128)(2,1)S(1)}, bf16[128,2048]{1,0:T(8,128)(2,1)S(1)}, u32[]{:S(2)}, u32[]{:S(2)}) collective-permute-start(bf16[128,2048]{1,0:T(8,128)(2,1)S(1)} %get-tuple-element.95), channel_id=1, source_target_pairs={{0,1},{1,0},{2,3},{3,2},{4,5},{5,4},{6,7},{7,6},{8,9},{9,8},{10,11... | collective-permute-start | bytes 1572872 | tf_op jit(solution)/shard_map/ppermute | solution.py:60
  283.1 12.9 %collective-permute-start.50 = (bf16[128,2048]{1,0:T(8,128)(2,1)S(1)}, bf16[128,2048]{1,0:T(8,128)(2,1)S(1)}, u32[]{:S(2)}, u32[]{:S(2)}) collective-permute-start(bf16[128,2048]{1,0:T(8,128)(2,1)S(1)} %collective-permute-done.49), channel_id=1, source_target_pairs={{0,1},{1,0},{2,3},{3,2},{4,5},{5,4},{6,7},{7,6},{8,9},{9,8},{10,11... | collective-permute-start | bytes 1572872 | tf_op jit(solution)/shard_map/ppermute | solution.py:60
  285.7 11.9 %collective-permute-start.55 = (bf16[128,2048]{1,0:T(8,128)(2,1)S(1)}, bf16[128,2048]{1,0:T(8,128)(2,1)S(1)}, u32[]{:S(2)}, u32[]{:S(2)}) collective-permute-start(bf16[128,2048]{1,0:T(8,128)(2,1)S(1)} %collective-permute-done.48), channel_id=1, source_target_pairs={{0,1},{1,0},{2,3},{3,2},{4,5},{5,4},{6,7},{7,6},{8,9},{9,8},{10,11... | collective-permute-start | bytes 1572872 | tf_op jit(solution)/shard_map/ppermute | solution.py:60
  358.4 12.9 %collective-permute-start.56 = (bf16[128,2048]{1,0:T(8,128)(2,1)S(1)}, bf16[128,2048]{1,0:T(8,128)(2,1)S(1)}, u32[]{:S(2)}, u32[]{:S(2)}) collective-permute-start(bf16[128,2048]{1,0:T(8,128)(2,1)S(1)} %copy-done.40), channel_id=1, source_target_pairs={{0,1},{1,0},{2,3},{3,2},{4,5},{5,4},{6,7},{7,6},{8,9},{9,8},{10,11... | collective-permute-start | bytes 1572872 | tf_op jit(solution)/shard_map/ppermute | solution.py:60
  364.7 12.1 %collective-permute-start.60 = (bf16[128,2048]{1,0:T(8,128)(2,1)S(1)}, bf16[128,2048]{1,0:T(8,128)(2,1)S(1)}, u32[]{:S(2)}, u32[]{:S(2)}) collective-permute-start(bf16[128,2048]{1,0:T(8,128)(2,1)S(1)} %pad_maximum_fusion.5), channel_id=1, source_target_pairs={{0,32},{32,64},{64,96},{96,0},{1,33},{33,65},{65,97},{97,1},{2,34}... | collective-permute-start | bytes 1572872 | tf_op jit(solution)/shard_map/ppermute | solution.py:60
  368.6 13.2 %collective-permute-start.63 = (bf16[128,2048]{1,0:T(8,128)(2,1)S(1)}, bf16[128,2048]{1,0:T(8,128)(2,1)S(1)}, u32[]{:S(2)}, u32[]{:S(2)}) collective-permute-start(bf16[128,2048]{1,0:T(8,128)(2,1)S(1)} %pad_maximum_fusion.6), channel_id=1, source_target_pairs={{0,96},{32,0},{64,32},{96,64},{1,97},{33,1},{65,33},{97,65},{2,98}... | collective-permute-start | bytes 1572872 | tf_op jit(solution)/shard_map/ppermute | solution.py:60
  392.4 31.2 %collective-permute-start.64 = (bf16[128,2048]{1,0:T(8,128)(2,1)}, bf16[128,2048]{1,0:T(8,128)(2,1)}, u32[]{:S(2)}, u32[]{:S(2)}) collective-permute-start(bf16[128,2048]{1,0:T(8,128)(2,1)} %get-tuple-element.109), channel_id=1, source_target_pairs={{0,1},{1,0},{2,3},{3,2},{4,5},{5,4},{6,7},{7,6},{8,9},{9,8},{10,11... | collective-permute-start | bytes 1572872 | tf_op jit(solution)/shard_map/ppermute | solution.py:60
  397.8 9.8 %collective-permute-start.67 = (bf16[64,2048]{1,0:T(8,128)(2,1)S(1)}, bf16[64,2048]{1,0:T(8,128)(2,1)S(1)}, u32[]{:S(2)}, u32[]{:S(2)}) collective-permute-start(bf16[64,2048]{1,0:T(8,128)(2,1)S(1)} %get-tuple-element.143), channel_id=1, source_target_pairs={{0,32},{32,64},{64,96},{96,0},{1,33},{33,65},{65,97},{97,1},{2,34}... | collective-permute-start | bytes 786440 | tf_op jit(solution)/shard_map/ppermute | solution.py:60
  408.6 15.0 %collective-permute-start.68 = (bf16[128,2048]{1,0:T(8,128)(2,1)}, bf16[128,2048]{1,0:T(8,128)(2,1)}, u32[]{:S(2)}, u32[]{:S(2)}) collective-permute-start(bf16[128,2048]{1,0:T(8,128)(2,1)} %pad_maximum_fusion.7), channel_id=1, source_target_pairs={{0,32},{32,64},{64,96},{96,0},{1,33},{33,65},{65,97},{97,1},{2,34}... | collective-permute-start | bytes 1572872 | tf_op jit(solution)/shard_map/ppermute | solution.py:60
  409.5 14.1 %collective-permute-start.71 = (bf16[128,2048]{1,0:T(8,128)(2,1)}, bf16[128,2048]{1,0:T(8,128)(2,1)}, u32[]{:S(2)}, u32[]{:S(2)}) collective-permute-start(bf16[128,2048]{1,0:T(8,128)(2,1)} %pad_maximum_fusion.8), channel_id=1, source_target_pairs={{0,96},{32,0},{64,32},{96,64},{1,97},{33,1},{65,33},{97,65},{2,98}... | collective-permute-start | bytes 1572872 | tf_op jit(solution)/shard_map/ppermute | solution.py:60
  414.7 17.1 %collective-permute-start.73 = (bf16[44,2048]{1,0:T(8,128)(2,1)}, bf16[44,2048]{1,0:T(8,128)(2,1)}, u32[]{:S(2)}, u32[]{:S(2)}) collective-permute-start(bf16[44,2048]{1,0:T(8,128)(2,1)} %pad_maximum_fusion.12), channel_id=1, source_target_pairs={{0,0},{1,16},{2,1},{3,17},{4,2},{5,18},{6,3},{7,19},{8,4},{9,20},{... | collective-permute-start | bytes 540680 | tf_op jit(solution)/shard_map/ppermute | solution.py:463
  420.2 14.9 %all-to-all-start.3 = ((bf16[8,16,1536]{2,1,0:T(8,128)(2,1)}), bf16[8,16,1536]{2,1,0:T(8,128)(2,1)S(1)}, u32[]{:S(2)}, u32[]{:S(2)}) async-start(bf16[8,16,1536]{2,1,0:T(8,128)(2,1)} %bitcast.407), calls=%async_computation.4 | async-start | bytes 786432 | tf_op jit(solution)/shard_map/all_to_all | solution.py:465
  439.8 14.8 %all-to-all-start.2 = ((bf16[8,16,896]{2,1,0:T(8,128)(2,1)}), bf16[8,16,896]{2,1,0:T(8,128)(2,1)S(1)}, u32[]{:S(2)}, u32[]{:S(2)}) async-start(bf16[8,16,896]{2,1,0:T(8,128)(2,1)} %bitcast.151), calls=%async_computation.3 | async-start | bytes 458752 | tf_op jit(solution)/shard_map/all_to_all | solution.py:477
  (84 other events, 667.4 us)
Sparse Core Ops, SparseCore 0:
  28.5 61.1 all-gather.4
  91.9 75.5 all-gather.6
  265.9 90.7 reduce-scatter.4
  360.3 76.9 reduce-scatter.6

commit v3 on v2

--- a/solution.py
+++ b/solution.py
@@ -80,20 +80,22 @@
 EVERY = tuple((r, k) for r in range(NY) for k in range(NC))
 
 
-def gather_y(own, half, hold):
+def gather_y(own, half, hold, late=None):
     from_prev = send(own, y=1)
     from_next = send(own, y=-1)
     from_prev, from_next, hold = lax.optimization_barrier((from_prev, from_next, hold))
     top = send(from_prev[:half], y=1)
     bottom = send(from_next[half:], y=-1)
+    if late:
+        top, bottom, hold = lax.optimization_barrier((top, bottom, late(*hold)))
     blocks = {(0, 0): (own,), (1, 0): (from_next,), (3, 0): (from_prev,), (2, 0): (top, bottom)}
     for r in (0, 1, 3, 2):
         blocks[(r, 1)] = tuple(send(b, c=1) for b in blocks[(r, 0)])
     return blocks, hold
 
 
-def gather_rows(own, place, hold=()):
-    blocks, hold = gather_y(own, TOK // 2, hold)
+def gather_rows(own, place, hold=(), late=None):
+    blocks, hold = gather_y(own, TOK // 2, hold, late)
     whole = jnp.zeros((NT,) + own.shape, own.dtype)
     for s in EVERY:
         at = 0
@@ -107,19 +109,11 @@
 def reduce_y(total, place, hold=()):
     total = total.reshape(NT, TOK, D)
     part = lambda r, k: lax.dynamic_index_in_dim(total, place.block(r, k), keepdims=False)
-    sums = {}
-    half = TOK // 2
-    for r in (2, 1, 3, 0):
-        other = send(part(r, 1), c=1)
-        sums[r] = part(r, 0).astype(f32) + other.astype(f32)
-    far, hold = lax.optimization_barrier((sums[2].astype(bf16), hold))
-    top = send(far[:half], y=1)
-    bottom = send(far[half:], y=-1)
-    one = jnp.concatenate([sums[1][:half] + top.astype(f32), sums[1][half:]], axis=0).astype(bf16)
-    three = jnp.concatenate([sums[3][:half], sums[3][half:] + bottom.astype(f32)], axis=0).astype(bf16)
-    from_prev = send(one, y=1)
-    from_next = send(three, y=-1)
-    out = sums[0] + from_prev.astype(f32) + from_next.astype(f32)
+    sums = {r: part(r, 0).astype(f32) + send(part(r, 1), c=1).astype(f32) for r in (2, 1, 3, 0)}
+    away, hold = lax.optimization_barrier(({r: sums[r].astype(bf16) for r in (2, 1, 3)}, hold))
+    out = sums[0]
+    for r in (2, 1, 3):
+        out = out + send(away[r], y=r).astype(f32)
     return (out, hold) if hold else out
 
 
@@ -374,7 +368,6 @@
     down_w = unpack_down(second_w[:, NT * ROWS :]).reshape(FT, D)
 
     cot_later, first_w = lax.optimization_barrier((cot, first_w))
-    grad_top = gather_rows(cot_later, place)
     out_w = first_w[:, :, 3 * HC + EXTRA :].reshape(NXZ, NT, ROWS, HC).transpose(0, 2, 1, 3).reshape(HC, D)
     first_w = first_w[:, :, : 3 * HC + EXTRA].reshape(D, 3 * HC + EXTRA)
     joined_w = first_w[:, : 3 * HC]
@@ -389,7 +382,8 @@
     mean_one, inv_one = norm_stats(tokens_f)
     hidden1 = ((tokens_f - mean_one) * inv_one * gain_one + shift_one).astype(bf16)
     projected = mm("td,de->te", hidden1, joined_w)
-    qkv, mixed = attention(projected, bias, cosine, sine, colq, rowk)
+    run = lambda projected: attention(projected, bias, cosine, sine, colq, rowk)
+    grad_top, (qkv, mixed) = gather_rows(cot_later, place, (projected,), run)
     mixed = mixed.astype(bf16)
     attended = mm("td,de->te", mixed, out_w).astype(bf16)
     resid = layer_pi.astype(f32) + reduce_y(attended, place)
@@ -427,19 +421,11 @@
     branch_all = gather_rows(grad_branch, place)
     grad_mixed = mm("te,de->td", branch_all, out_w)
     grad_proj, bias_part = attention_back(qkv, grad_mixed, cosine, sine, colq, rowk)
-    grad_proj = grad_proj.astype(bf16)
+    grad_proj, mixed, branch_all = lax.optimization_barrier((grad_proj.astype(bf16), mixed, branch_all))
     h1_part = mm("te,de->td", grad_proj, joined_w)
     normed1 = (tokens_f - mean_one) * inv_one
     gain_one_part = jnp.sum(h1_part * normed1, axis=0)
     shift_one_part = jnp.sum(h1_part, axis=0)
-    later = (hidden1, mixed, branch_all)
-    grad_h1, (hidden1, mixed, branch_all) = reduce_y(h1_part.astype(bf16), place, later)
-    grad_h1, product = lax.optimization_barrier((grad_h1, product))
-    out_part = mm("tf,fd->td", product, down_w).astype(bf16)
-    layer_out = from_pi((resid + reduce_y(out_part, place)).astype(bf16))[None]
-    input_grad = grad_resid + norm_back(grad_h1, own_rows(normed1), own_rows(inv_one), gain_one)
-    input_grad = from_pi(input_grad.astype(bf16))[None]
-
     out_grad = mm("td,te->de", mixed, branch_all).astype(bf16).reshape(NXZ, ROWS, D)
     joined_grad = mm("td,te->de", hidden1, grad_proj)
     bias_block = jnp.broadcast_to(bias_part.reshape(1, ROWS, 3 * HC // ROWS), (D // ROWS, ROWS, 3 * HC // ROWS))
@@ -454,11 +440,20 @@
         ],
         axis=1,
     )
-    joined_chunks = jnp.concatenate([joined_grad, extra], axis=1).astype(bf16).reshape(NXZ, NT * ROWS, 3 * HC + EXTRA)
+    blocks = lambda a: a.astype(bf16).reshape(NXZ, NT * ROWS, a.shape[-1])
     out_chunks = out_grad.reshape(NXZ, ROWS, NT, HC).transpose(0, 2, 1, 3).reshape(NXZ, NT * ROWS, HC)
-    first_chunks = jnp.concatenate([joined_chunks, out_chunks], axis=2)
-    first_chunks, second_sum = lax.optimization_barrier((first_chunks, second_sum))
-    first_sum = lax.psum_scatter(first_chunks, XZ, scatter_dimension=0)
+    extra = lax.optimization_barrier(blocks(extra))
+    first_chunks = jnp.concatenate([blocks(joined_grad), extra, out_chunks], axis=2)
+    hold = (first_chunks, second_sum, h1_part.astype(bf16), product)
+    first_chunks, second_sum, h1_part, product = lax.optimization_barrier(hold)
+    first_sum = lax.psum_scatter(first_chunks.reshape(D, -1), XZ, scatter_dimension=0, tiled=True)
+    grad_h1 = reduce_y(h1_part, place)
+    out_part = mm("tf,fd->td", product, down_w).astype(bf16)
+    layer_out = from_pi((resid + reduce_y(out_part, place)).astype(bf16))[None]
+    input_grad = grad_resid + norm_back(grad_h1, own_rows(normed1), own_rows(inv_one), gain_one)
+    input_grad = from_pi(input_grad.astype(bf16))[None]
+
+    first_sum, layer_out, input_grad = lax.optimization_barrier((first_sum, layer_out, input_grad))
     down_sum = unpack_down(second_sum[NT * ROWS :])[:FROWS]
     down_sum = from_pi(lax.ppermute(plain(down_sum), ("x", "z", "c"), pairs)).astype(f32)
     gate_up_sum = second_sum[: NT * ROWS].reshape(NT, ROWS, 2 * FT)
@@ -471,7 +466,7 @@
     gate_sum = weight_cols(gate_up_sum[:, :, :FT])
     up_sum = weight_cols(gate_up_sum[:, :, FT:])
 
-    out_mine = first_sum[:, 3 * HC + EXTRA :].reshape(NT, ROWS, HC).transpose(1, 0, 2).reshape(ROWS, D)
+    out_mine = first_sum[:, 3 * HC + EXTRA : 4 * HC + EXTRA].reshape(NT, ROWS, HC).transpose(1, 0, 2).reshape(ROWS, D)
     out_sum = from_pi(lax.ppermute(out_mine, ("x", "z", "c"), pairs)).astype(f32)
     joined_sum = first_sum[:, : 3 * HC + EXTRA].reshape(NT, ROWS, 3 * HC + EXTRA)
     joined_sum = lax.all_to_all(joined_sum, YC, 0, 0, tiled=True).astype(f32)

time: 473 us -> 473 us (level)
  the two profiles are of different devices: /device:TPU:1 before, /device:TPU:74 now
where the time goes in v3:
time: 473 us; the launch traced here: 465 us
  waiting for transfers between devices  126 us (27%)
  local copies, waits for them, and re-layouts  100 us (21%)
  starting transfers between devices  83.3 us (18%)
  matrix products  74.7 us (16%)
  other arithmetic  47.2 us (10%)
  Pallas kernels  17 us (4%)
  between operations  15.5 us (3%)
    ppermute x66, waiting for transfers between devices, send(): return plain(lax.ppermute(plain(value), axes, shift_perm(axes, deltas)))  113 us
    dot_general x16, matrix products, mm(): return jnp.einsum(spec, a, b, preferred_element_type=f32)  74.7 us
    ppermute x66, starting transfers between devices, send(): return plain(lax.ppermute(plain(value), axes, shift_perm(axes, deltas)))  47.1 us
    dynamic_update_slice x38, local copies, waits for them, and re-layouts, gather_rows(): whole = lax.dynamic_update_slice(whole, b[None], (place.block(*s), at, 0))  25.3 us
    unnamed x80, local copies, waits for them, and re-layouts  13.9 us
    pallas_call x1, Pallas kernels, attention_back(): pl.pallas_call(attend_back_kernel, grid=(n // GR,), in_specs=[s['wide'],...  10.7 us
    concatenate x1, other arithmetic, on_device(): jnp.concatenate([gate_up_grad.astype(bf16).reshape(NXZ, NT * ROWS, 2 * FT...  9.51 us
  transfers between devices with their start and end apart: 78, of which 32 were waited for; matrix products, arithmetic and copies ran while one was open for 37% of the time, Pallas kernels for 4%

profile of v3, /device:TPU:74, one launch (start us, length us, event | category | flops | bytes accessed | tf_op | source)
XLA Modules:
  0.0 464.7 jit_solution(6791237781388624637)
XLA Ops:
  13.1 4.9 %all-to-all-start = ((bf16[8,16,896]{2,1,0:T(8,128)(2,1)}), bf16[8,16,896]{2,1,0:T(8,128)(2,1)S(1)}, u32[]{:S(2)}, u32[]{:S(2)}) async-start(bf16[8,16,896]{2,1,0:T(8,128)(2,1)} %pad_maximum_fusion.4), calls=%async_computation | async-start | bytes 458752 | tf_op jit(solution)/shard_map/all_to_all | solution.py:323
  19.5 3.1 collective-permute-start.9
  22.6 4.5 collective-permute-done.9
  30.5 2.6 broadcast.180.clone
  33.9 8.0 %collective-permute-done.1 = bf16[128,2048]{1,0:T(8,128)(2,1)S(1)} collective-permute-done((bf16[128,2048]{1,0:T(8,128)(2,1)S(1)}, bf16[128,2048]{1,0:T(8,128)(2,1)S(1)}, u32[]{:S(2)}, u32[]{:S(2)}) %collective-permute-start.1) | collective-permute-done | bytes 524320 | tf_op jit(solution)/shard_map/ppermute | solution.py:60
  48.6 3.5 collective-permute-done.4
  58.9 3.7 collective-permute-start.30
  64.1 5.1 %all-to-all-start.1 = ((bf16[8,16,1536]{2,1,0:T(8,128)(2,1)}), bf16[8,16,1536]{2,1,0:T(8,128)(2,1)S(1)}, u32[]{:S(2)}, u32[]{:S(2)}) async-start(bf16[8,16,1536]{2,1,0:T(8,128)(2,1)} %pad_maximum_fusion.2), calls=%async_computation.1 | async-start | bytes 786432 | tf_op jit(solution)/shard_map/all_to_all | solution.py:352
  69.3 4.2 collective-permute-done.30
  83.7 3.8 fusion.9
  87.5 2.8 convert_reduce_fusion
  90.3 3.4 fusion.2
  104.9 6.8 %fusion.6.proj_ref = f32[1024,768]{1,0:T(8,128)S(1)} fusion(bf16[2048,896]{1,0:T(8,128)(2,1)} %bitcast.366, f32[2048]{0:T(1024)S(1)} %bitcast.445, f32[2048]{0:T(1024)S(1)} %bitcast.436, bf16[1024,2048]{1,0:T(8,128)(2,1)} %bitcast.14, f32[1024]{0:T(1024)S(1)} %add_rsqrt_fusion, f32[1024]{0:T(1024)S(1)} %broadcast_multiply_fusion), kind=kOutput, calls=%fused_computation.24 | convolution fusion | flops 3233808384 | bytes 10510336 | tf_op jit(solution)/shard_map/td,de->te/dot_general | solution.py:287
  117.5 2.8 collective-permute-start.13
  122.5 6.3 %attention.1 = (f32[1024,768]{1,0:T(8,128)S(1)}, f32[1024,256]{1,0:T(8,128)S(1)}) custom-call(f32[1024,768]{1,0:T(8,128)S(1)} %fusion.6.proj_ref, f32[1,768]{1,0:T(1,128)S(1)} %convert.47.bias_ref, f32[1024,256]{1,0:T(8,128)S(1)} %get-tuple-element.190.cos_ref, f32[1024,256]{1,0:T(8,128)S(1)} %get-tuple-element.189.sin_ref, f32[1024,2]{1,0:T(8,128)S(1)} %copy.186.colq_ref, ...), custom_call_target="tpu_custom_call" | custom-call | flops 1073741824 | bytes 7340032 | tf_op jit(solution)/shard_map/attention/pallas_call | solution.py:259
  135.0 3.1 collective-permute-start.20
  141.3 10.1 %collective-permute-done.20 = bf16[128,2048]{1,0:T(8,128)(2,1)S(1)} collective-permute-done((bf16[128,2048]{1,0:T(8,128)(2,1)S(1)}, bf16[128,2048]{1,0:T(8,128)(2,1)S(1)}, u32[]{:S(2)}, u32[]{:S(2)}) %collective-permute-start.20) | collective-permute-done | bytes 524320 | tf_op jit(solution)/shard_map/ppermute | solution.py:60
  151.4 10.5 %collective-permute-done.21 = bf16[128,2048]{1,0:T(8,128)(2,1)S(1)} collective-permute-done((bf16[128,2048]{1,0:T(8,128)(2,1)S(1)}, bf16[128,2048]{1,0:T(8,128)(2,1)S(1)}, u32[]{:S(2)}, u32[]{:S(2)}) %collective-permute-start.21) | collective-permute-done | bytes 524320 | tf_op jit(solution)/shard_map/ppermute | solution.py:60
  171.3 3.4 slice.225
  178.0 4.3 collective-permute-done.28
  189.0 5.5 %collective-permute-done.33 = bf16[64,2048]{1,0:T(8,128)(2,1)S(1)} collective-permute-done((bf16[64,2048]{1,0:T(8,128)(2,1)S(1)}, bf16[64,2048]{1,0:T(8,128)(2,1)S(1)}, u32[]{:S(2)}, u32[]{:S(2)}) %collective-permute-start.33) | collective-permute-done | bytes 262176 | tf_op jit(solution)/shard_map/ppermute | solution.py:60
  198.4 8.9 %fusion.62 = f32[1024,1536]{0,1:T(8,128)} fusion(bf16[1024,2048]{1,0:T(8,128)(2,1)S(1)} %bitcast.373, bf16[2048,1536]{1,0:T(8,128)(2,1)S(1)} %bitcast.361), kind=kOutput, calls=%fused_computation.214 | convolution fusion | flops 6442450944 | bytes 16777216 | tf_op jit(solution)/shard_map/td,de->te/dot_general | solution.py:287
  207.3 8.6 %multiply_convert_fusion.2 = (bf16[1024,768]{0,1:T(8,128)(2,1)S(1)}, bf16[1024,768]{0,1:T(8,128)(2,1)S(1)}, bf16[1024,768]{0,1:T(8,128)(2,1)}) fusion(f32[1024,1536]{0,1:T(8,128)} %fusion.62, bf16[1024,2048]{1,0:T(8,128)(2,1)S(1)} %bitcast.375, bf16[768,2048]{1,0:T(8,128)(2,1)} %bitcast.391), kind=kOutput, calls=%fused_computation.19 | convolution fusion | flops 3233021952 | bytes 18350080 | tf_op jit(solution)/shard_map/td,fd->tf/dot_general | solution.py:287
  215.9 8.3 %convolution_convert_fusion.1 = bf16[1024,2048]{1,0:T(8,128)(2,1)} fusion(bf16[2048,1536]{1,0:T(8,128)(2,1)S(1)} %bitcast.362, bf16[1024,768]{0,1:T(8,128)(2,1)S(1)} %get-tuple-element.139, bf16[1024,768]{0,1:T(8,128)(2,1)S(1)} %get-tuple-element.138), kind=kOutput, calls=%fused_computation.10 | convolution fusion | flops 6450839552 | bytes 13631488 | tf_op jit(solution)/shard_map/tf,df->td/dot_general | solution.py:287
  230.0 3.7 convolution_convert_fusion.5
  234.0 2.8 collective-permute-start.42
  238.8 7.5 %convolution_convert_fusion = bf16[2048,1536]{1,0:T(8,128)(2,1)S(1)} fusion(bf16[1024,2048]{1,0:T(8,128)(2,1)S(1)} %bitcast.374, bf16[1024,1536]{0,1:T(8,128)(2,1)S(1)} %pad_maximum_fusion.1), kind=kOutput, calls=%fused_computation.8 | convolution fusion | flops 6445596672 | bytes 13631488 | tf_op jit(solution)/shard_map/td,tf->df/dot_general | solution.py:287
  246.3 9.5 %maximum_maximum_fusion = bf16[16,192,1536]{2,1,0:T(8,128)(2,1)} fusion(bf16[16,16,512]{2,1,0:T(8,128)(2,1)S(1)} %get-tuple-element.175, bf16[16,16,512]{2,1,0:T(8,128)(2,1)S(1)} %get-tuple-element.176, bf16[16,16,512]{2,1,0:T(8,128)(2,1)S(1)} %get-tuple-element.174, bf16[16,48,1536]{2,1,0:T(8,128)(2,1)S(1)} %slice.232, bf16[16,128,1536]{2,1,0:T(8,128)(2,1)S(1)} %bitcast.363), kind=kLoop, calls=%fused_computation.4 | loop fusion | flops 47185920 | bytes 18874368 | tf_op jit(solution)/shard_map/concatenate | solution.py:411
  255.8 5.2 %collective-permute-done.43 = bf16[128,2048]{1,0:T(8,128)(2,1)S(1)} collective-permute-done((bf16[128,2048]{1,0:T(8,128)(2,1)S(1)}, bf16[128,2048]{1,0:T(8,128)(2,1)S(1)}, u32[]{:S(2)}, u32[]{:S(2)}) %collective-permute-start.43) | collective-permute-done | bytes 524320 | tf_op jit(solution)/shard_map/ppermute | solution.py:60
  272.4 10.4 %collective-permute-done.46 = bf16[128,2048]{1,0:T(8,128)(2,1)} collective-permute-done((bf16[128,2048]{1,0:T(8,128)(2,1)}, bf16[128,2048]{1,0:T(8,128)(2,1)}, u32[]{:S(2)}, u32[]{:S(2)}) %collective-permute-start.46) | collective-permute-done | bytes 524320 | tf_op jit(solution)/shard_map/ppermute | solution.py:60
  292.5 2.5 collective-permute-done.49
  303.5 3.9 fusion.63.grad_ref
  307.4 10.7 %attention_back.1 = (f32[1024,768]{1,0:T(8,128)S(1)}, f32[1,768]{1,0:T(1,128)S(1)}) custom-call(f32[1024,768]{1,0:T(8,128)S(1)} %copy-done.1, f32[1024,256]{1,0:T(8,128)S(1)} %fusion.63.grad_ref, f32[1024,256]{1,0:T(8,128)S(1)} %get-tuple-element.190.cos_ref, f32[1024,256]{1,0:T(8,128)S(1)} %get-tuple-element.189.sin_ref, f32[1024,2]{1,0:T(8,128)S(1)} %copy.186.colq_ref, ...), custom_call_target="tpu_custom_call" | custom-call | flops 2684354560 | bytes 6291456 | tf_op jit(solution)/shard_map/attention_back/pallas_call | solution.py:274
  320.3 8.7 %fusion.52 = (bf16[2048]{0:T(1024)(128)(2,1)S(1)}, bf16[2048]{0:T(1024)(128)(2,1)S(1)}, bf16[1024,2048]{1,0:T(8,128)(2,1)}, f32[1024,2048]{1,0:T(8,128)}) fusion(f32[1024]{0:T(1024)S(1)} %add_rsqrt_fusion, f32[1024]{0:T(1024)S(1)} %broadcast_multiply_fusion, bf16[1024,2048]{1,0:T(8,128)(2,1)} %bitcast.14, bf16[1024,768]{1,0:T(8,128)(2,1)S(1)} %convert_element_type.371, ...), kind=kOutput, calls=%fused_computation.206 | convolution fusion | flops 3235901440 | bytes 21512192 | tf_op jit(solution)/shard_map/te,de->td/dot_general | solution.py:287
  331.5 3.0 concatenate.77
  334.5 3.9 convolution_convert_fusion.6
  339.8 6.5 %convolution_convert_fusion.4 = bf16[2048,768]{1,0:T(8,128)(2,1)S(1)} fusion(bf16[1024,768]{1,0:T(8,128)(2,1)S(1)} %copy-done.28, f32[2048]{0:T(1024)S(1)} %bitcast.446, f32[2048]{0:T(1024)S(1)} %bitcast.437, bf16[1024,2048]{1,0:T(8,128)(2,1)} %bitcast.14, f32[1024]{0:T(1024)S(1)} %add_rsqrt_fusion, f32[1024]{0:T(1024)S(1)} %broadcast_multiply_fusion), kind=kOutput, calls=%fused_computation.13 | convolution fusion | flops 3235381248 | bytes 8937472 | tf_op jit(solution)/shard_map/td,te->de/dot_general | solution.py:287
  346.3 2.5 pad_maximum_fusion
  353.1 4.7 %collective-permute-start.69 = (bf16[44,2048]{1,0:T(8,128)(2,1)}, bf16[44,2048]{1,0:T(8,128)(2,1)}, u32[]{:S(2)}, u32[]{:S(2)}) collective-permute-start(bf16[44,2048]{1,0:T(8,128)(2,1)} %pad_maximum_fusion.5), channel_id=1, source_target_pairs={{0,0},{1,16},{2,1},{3,17},{4,2},{5,18},{6,3},{7,19},{8,4},{9,20},{... | collective-permute-start | bytes 540680 | tf_op jit(solution)/shard_map/ppermute | solution.py:458
  357.8 2.9 dynamic-slice_bitcast_fusion.3
  361.9 4.9 %all-to-all-start.3 = ((bf16[8,16,1536]{2,1,0:T(8,128)(2,1)}), bf16[8,16,1536]{2,1,0:T(8,128)(2,1)S(1)}, u32[]{:S(2)}, u32[]{:S(2)}) async-start(bf16[8,16,1536]{2,1,0:T(8,128)(2,1)} %bitcast.408), calls=%async_computation.5 | async-start | bytes 786432 | tf_op jit(solution)/shard_map/all_to_all | solution.py:460
  366.8 5.1 %convolution_convert_fusion.3 = bf16[1024,2048]{1,0:T(8,128)(2,1)S(1)} fusion(bf16[1024,768]{0,1:T(8,128)(2,1)} %get-tuple-element.106, bf16[768,2048]{1,0:T(8,128)(2,1)S(1)} %bitcast.392), kind=kOutput, calls=%fused_computation.12 | convolution fusion | flops 3223322624 | bytes 8912896 | tf_op jit(solution)/shard_map/tf,fd->td/dot_general | solution.py:287
  389.9 9.0 %collective-permute-done.65 = bf16[128,2048]{1,0:T(8,128)(2,1)S(1)} collective-permute-done((bf16[128,2048]{1,0:T(8,128)(2,1)S(1)}, bf16[128,2048]{1,0:T(8,128)(2,1)S(1)}, u32[]{:S(2)}, u32[]{:S(2)}) %collective-permute-start.65) | collective-permute-done | bytes 524320 | tf_op jit(solution)/shard_map/ppermute | solution.py:60
  400.4 9.8 %collective-permute-done.66 = bf16[128,2048]{1,0:T(8,128)(2,1)S(1)} collective-permute-done((bf16[128,2048]{1,0:T(8,128)(2,1)S(1)}, bf16[128,2048]{1,0:T(8,128)(2,1)S(1)}, u32[]{:S(2)}, u32[]{:S(2)}) %collective-permute-start.66) | collective-permute-done | bytes 524320 | tf_op jit(solution)/shard_map/ppermute | solution.py:60
  412.6 8.9 %collective-permute-done.58 = bf16[128,2048]{1,0:T(8,128)(2,1)S(1)} collective-permute-done((bf16[128,2048]{1,0:T(8,128)(2,1)S(1)}, bf16[128,2048]{1,0:T(8,128)(2,1)S(1)}, u32[]{:S(2)}, u32[]{:S(2)}) %collective-permute-start.58) | collective-permute-done | bytes 524320 | tf_op jit(solution)/shard_map/ppermute | solution.py:60
  421.4 10.6 %collective-permute-done.59 = bf16[128,2048]{1,0:T(8,128)(2,1)S(1)} collective-permute-done((bf16[128,2048]{1,0:T(8,128)(2,1)S(1)}, bf16[128,2048]{1,0:T(8,128)(2,1)S(1)}, u32[]{:S(2)}, u32[]{:S(2)}) %collective-permute-start.59) | collective-permute-done | bytes 524320 | tf_op jit(solution)/shard_map/ppermute | solution.py:60
  439.2 4.4 all-to-all-start.2
  443.7 5.2 %collective-permute-start.68 = (bf16[16,2048]{1,0:T(8,128)(2,1)S(1)}, bf16[16,2048]{1,0:T(8,128)(2,1)S(1)}, u32[]{:S(2)}, u32[]{:S(2)}) collective-permute-start(bf16[16,2048]{1,0:T(8,128)(2,1)S(1)} %bitcast.434), channel_id=1, source_target_pairs={{0,0},{1,16},{2,1},{3,17},{4,2},{5,18},{6,3},{7,19},{8,4},{9,20},{... | collective-permute-start | bytes 196616 | tf_op jit(solution)/shard_map/ppermute | solution.py:470
  (398 shorter events, 174.5 us)
Async XLA Ops:
  13.1 14.0 %all-to-all-start = ((bf16[8,16,896]{2,1,0:T(8,128)(2,1)}), bf16[8,16,896]{2,1,0:T(8,128)(2,1)S(1)}, u32[]{:S(2)}, u32[]{:S(2)}) async-start(bf16[8,16,896]{2,1,0:T(8,128)(2,1)} %pad_maximum_fusion.4), calls=%async_computation | async-start | bytes 458752 | tf_op jit(solution)/shard_map/all_to_all | solution.py:323
  18.0 75.7 %all-gather.5.cloned.1.call-start = ((), (), s32[]{:S(2)}) async-start(), calls=%async_computation.8 | async-start | bytes 5013504 | tf_op jit(solution)/shard_map/all_gather | solution.py:338
  28.4 13.5 %collective-permute-start.1 = (bf16[128,2048]{1,0:T(8,128)(2,1)S(1)}, bf16[128,2048]{1,0:T(8,128)(2,1)S(1)}, u32[]{:S(2)}, u32[]{:S(2)}) collective-permute-start(bf16[128,2048]{1,0:T(8,128)(2,1)S(1)} %copy.172), channel_id=1, source_target_pairs={{0,32},{32,64},{64,96},{96,0},{1,33},{33,65},{65,97},{97,1},{2,34}... | collective-permute-start | bytes 1572872 | tf_op jit(solution)/shard_map/ppermute | solution.py:60
  30.0 13.2 %collective-permute-start.2 = (bf16[128,2048]{1,0:T(8,128)(2,1)S(1)}, bf16[128,2048]{1,0:T(8,128)(2,1)S(1)}, u32[]{:S(2)}, u32[]{:S(2)}) collective-permute-start(bf16[128,2048]{1,0:T(8,128)(2,1)S(1)} %copy.172), channel_id=1, source_target_pairs={{0,96},{32,0},{64,32},{96,64},{1,97},{33,1},{65,33},{97,65},{2,98}... | collective-permute-start | bytes 1572872 | tf_op jit(solution)/shard_map/ppermute | solution.py:60
  30.5 15.3 %collective-permute-start = (bf16[128,2048]{1,0:T(8,128)(2,1)S(1)}, bf16[128,2048]{1,0:T(8,128)(2,1)}, u32[]{:S(2)}, u32[]{:S(2)}) collective-permute-start(bf16[128,2048]{1,0:T(8,128)(2,1)S(1)} %copy.172), channel_id=1, source_target_pairs={{0,1},{1,0},{2,3},{3,2},{4,5},{5,4},{6,7},{7,6},{8,9},{9,8},{10,11... | collective-permute-start | bytes 1572872 | tf_op jit(solution)/shard_map/ppermute | solution.py:60
  43.2 14.4 %collective-permute-start.8 = (bf16[128,2048]{1,0:T(8,128)(2,1)S(1)}, bf16[128,2048]{1,0:T(8,128)(2,1)S(1)}, u32[]{:S(2)}, u32[]{:S(2)}) collective-permute-start(bf16[128,2048]{1,0:T(8,128)(2,1)S(1)} %collective-permute-done.1), channel_id=1, source_target_pairs={{0,1},{1,0},{2,3},{3,2},{4,5},{5,4},{6,7},{7,6},{8,9},{9,8},{10,11... | collective-permute-start | bytes 1572872 | tf_op jit(solution)/shard_map/ppermute | solution.py:60
  58.9 14.6 %collective-permute-start.30 = (bf16[44,2048]{1,0:T(8,128)(2,1)S(1)}, bf16[44,2048]{1,0:T(8,128)(2,1)S(1)}, u32[]{:S(2)}, u32[]{:S(2)}) collective-permute-start(bf16[44,2048]{1,0:T(8,128)(2,1)S(1)} %copy-done.35), channel_id=1, source_target_pairs={{0,0},{16,1},{1,2},{17,3},{2,4},{18,5},{3,6},{19,7},{4,8},{20,9},{... | collective-permute-start | bytes 540680 | tf_op jit(solution)/shard_map/ppermute | solution.py:353
  64.1 12.6 %all-to-all-start.1 = ((bf16[8,16,1536]{2,1,0:T(8,128)(2,1)}), bf16[8,16,1536]{2,1,0:T(8,128)(2,1)S(1)}, u32[]{:S(2)}, u32[]{:S(2)}) async-start(bf16[8,16,1536]{2,1,0:T(8,128)(2,1)} %pad_maximum_fusion.2), calls=%async_computation.1 | async-start | bytes 786432 | tf_op jit(solution)/shard_map/all_to_all | solution.py:352
  69.3 100.3 %all-gather.7.cloned.1.call-start = ((), (), s32[]{:S(2)}) async-start(), calls=%async_computation.9 | async-start | bytes 10027008 | tf_op jit(solution)/shard_map/all_gather | solution.py:366
  77.6 272.1 %reduce-scatter.3.cloned.1.call-start = ((), (), s32[]{:S(2)}) async-start(), calls=%async_computation.6 | async-start | bytes 10027008 | tf_op jit(solution)/shard_map/reduce_scatter | solution.py:419
  93.7 20.6 %collective-permute-start.10 = (bf16[128,2048]{1,0:T(8,128)(2,1)}, bf16[128,2048]{1,0:T(8,128)(2,1)}, u32[]{:S(2)}, u32[]{:S(2)}) collective-permute-start(bf16[128,2048]{1,0:T(8,128)(2,1)} %copy.175), channel_id=1, source_target_pairs={{0,32},{32,64},{64,96},{96,0},{1,33},{33,65},{65,97},{97,1},{2,34}... | collective-permute-start | bytes 1572872 | tf_op jit(solution)/shard_map/ppermute | solution.py:60
  93.8 20.5 %collective-permute-start.11 = (bf16[128,2048]{1,0:T(8,128)(2,1)}, bf16[128,2048]{1,0:T(8,128)(2,1)}, u32[]{:S(2)}, u32[]{:S(2)}) collective-permute-start(bf16[128,2048]{1,0:T(8,128)(2,1)} %copy.175), channel_id=1, source_target_pairs={{0,96},{32,0},{64,32},{96,64},{1,97},{33,1},{65,33},{97,65},{2,98}... | collective-permute-start | bytes 1572872 | tf_op jit(solution)/shard_map/ppermute | solution.py:60
  95.8 24.5 %collective-permute-start.23 = (bf16[128,2048]{1,0:T(8,128)(2,1)}, bf16[128,2048]{1,0:T(8,128)(2,1)}, u32[]{:S(2)}, u32[]{:S(2)}) collective-permute-start(bf16[128,2048]{1,0:T(8,128)(2,1)} %copy.175), channel_id=1, source_target_pairs={{0,1},{1,0},{2,3},{3,2},{4,5},{5,4},{6,7},{7,6},{8,9},{9,8},{10,11... | collective-permute-start | bytes 1572872 | tf_op jit(solution)/shard_map/ppermute | solution.py:60
  114.4 16.7 %collective-permute-start.24 = (bf16[128,2048]{1,0:T(8,128)(2,1)}, bf16[128,2048]{1,0:T(8,128)(2,1)S(1)}, u32[]{:S(2)}, u32[]{:S(2)}) collective-permute-start(bf16[128,2048]{1,0:T(8,128)(2,1)} %collective-permute-done.11), channel_id=1, source_target_pairs={{0,1},{1,0},{2,3},{3,2},{4,5},{5,4},{6,7},{7,6},{8,9},{9,8},{10,11... | collective-permute-start | bytes 1572872 | tf_op jit(solution)/shard_map/ppermute | solution.py:60
  117.1 24.1 %collective-permute-start.27 = (bf16[128,2048]{1,0:T(8,128)(2,1)}, bf16[128,2048]{1,0:T(8,128)(2,1)S(1)}, u32[]{:S(2)}, u32[]{:S(2)}) collective-permute-start(bf16[128,2048]{1,0:T(8,128)(2,1)} %collective-permute-done.10), channel_id=1, source_target_pairs={{0,1},{1,0},{2,3},{3,2},{4,5},{5,4},{6,7},{7,6},{8,9},{9,8},{10,11... | collective-permute-start | bytes 1572872 | tf_op jit(solution)/shard_map/ppermute | solution.py:60
  117.2 11.6 %collective-permute-start.12 = (bf16[64,2048]{1,0:T(8,128)(2,1)S(1)}, bf16[64,2048]{1,0:T(8,128)(2,1)S(1)}, u32[]{:S(2)}, u32[]{:S(2)}) collective-permute-start(bf16[64,2048]{1,0:T(8,128)(2,1)S(1)} %slice.172), channel_id=1, source_target_pairs={{0,32},{32,64},{64,96},{96,0},{1,33},{33,65},{65,97},{97,1},{2,34}... | collective-permute-start | bytes 786440 | tf_op jit(solution)/shard_map/ppermute | solution.py:60
  135.0 16.4 %collective-permute-start.20 = (bf16[128,2048]{1,0:T(8,128)(2,1)S(1)}, bf16[128,2048]{1,0:T(8,128)(2,1)S(1)}, u32[]{:S(2)}, u32[]{:S(2)}) collective-permute-start(bf16[128,2048]{1,0:T(8,128)(2,1)S(1)} %get-tuple-element.77), channel_id=1, source_target_pairs={{0,64},{32,96},{64,0},{96,32},{1,65},{33,97},{65,1},{97,33},{2,66}... | collective-permute-start | bytes 1572872 | tf_op jit(solution)/shard_map/ppermute | solution.py:60
  138.1 23.8 %collective-permute-start.21 = (bf16[128,2048]{1,0:T(8,128)(2,1)S(1)}, bf16[128,2048]{1,0:T(8,128)(2,1)S(1)}, u32[]{:S(2)}, u32[]{:S(2)}) collective-permute-start(bf16[128,2048]{1,0:T(8,128)(2,1)S(1)} %get-tuple-element.78), channel_id=1, source_target_pairs={{0,32},{32,64},{64,96},{96,0},{1,33},{33,65},{65,97},{97,1},{2,34}... | collective-permute-start | bytes 1572872 | tf_op jit(solution)/shard_map/ppermute | solution.py:60
  139.9 22.0 %collective-permute-start.22 = (bf16[128,2048]{1,0:T(8,128)(2,1)S(1)}, bf16[128,2048]{1,0:T(8,128)(2,1)S(1)}, u32[]{:S(2)}, u32[]{:S(2)}) collective-permute-start(bf16[128,2048]{1,0:T(8,128)(2,1)S(1)} %get-tuple-element.79), channel_id=1, source_target_pairs={{0,96},{32,0},{64,32},{96,64},{1,97},{33,1},{65,33},{97,65},{2,98}... | collective-permute-start | bytes 1572872 | tf_op jit(solution)/shard_map/ppermute | solution.py:60
  166.5 16.1 %collective-permute-start.31 = (bf16[128,2048]{1,0:T(8,128)(2,1)}, bf16[128,2048]{1,0:T(8,128)(2,1)}, u32[]{:S(2)}, u32[]{:S(2)}) collective-permute-start(bf16[128,2048]{1,0:T(8,128)(2,1)} %get-tuple-element.135), channel_id=1, source_target_pairs={{0,1},{1,0},{2,3},{3,2},{4,5},{5,4},{6,7},{7,6},{8,9},{9,8},{10,11... | collective-permute-start | bytes 1572872 | tf_op jit(solution)/shard_map/ppermute | solution.py:60
  166.5 15.8 %collective-permute-start.28 = (bf16[128,2048]{1,0:T(8,128)(2,1)}, bf16[128,2048]{1,0:T(8,128)(2,1)S(1)}, u32[]{:S(2)}, u32[]{:S(2)}) collective-permute-start(bf16[128,2048]{1,0:T(8,128)(2,1)} %get-tuple-element.135), channel_id=1, source_target_pairs={{0,32},{32,64},{64,96},{96,0},{1,33},{33,65},{65,97},{97,1},{2,34}... | collective-permute-start | bytes 1572872 | tf_op jit(solution)/shard_map/ppermute | solution.py:60
  168.1 14.5 %collective-permute-start.29 = (bf16[128,2048]{1,0:T(8,128)(2,1)}, bf16[128,2048]{1,0:T(8,128)(2,1)}, u32[]{:S(2)}, u32[]{:S(2)}) collective-permute-start(bf16[128,2048]{1,0:T(8,128)(2,1)} %get-tuple-element.135), channel_id=1, source_target_pairs={{0,96},{32,0},{64,32},{96,64},{1,97},{33,1},{65,33},{97,65},{2,98}... | collective-permute-start | bytes 1572872 | tf_op jit(solution)/shard_map/ppermute | solution.py:60
  182.6 14.1 %collective-permute-start.32 = (bf16[128,2048]{1,0:T(8,128)(2,1)}, bf16[128,2048]{1,0:T(8,128)(2,1)S(1)}, u32[]{:S(2)}, u32[]{:S(2)}) collective-permute-start(bf16[128,2048]{1,0:T(8,128)(2,1)} %collective-permute-done.29), channel_id=1, source_target_pairs={{0,1},{1,0},{2,3},{3,2},{4,5},{5,4},{6,7},{7,6},{8,9},{9,8},{10,11... | collective-permute-start | bytes 1572872 | tf_op jit(solution)/shard_map/ppermute | solution.py:60
  184.7 13.6 %collective-permute-start.37 = (bf16[128,2048]{1,0:T(8,128)(2,1)S(1)}, bf16[128,2048]{1,0:T(8,128)(2,1)S(1)}, u32[]{:S(2)}, u32[]{:S(2)}) collective-permute-start(bf16[128,2048]{1,0:T(8,128)(2,1)S(1)} %collective-permute-done.28), channel_id=1, source_target_pairs={{0,1},{1,0},{2,3},{3,2},{4,5},{5,4},{6,7},{7,6},{8,9},{9,8},{10,11... | collective-permute-start | bytes 1572872 | tf_op jit(solution)/shard_map/ppermute | solution.py:60
  226.6 29.2 %collective-permute-start.38 = (bf16[128,2048]{1,0:T(8,128)(2,1)S(1)}, bf16[128,2048]{1,0:T(8,128)(2,1)S(1)}, u32[]{:S(2)}, u32[]{:S(2)}) collective-permute-start(bf16[128,2048]{1,0:T(8,128)(2,1)S(1)} %get-tuple-element.160), channel_id=1, source_target_pairs={{0,1},{1,0},{2,3},{3,2},{4,5},{5,4},{6,7},{7,6},{8,9},{9,8},{10,11... | collective-permute-start | bytes 1572872 | tf_op jit(solution)/shard_map/ppermute | solution.py:60
  234.0 21.9 %collective-permute-start.42 = (bf16[128,2048]{1,0:T(8,128)(2,1)S(1)}, bf16[128,2048]{1,0:T(8,128)(2,1)S(1)}, u32[]{:S(2)}, u32[]{:S(2)}) collective-permute-start(bf16[128,2048]{1,0:T(8,128)(2,1)S(1)} %get-tuple-element.89), channel_id=1, source_target_pairs={{0,64},{32,96},{64,0},{96,32},{1,65},{33,97},{65,1},{97,33},{2,66}... | collective-permute-start | bytes 1572872 | tf_op jit(solution)/shard_map/ppermute | solution.py:60
  236.8 24.3 %collective-permute-start.43 = (bf16[128,2048]{1,0:T(8,128)(2,1)S(1)}, bf16[128,2048]{1,0:T(8,128)(2,1)S(1)}, u32[]{:S(2)}, u32[]{:S(2)}) collective-permute-start(bf16[128,2048]{1,0:T(8,128)(2,1)S(1)} %get-tuple-element.90), channel_id=1, source_target_pairs={{0,32},{32,64},{64,96},{96,0},{1,33},{33,65},{65,97},{97,1},{2,34}... | collective-permute-start | bytes 1572872 | tf_op jit(solution)/shard_map/ppermute | solution.py:60
  237.2 23.9 %collective-permute-start.44 = (bf16[128,2048]{1,0:T(8,128)(2,1)S(1)}, bf16[128,2048]{1,0:T(8,128)(2,1)S(1)}, u32[]{:S(2)}, u32[]{:S(2)}) collective-permute-start(bf16[128,2048]{1,0:T(8,128)(2,1)S(1)} %get-tuple-element.91), channel_id=1, source_target_pairs={{0,96},{32,0},{64,32},{96,64},{1,97},{33,1},{65,33},{97,65},{2,98}... | collective-permute-start | bytes 1572872 | tf_op jit(solution)/shard_map/ppermute | solution.py:60
  262.5 174.2 %reduce-scatter.5.cloned.1.call-start = ((), (), s32[]{:S(2)}) async-start(), calls=%async_computation.7 | async-start | bytes 5013504 | tf_op jit(solution)/shard_map/reduce_scatter | solution.py:449
  269.0 13.8 %collective-permute-start.46 = (bf16[128,2048]{1,0:T(8,128)(2,1)}, bf16[128,2048]{1,0:T(8,128)(2,1)}, u32[]{:S(2)}, u32[]{:S(2)}) collective-permute-start(bf16[128,2048]{1,0:T(8,128)(2,1)} %get-tuple-element.132), channel_id=1, source_target_pairs={{0,32},{32,64},{64,96},{96,0},{1,33},{33,65},{65,97},{97,1},{2,34}... | collective-permute-start | bytes 1572872 | tf_op jit(solution)/shard_map/ppermute | solution.py:60
  270.1 14.1 %collective-permute-start.47 = (bf16[128,2048]{1,0:T(8,128)(2,1)}, bf16[128,2048]{1,0:T(8,128)(2,1)}, u32[]{:S(2)}, u32[]{:S(2)}) collective-permute-start(bf16[128,2048]{1,0:T(8,128)(2,1)} %get-tuple-element.132), channel_id=1, source_target_pairs={{0,96},{32,0},{64,32},{96,64},{1,97},{33,1},{65,33},{97,65},{2,98}... | collective-permute-start | bytes 1572872 | tf_op jit(solution)/shard_map/ppermute | solution.py:60
  271.0 17.7 %collective-permute-start.45 = (bf16[128,2048]{1,0:T(8,128)(2,1)}, bf16[128,2048]{1,0:T(8,128)(2,1)}, u32[]{:S(2)}, u32[]{:S(2)}) collective-permute-start(bf16[128,2048]{1,0:T(8,128)(2,1)} %get-tuple-element.132), channel_id=1, source_target_pairs={{0,1},{1,0},{2,3},{3,2},{4,5},{5,4},{6,7},{7,6},{8,9},{9,8},{10,11... | collective-permute-start | bytes 1572872 | tf_op jit(solution)/shard_map/ppermute | solution.py:60
  284.2 12.8 %collective-permute-start.48 = (bf16[128,2048]{1,0:T(8,128)(2,1)}, bf16[128,2048]{1,0:T(8,128)(2,1)S(1)}, u32[]{:S(2)}, u32[]{:S(2)}) collective-permute-start(bf16[128,2048]{1,0:T(8,128)(2,1)} %collective-permute-done.47), channel_id=1, source_target_pairs={{0,1},{1,0},{2,3},{3,2},{4,5},{5,4},{6,7},{7,6},{8,9},{9,8},{10,11... | collective-permute-start | bytes 1572872 | tf_op jit(solution)/shard_map/ppermute | solution.py:60
  286.1 16.5 %collective-permute-start.53 = (bf16[128,2048]{1,0:T(8,128)(2,1)}, bf16[128,2048]{1,0:T(8,128)(2,1)S(1)}, u32[]{:S(2)}, u32[]{:S(2)}) collective-permute-start(bf16[128,2048]{1,0:T(8,128)(2,1)} %collective-permute-done.46), channel_id=1, source_target_pairs={{0,1},{1,0},{2,3},{3,2},{4,5},{5,4},{6,7},{7,6},{8,9},{9,8},{10,11... | collective-permute-start | bytes 1572872 | tf_op jit(solution)/shard_map/ppermute | solution.py:60
  353.1 22.2 %collective-permute-start.69 = (bf16[44,2048]{1,0:T(8,128)(2,1)}, bf16[44,2048]{1,0:T(8,128)(2,1)}, u32[]{:S(2)}, u32[]{:S(2)}) collective-permute-start(bf16[44,2048]{1,0:T(8,128)(2,1)} %pad_maximum_fusion.5), channel_id=1, source_target_pairs={{0,0},{1,16},{2,1},{3,17},{4,2},{5,18},{6,3},{7,19},{8,4},{9,20},{... | collective-permute-start | bytes 540680 | tf_op jit(solution)/shard_map/ppermute | solution.py:458
  360.7 18.5 %collective-permute-start.62 = (bf16[128,2048]{1,0:T(8,128)(2,1)}, bf16[128,2048]{1,0:T(8,128)(2,1)}, u32[]{:S(2)}, u32[]{:S(2)}) collective-permute-start(bf16[128,2048]{1,0:T(8,128)(2,1)} %get-tuple-element.149), channel_id=1, source_target_pairs={{0,1},{1,0},{2,3},{3,2},{4,5},{5,4},{6,7},{7,6},{8,9},{9,8},{10,11... | collective-permute-start | bytes 1572872 | tf_op jit(solution)/shard_map/ppermute | solution.py:60
  360.7 18.9 %collective-permute-start.63 = (bf16[128,2048]{1,0:T(8,128)(2,1)}, bf16[128,2048]{1,0:T(8,128)(2,1)}, u32[]{:S(2)}, u32[]{:S(2)}) collective-permute-start(bf16[128,2048]{1,0:T(8,128)(2,1)} %get-tuple-element.148), channel_id=1, source_target_pairs={{0,1},{1,0},{2,3},{3,2},{4,5},{5,4},{6,7},{7,6},{8,9},{9,8},{10,11... | collective-permute-start | bytes 1572872 | tf_op jit(solution)/shard_map/ppermute | solution.py:60
  361.2 18.6 %collective-permute-start.64 = (bf16[128,2048]{1,0:T(8,128)(2,1)}, bf16[128,2048]{1,0:T(8,128)(2,1)}, u32[]{:S(2)}, u32[]{:S(2)}) collective-permute-start(bf16[128,2048]{1,0:T(8,128)(2,1)} %get-tuple-element.147), channel_id=1, source_target_pairs={{0,1},{1,0},{2,3},{3,2},{4,5},{5,4},{6,7},{7,6},{8,9},{9,8},{10,11... | collective-permute-start | bytes 1572872 | tf_op jit(solution)/shard_map/ppermute | solution.py:60
  361.4 26.9 %collective-permute-start.61 = (bf16[128,2048]{1,0:T(8,128)(2,1)}, bf16[128,2048]{1,0:T(8,128)(2,1)}, u32[]{:S(2)}, u32[]{:S(2)}) collective-permute-start(bf16[128,2048]{1,0:T(8,128)(2,1)} %get-tuple-element.146), channel_id=1, source_target_pairs={{0,1},{1,0},{2,3},{3,2},{4,5},{5,4},{6,7},{7,6},{8,9},{9,8},{10,11... | collective-permute-start | bytes 1572872 | tf_op jit(solution)/shard_map/ppermute | solution.py:60
  361.9 16.8 %all-to-all-start.3 = ((bf16[8,16,1536]{2,1,0:T(8,128)(2,1)}), bf16[8,16,1536]{2,1,0:T(8,128)(2,1)S(1)}, u32[]{:S(2)}, u32[]{:S(2)}) async-start(bf16[8,16,1536]{2,1,0:T(8,128)(2,1)} %bitcast.408), calls=%async_computation.5 | async-start | bytes 786432 | tf_op jit(solution)/shard_map/all_to_all | solution.py:460
  379.8 32.8 %collective-permute-start.54 = (bf16[128,2048]{1,0:T(8,128)(2,1)}, bf16[128,2048]{1,0:T(8,128)(2,1)S(1)}, u32[]{:S(2)}, u32[]{:S(2)}) collective-permute-start(bf16[128,2048]{1,0:T(8,128)(2,1)} %get-tuple-element.153), channel_id=1, source_target_pairs={{0,1},{1,0},{2,3},{3,2},{4,5},{5,4},{6,7},{7,6},{8,9},{9,8},{10,11... | collective-permute-start | bytes 1572872 | tf_op jit(solution)/shard_map/ppermute | solution.py:60
  382.5 16.4 %collective-permute-start.65 = (bf16[128,2048]{1,0:T(8,128)(2,1)S(1)}, bf16[128,2048]{1,0:T(8,128)(2,1)S(1)}, u32[]{:S(2)}, u32[]{:S(2)}) collective-permute-start(bf16[128,2048]{1,0:T(8,128)(2,1)S(1)} %get-tuple-element.111), channel_id=1, source_target_pairs={{0,64},{32,96},{64,0},{96,32},{1,65},{33,97},{65,1},{97,33},{2,66}... | collective-permute-start | bytes 1572872 | tf_op jit(solution)/shard_map/ppermute | solution.py:60
  384.7 25.5 %collective-permute-start.66 = (bf16[128,2048]{1,0:T(8,128)(2,1)S(1)}, bf16[128,2048]{1,0:T(8,128)(2,1)S(1)}, u32[]{:S(2)}, u32[]{:S(2)}) collective-permute-start(bf16[128,2048]{1,0:T(8,128)(2,1)S(1)} %get-tuple-element.112), channel_id=1, source_target_pairs={{0,32},{32,64},{64,96},{96,0},{1,33},{33,65},{65,97},{97,1},{2,34}... | collective-permute-start | bytes 1572872 | tf_op jit(solution)/shard_map/ppermute | solution.py:60
  384.7 25.8 %collective-permute-start.67 = (bf16[128,2048]{1,0:T(8,128)(2,1)S(1)}, bf16[128,2048]{1,0:T(8,128)(2,1)S(1)}, u32[]{:S(2)}, u32[]{:S(2)}) collective-permute-start(bf16[128,2048]{1,0:T(8,128)(2,1)S(1)} %get-tuple-element.113), channel_id=1, source_target_pairs={{0,96},{32,0},{64,32},{96,64},{1,97},{33,1},{65,33},{97,65},{2,98}... | collective-permute-start | bytes 1572872 | tf_op jit(solution)/shard_map/ppermute | solution.py:60
  388.3 33.1 %collective-permute-start.58 = (bf16[128,2048]{1,0:T(8,128)(2,1)S(1)}, bf16[128,2048]{1,0:T(8,128)(2,1)S(1)}, u32[]{:S(2)}, u32[]{:S(2)}) collective-permute-start(bf16[128,2048]{1,0:T(8,128)(2,1)S(1)} %get-tuple-element.107), channel_id=1, source_target_pairs={{0,64},{32,96},{64,0},{96,32},{1,65},{33,97},{65,1},{97,33},{2,66}... | collective-permute-start | bytes 1572872 | tf_op jit(solution)/shard_map/ppermute | solution.py:60
  398.9 33.1 %collective-permute-start.59 = (bf16[128,2048]{1,0:T(8,128)(2,1)S(1)}, bf16[128,2048]{1,0:T(8,128)(2,1)S(1)}, u32[]{:S(2)}, u32[]{:S(2)}) collective-permute-start(bf16[128,2048]{1,0:T(8,128)(2,1)S(1)} %get-tuple-element.108), channel_id=1, source_target_pairs={{0,32},{32,64},{64,96},{96,0},{1,33},{33,65},{65,97},{97,1},{2,34}... | collective-permute-start | bytes 1572872 | tf_op jit(solution)/shard_map/ppermute | solution.py:60
  410.1 21.9 %collective-permute-start.60 = (bf16[128,2048]{1,0:T(8,128)(2,1)S(1)}, bf16[128,2048]{1,0:T(8,128)(2,1)S(1)}, u32[]{:S(2)}, u32[]{:S(2)}) collective-permute-start(bf16[128,2048]{1,0:T(8,128)(2,1)S(1)} %get-tuple-element.109), channel_id=1, source_target_pairs={{0,96},{32,0},{64,32},{96,64},{1,97},{33,1},{65,33},{97,65},{2,98}... | collective-permute-start | bytes 1572872 | tf_op jit(solution)/shard_map/ppermute | solution.py:60
  439.2 15.7 %all-to-all-start.2 = ((bf16[8,16,896]{2,1,0:T(8,128)(2,1)}), bf16[8,16,896]{2,1,0:T(8,128)(2,1)S(1)}, u32[]{:S(2)}, u32[]{:S(2)}) async-start(bf16[8,16,896]{2,1,0:T(8,128)(2,1)} %bitcast.151), calls=%async_computation.4 | async-start | bytes 458752 | tf_op jit(solution)/shard_map/all_to_all | solution.py:472
  (68 other events, 587.3 us)
Sparse Core Ops, SparseCore 0:
  28.0 59.1 all-gather.4
  89.4 74.8 all-gather.6
  262.6 87.0 reduce-scatter.2
  353.3 77.8 reduce-scatter.4

commit v4 on v3

--- a/solution.py
+++ b/solution.py
@@ -114,6 +114,25 @@
     out = sums[0]
     for r in (2, 1, 3):
         out = out + send(away[r], y=r).astype(f32)
+    return (out, hold) if hold else out
+
+
+def reduce_y_steps(total, place, hold=()):
+    total = total.reshape(NT, TOK, D)
+    part = lambda r, k: lax.dynamic_index_in_dim(total, place.block(r, k), keepdims=False)
+    sums = {}
+    half = TOK // 2
+    for r in (2, 1, 3, 0):
+        other = send(part(r, 1), c=1)
+        sums[r] = part(r, 0).astype(f32) + other.astype(f32)
+    far, hold = lax.optimization_barrier((sums[2].astype(bf16), hold))
+    top = send(far[:half], y=1)
+    bottom = send(far[half:], y=-1)
+    one = jnp.concatenate([sums[1][:half] + top.astype(f32), sums[1][half:]], axis=0).astype(bf16)
+    three = jnp.concatenate([sums[3][:half], sums[3][half:] + bottom.astype(f32)], axis=0).astype(bf16)
+    from_prev = send(one, y=1)
+    from_next = send(three, y=-1)
+    out = sums[0] + from_prev.astype(f32) + from_next.astype(f32)
     return (out, hold) if hold else out
 
 
@@ -447,9 +466,9 @@
     hold = (first_chunks, second_sum, h1_part.astype(bf16), product)
     first_chunks, second_sum, h1_part, product = lax.optimization_barrier(hold)
     first_sum = lax.psum_scatter(first_chunks.reshape(D, -1), XZ, scatter_dimension=0, tiled=True)
-    grad_h1 = reduce_y(h1_part, place)
+    grad_h1 = reduce_y_steps(h1_part, place)
     out_part = mm("tf,fd->td", product, down_w).astype(bf16)
-    layer_out = from_pi((resid + reduce_y(out_part, place)).astype(bf16))[None]
+    layer_out = from_pi((resid + reduce_y_steps(out_part, place)).astype(bf16))[None]
     input_grad = grad_resid + norm_back(grad_h1, own_rows(normed1), own_rows(inv_one), gain_one)
     input_grad = from_pi(input_grad.astype(bf16))[None]
 

time: 473 us -> 469 us (level)
  the two profiles are of different devices: /device:TPU:74 before, /device:TPU:1 now
where the time goes in v4:
time: 469 us; the launch traced here: 460 us
  waiting for transfers between devices  110 us (23%)
  local copies, waits for them, and re-layouts  100 us (21%)
  starting transfers between devices  95.1 us (20%)
  matrix products  74.2 us (16%)
  other arithmetic  47.6 us (10%)
  Pallas kernels  16.8 us (4%)
  between operations  15.8 us (3%)
    ppermute x68, waiting for transfers between devices, send(): return plain(lax.ppermute(plain(value), axes, shift_perm(axes, deltas)))  91.9 us
    dot_general x16, matrix products, mm(): return jnp.einsum(spec, a, b, preferred_element_type=f32)  74.2 us
    ppermute x68, starting transfers between devices, send(): return plain(lax.ppermute(plain(value), axes, shift_perm(axes, deltas)))  56.5 us
    dynamic_update_slice x38, local copies, waits for them, and re-layouts, gather_rows(): whole = lax.dynamic_update_slice(whole, b[None], (place.block(*s), at, 0))  25.2 us
    unnamed x80, local copies, waits for them, and re-layouts  13.8 us
    pallas_call x1, Pallas kernels, attention_back(): pl.pallas_call(attend_back_kernel, grid=(n // GR,), in_specs=[s['wide'],...  10.5 us
    concatenate x1, other arithmetic, on_device(): jnp.concatenate([gate_up_grad.astype(bf16).reshape(NXZ, NT * ROWS, 2 * FT...  9.56 us
  transfers between devices with their start and end apart: 80, of which 29 were waited for; matrix products, arithmetic and copies ran while one was open for 37% of the time, Pallas kernels for 4%

profile of v4, /device:TPU:1, one launch (start us, length us, event | category | flops | bytes accessed | tf_op | source)
XLA Modules:
  0.0 459.8 jit_solution(15776811074175396501)
XLA Ops:
  13.1 6.0 %all-to-all-start = ((bf16[8,16,896]{2,1,0:T(8,128)(2,1)}), bf16[8,16,896]{2,1,0:T(8,128)(2,1)S(1)}, u32[]{:S(2)}, u32[]{:S(2)}) async-start(bf16[8,16,896]{2,1,0:T(8,128)(2,1)} %pad_maximum_fusion.8), calls=%async_computation | async-start | bytes 458752 | tf_op jit(solution)/shard_map/all_to_all | solution.py:342
  20.6 3.5 collective-permute-start.9
  24.0 3.6 collective-permute-done.9
  35.1 7.8 %collective-permute-done.1 = bf16[128,2048]{1,0:T(8,128)(2,1)S(1)} collective-permute-done((bf16[128,2048]{1,0:T(8,128)(2,1)S(1)}, bf16[128,2048]{1,0:T(8,128)(2,1)S(1)}, u32[]{:S(2)}, u32[]{:S(2)}) %collective-permute-start.1) | collective-permute-done | bytes 524320 | tf_op jit(solution)/shard_map/ppermute | solution.py:60
  43.7 3.0 collective-permute-start.5
  49.3 4.0 collective-permute-done.4
  59.7 4.5 collective-permute-start.30
  65.7 3.8 all-to-all-start.1
  69.5 3.3 collective-permute-done.30
  74.5 3.1 all-to-all-done.1
  85.1 3.8 fusion.9
  88.9 2.8 convert_reduce_fusion
  91.7 3.4 fusion.2
  107.5 6.8 %fusion.6.proj_ref = f32[1024,768]{1,0:T(8,128)S(1)} fusion(bf16[2048,896]{1,0:T(8,128)(2,1)} %bitcast.366, f32[2048]{0:T(1024)S(1)} %bitcast.445, f32[2048]{0:T(1024)S(1)} %bitcast.436, bf16[1024,2048]{1,0:T(8,128)(2,1)} %bitcast.14, f32[1024]{0:T(1024)S(1)} %add_rsqrt_fusion, f32[1024]{0:T(1024)S(1)} %broadcast_multiply_fusion), kind=kOutput, calls=%fused_computation.24 | convolution fusion | flops 3233808384 | bytes 10510336 | tf_op jit(solution)/shard_map/td,de->te/dot_general | solution.py:306
  120.0 2.7 collective-permute-start.13
  124.9 6.3 %attention.1 = (f32[1024,768]{1,0:T(8,128)S(1)}, f32[1024,256]{1,0:T(8,128)S(1)}) custom-call(f32[1024,768]{1,0:T(8,128)S(1)} %fusion.6.proj_ref, f32[1,768]{1,0:T(1,128)S(1)} %convert.83.bias_ref, f32[1024,256]{1,0:T(8,128)S(1)} %get-tuple-element.182.cos_ref, f32[1024,256]{1,0:T(8,128)S(1)} %get-tuple-element.181.sin_ref, f32[1024,2]{1,0:T(8,128)S(1)} %copy.186.colq_ref, ...), custom_call_target="tpu_custom_call" | custom-call | flops 1073741824 | bytes 7340032 | tf_op jit(solution)/shard_map/attention/pallas_call | solution.py:278
  141.7 10.7 %collective-permute-done.20 = bf16[128,2048]{1,0:T(8,128)(2,1)S(1)} collective-permute-done((bf16[128,2048]{1,0:T(8,128)(2,1)S(1)}, bf16[128,2048]{1,0:T(8,128)(2,1)S(1)}, u32[]{:S(2)}, u32[]{:S(2)}) %collective-permute-start.20) | collective-permute-done | bytes 524320 | tf_op jit(solution)/shard_map/ppermute | solution.py:60
  152.5 11.6 %collective-permute-done.21 = bf16[128,2048]{1,0:T(8,128)(2,1)S(1)} collective-permute-done((bf16[128,2048]{1,0:T(8,128)(2,1)S(1)}, bf16[128,2048]{1,0:T(8,128)(2,1)S(1)}, u32[]{:S(2)}, u32[]{:S(2)}) %collective-permute-start.21) | collective-permute-done | bytes 524320 | tf_op jit(solution)/shard_map/ppermute | solution.py:60
  173.7 3.4 slice.277
  180.4 3.8 collective-permute-done.28
  187.3 2.8 collective-permute-start.34
  191.2 4.9 %collective-permute-done.33 = bf16[64,2048]{1,0:T(8,128)(2,1)S(1)} collective-permute-done((bf16[64,2048]{1,0:T(8,128)(2,1)S(1)}, bf16[64,2048]{1,0:T(8,128)(2,1)S(1)}, u32[]{:S(2)}, u32[]{:S(2)}) %collective-permute-start.33) | collective-permute-done | bytes 262176 | tf_op jit(solution)/shard_map/ppermute | solution.py:60
  199.2 8.9 %fusion.62 = f32[1024,1536]{0,1:T(8,128)} fusion(bf16[1024,2048]{1,0:T(8,128)(2,1)S(1)} %bitcast.373, bf16[2048,1536]{1,0:T(8,128)(2,1)S(1)} %bitcast.361), kind=kOutput, calls=%fused_computation.226 | convolution fusion | flops 6442450944 | bytes 16777216 | tf_op jit(solution)/shard_map/td,de->te/dot_general | solution.py:306
  208.1 8.7 %multiply_convert_fusion.2 = (bf16[1024,768]{0,1:T(8,128)(2,1)S(1)}, bf16[1024,768]{0,1:T(8,128)(2,1)S(1)}, bf16[1024,768]{0,1:T(8,128)(2,1)}) fusion(f32[1024,1536]{0,1:T(8,128)} %fusion.62, bf16[1024,2048]{1,0:T(8,128)(2,1)S(1)} %bitcast.375, bf16[768,2048]{1,0:T(8,128)(2,1)} %bitcast.391), kind=kOutput, calls=%fused_computation.19 | convolution fusion | flops 3233021952 | bytes 18350080 | tf_op jit(solution)/shard_map/td,fd->tf/dot_general | solution.py:306
  216.7 8.3 %convolution_convert_fusion.1 = bf16[1024,2048]{1,0:T(8,128)(2,1)} fusion(bf16[2048,1536]{1,0:T(8,128)(2,1)S(1)} %bitcast.362, bf16[1024,768]{0,1:T(8,128)(2,1)S(1)} %get-tuple-element.127, bf16[1024,768]{0,1:T(8,128)(2,1)S(1)} %get-tuple-element.126), kind=kOutput, calls=%fused_computation.10 | convolution fusion | flops 6450839552 | bytes 13631488 | tf_op jit(solution)/shard_map/tf,df->td/dot_general | solution.py:306
  230.8 3.7 convolution_convert_fusion.5
  239.6 7.5 %convolution_convert_fusion = bf16[2048,1536]{1,0:T(8,128)(2,1)S(1)} fusion(bf16[1024,2048]{1,0:T(8,128)(2,1)S(1)} %bitcast.374, bf16[1024,1536]{0,1:T(8,128)(2,1)S(1)} %pad_maximum_fusion.1), kind=kOutput, calls=%fused_computation.8 | convolution fusion | flops 6445596672 | bytes 13631488 | tf_op jit(solution)/shard_map/td,tf->df/dot_general | solution.py:306
  247.1 9.6 %maximum_maximum_fusion = bf16[16,192,1536]{2,1,0:T(8,128)(2,1)} fusion(bf16[16,16,512]{2,1,0:T(8,128)(2,1)S(1)} %get-tuple-element.163, bf16[16,16,512]{2,1,0:T(8,128)(2,1)S(1)} %get-tuple-element.164, bf16[16,16,512]{2,1,0:T(8,128)(2,1)S(1)} %get-tuple-element.162, bf16[16,48,1536]{2,1,0:T(8,128)(2,1)S(1)} %slice.284, bf16[16,128,1536]{2,1,0:T(8,128)(2,1)S(1)} %bitcast.363), kind=kLoop, calls=%fused_computation.4 | loop fusion | flops 47185920 | bytes 18874368 | tf_op jit(solution)/shard_map/concatenate | solution.py:430
  256.7 4.7 %collective-permute-done.43 = bf16[128,2048]{1,0:T(8,128)(2,1)S(1)} collective-permute-done((bf16[128,2048]{1,0:T(8,128)(2,1)S(1)}, bf16[128,2048]{1,0:T(8,128)(2,1)S(1)}, u32[]{:S(2)}, u32[]{:S(2)}) %collective-permute-start.43) | collective-permute-done | bytes 524320 | tf_op jit(solution)/shard_map/ppermute | solution.py:60
  274.5 9.4 %collective-permute-done.46 = bf16[128,2048]{1,0:T(8,128)(2,1)} collective-permute-done((bf16[128,2048]{1,0:T(8,128)(2,1)}, bf16[128,2048]{1,0:T(8,128)(2,1)}, u32[]{:S(2)}, u32[]{:S(2)}) %collective-permute-start.46) | collective-permute-done | bytes 524320 | tf_op jit(solution)/shard_map/ppermute | solution.py:60
  303.8 3.9 fusion.63.grad_ref
  307.7 10.5 %attention_back.1 = (f32[1024,768]{1,0:T(8,128)S(1)}, f32[1,768]{1,0:T(1,128)S(1)}) custom-call(f32[1024,768]{1,0:T(8,128)S(1)} %copy-done.1, f32[1024,256]{1,0:T(8,128)S(1)} %fusion.63.grad_ref, f32[1024,256]{1,0:T(8,128)S(1)} %get-tuple-element.182.cos_ref, f32[1024,256]{1,0:T(8,128)S(1)} %get-tuple-element.181.sin_ref, f32[1024,2]{1,0:T(8,128)S(1)} %copy.186.colq_ref, ...), custom_call_target="tpu_custom_call" | custom-call | flops 2684354560 | bytes 6291456 | tf_op jit(solution)/shard_map/attention_back/pallas_call | solution.py:293
  320.3 8.7 %fusion.50 = (bf16[2048]{0:T(1024)(128)(2,1)S(1)}, bf16[2048]{0:T(1024)(128)(2,1)S(1)}, bf16[1024,2048]{1,0:T(8,128)(2,1)}, f32[1024,2048]{1,0:T(8,128)}) fusion(f32[1024]{0:T(1024)S(1)} %add_rsqrt_fusion, f32[1024]{0:T(1024)S(1)} %broadcast_multiply_fusion, bf16[1024,2048]{1,0:T(8,128)(2,1)} %bitcast.14, bf16[1024,768]{1,0:T(8,128)(2,1)S(1)} %convert_element_type.369, ...), kind=kOutput, calls=%fused_computation.216 | convolution fusion | flops 3235901440 | bytes 21512192 | tf_op jit(solution)/shard_map/te,de->td/dot_general | solution.py:306
  331.5 3.0 concatenate.93
  334.5 3.5 convolution_convert_fusion.6
  339.4 6.4 %convolution_convert_fusion.4 = bf16[2048,768]{1,0:T(8,128)(2,1)S(1)} fusion(bf16[1024,768]{1,0:T(8,128)(2,1)S(1)} %copy-done.28, f32[2048]{0:T(1024)S(1)} %bitcast.446, f32[2048]{0:T(1024)S(1)} %bitcast.437, bf16[1024,2048]{1,0:T(8,128)(2,1)} %bitcast.14, f32[1024]{0:T(1024)S(1)} %add_rsqrt_fusion, f32[1024]{0:T(1024)S(1)} %broadcast_multiply_fusion), kind=kOutput, calls=%fused_computation.13 | convolution fusion | flops 3235381248 | bytes 8937472 | tf_op jit(solution)/shard_map/td,te->de/dot_general | solution.py:306
  348.3 3.9 reduce-scatter.3.cloned.1.call-done
  355.6 5.7 %collective-permute-start.71 = (bf16[44,2048]{1,0:T(8,128)(2,1)}, bf16[44,2048]{1,0:T(8,128)(2,1)}, u32[]{:S(2)}, u32[]{:S(2)}) collective-permute-start(bf16[44,2048]{1,0:T(8,128)(2,1)} %pad_maximum_fusion.9), channel_id=1, source_target_pairs={{0,0},{1,16},{2,1},{3,17},{4,2},{5,18},{6,3},{7,19},{8,4},{9,20},{... | collective-permute-start | bytes 540680 | tf_op jit(solution)/shard_map/ppermute | solution.py:477
  361.3 2.9 dynamic-slice_bitcast_fusion.3
  365.5 4.4 all-to-all-start.3
  369.9 5.1 %convolution_convert_fusion.3 = bf16[1024,2048]{1,0:T(8,128)(2,1)S(1)} fusion(bf16[1024,768]{0,1:T(8,128)(2,1)} %get-tuple-element.100, bf16[768,2048]{1,0:T(8,128)(2,1)S(1)} %bitcast.392), kind=kOutput, calls=%fused_computation.12 | convolution fusion | flops 3223322624 | bytes 8912896 | tf_op jit(solution)/shard_map/tf,fd->td/dot_general | solution.py:306
  390.9 4.3 collective-permute-done.65
  396.9 4.0 collective-permute-done.57
  405.2 5.5 %collective-permute-done.66 = bf16[128,2048]{1,0:T(8,128)(2,1)S(1)} collective-permute-done((bf16[128,2048]{1,0:T(8,128)(2,1)S(1)}, bf16[128,2048]{1,0:T(8,128)(2,1)S(1)}, u32[]{:S(2)}, u32[]{:S(2)}) %collective-permute-start.66) | collective-permute-done | bytes 524320 | tf_op jit(solution)/shard_map/ppermute | solution.py:60
  414.9 7.0 %collective-permute-done.58 = bf16[128,2048]{1,0:T(8,128)(2,1)S(1)} collective-permute-done((bf16[128,2048]{1,0:T(8,128)(2,1)S(1)}, bf16[128,2048]{1,0:T(8,128)(2,1)S(1)}, u32[]{:S(2)}, u32[]{:S(2)}) %collective-permute-start.58) | collective-permute-done | bytes 524320 | tf_op jit(solution)/shard_map/ppermute | solution.py:60
  428.7 4.1 reduce-scatter.5.cloned.1.call-done
  435.2 6.6 %all-to-all-start.2 = ((bf16[8,16,896]{2,1,0:T(8,128)(2,1)}), bf16[8,16,896]{2,1,0:T(8,128)(2,1)S(1)}, u32[]{:S(2)}, u32[]{:S(2)}) async-start(bf16[8,16,896]{2,1,0:T(8,128)(2,1)} %bitcast.151), calls=%async_computation.4 | async-start | bytes 458752 | tf_op jit(solution)/shard_map/all_to_all | solution.py:491
  441.8 4.1 collective-permute-start.70
  (416 shorter events, 184.2 us)
Async XLA Ops:
  13.1 14.5 %all-to-all-start = ((bf16[8,16,896]{2,1,0:T(8,128)(2,1)}), bf16[8,16,896]{2,1,0:T(8,128)(2,1)S(1)}, u32[]{:S(2)}, u32[]{:S(2)}) async-start(bf16[8,16,896]{2,1,0:T(8,128)(2,1)} %pad_maximum_fusion.8), calls=%async_computation | async-start | bytes 458752 | tf_op jit(solution)/shard_map/all_to_all | solution.py:342
  19.1 76.1 %all-gather.5.cloned.1.call-start = ((), (), s32[]{:S(2)}) async-start(), calls=%async_computation.8 | async-start | bytes 5013504 | tf_op jit(solution)/shard_map/all_gather | solution.py:357
  29.0 14.0 %collective-permute-start.1 = (bf16[128,2048]{1,0:T(8,128)(2,1)S(1)}, bf16[128,2048]{1,0:T(8,128)(2,1)S(1)}, u32[]{:S(2)}, u32[]{:S(2)}) collective-permute-start(bf16[128,2048]{1,0:T(8,128)(2,1)S(1)} %copy.172), channel_id=1, source_target_pairs={{0,32},{32,64},{64,96},{96,0},{1,33},{33,65},{65,97},{97,1},{2,34}... | collective-permute-start | bytes 1572872 | tf_op jit(solution)/shard_map/ppermute | solution.py:60
  30.4 12.6 %collective-permute-start.2 = (bf16[128,2048]{1,0:T(8,128)(2,1)S(1)}, bf16[128,2048]{1,0:T(8,128)(2,1)S(1)}, u32[]{:S(2)}, u32[]{:S(2)}) collective-permute-start(bf16[128,2048]{1,0:T(8,128)(2,1)S(1)} %copy.172), channel_id=1, source_target_pairs={{0,96},{32,0},{64,32},{96,64},{1,97},{33,1},{65,33},{97,65},{2,98}... | collective-permute-start | bytes 1572872 | tf_op jit(solution)/shard_map/ppermute | solution.py:60
  31.7 14.9 %collective-permute-start = (bf16[128,2048]{1,0:T(8,128)(2,1)S(1)}, bf16[128,2048]{1,0:T(8,128)(2,1)}, u32[]{:S(2)}, u32[]{:S(2)}) collective-permute-start(bf16[128,2048]{1,0:T(8,128)(2,1)S(1)} %copy.172), channel_id=1, source_target_pairs={{0,1},{1,0},{2,3},{3,2},{4,5},{5,4},{6,7},{7,6},{8,9},{9,8},{10,11... | collective-permute-start | bytes 1572872 | tf_op jit(solution)/shard_map/ppermute | solution.py:60
  43.0 10.9 %collective-permute-start.3 = (bf16[128,2048]{1,0:T(8,128)(2,1)S(1)}, bf16[128,2048]{1,0:T(8,128)(2,1)S(1)}, u32[]{:S(2)}, u32[]{:S(2)}) collective-permute-start(bf16[128,2048]{1,0:T(8,128)(2,1)S(1)} %collective-permute-done.2), channel_id=1, source_target_pairs={{0,1},{1,0},{2,3},{3,2},{4,5},{5,4},{6,7},{7,6},{8,9},{9,8},{10,11... | collective-permute-start | bytes 1572872 | tf_op jit(solution)/shard_map/ppermute | solution.py:60
  43.1 15.4 %collective-permute-start.8 = (bf16[128,2048]{1,0:T(8,128)(2,1)S(1)}, bf16[128,2048]{1,0:T(8,128)(2,1)S(1)}, u32[]{:S(2)}, u32[]{:S(2)}) collective-permute-start(bf16[128,2048]{1,0:T(8,128)(2,1)S(1)} %collective-permute-done.1), channel_id=1, source_target_pairs={{0,1},{1,0},{2,3},{3,2},{4,5},{5,4},{6,7},{7,6},{8,9},{9,8},{10,11... | collective-permute-start | bytes 1572872 | tf_op jit(solution)/shard_map/ppermute | solution.py:60
  59.7 13.1 %collective-permute-start.30 = (bf16[44,2048]{1,0:T(8,128)(2,1)S(1)}, bf16[44,2048]{1,0:T(8,128)(2,1)S(1)}, u32[]{:S(2)}, u32[]{:S(2)}) collective-permute-start(bf16[44,2048]{1,0:T(8,128)(2,1)S(1)} %copy-done.35), channel_id=1, source_target_pairs={{0,0},{16,1},{1,2},{17,3},{2,4},{18,5},{3,6},{19,7},{4,8},{20,9},{... | collective-permute-start | bytes 540680 | tf_op jit(solution)/shard_map/ppermute | solution.py:372
  65.7 11.9 %all-to-all-start.1 = ((bf16[8,16,1536]{2,1,0:T(8,128)(2,1)}), bf16[8,16,1536]{2,1,0:T(8,128)(2,1)S(1)}, u32[]{:S(2)}, u32[]{:S(2)}) async-start(bf16[8,16,1536]{2,1,0:T(8,128)(2,1)} %pad_maximum_fusion.6), calls=%async_computation.1 | async-start | bytes 786432 | tf_op jit(solution)/shard_map/all_to_all | solution.py:371
  69.5 102.4 %all-gather.7.cloned.1.call-start = ((), (), s32[]{:S(2)}) async-start(), calls=%async_computation.9 | async-start | bytes 10027008 | tf_op jit(solution)/shard_map/all_gather | solution.py:385
  78.5 273.7 %reduce-scatter.3.cloned.1.call-start = ((), (), s32[]{:S(2)}) async-start(), calls=%async_computation.6 | async-start | bytes 10027008 | tf_op jit(solution)/shard_map/reduce_scatter | solution.py:438
  95.1 21.9 %collective-permute-start.10 = (bf16[128,2048]{1,0:T(8,128)(2,1)}, bf16[128,2048]{1,0:T(8,128)(2,1)}, u32[]{:S(2)}, u32[]{:S(2)}) collective-permute-start(bf16[128,2048]{1,0:T(8,128)(2,1)} %copy.175), channel_id=1, source_target_pairs={{0,32},{32,64},{64,96},{96,0},{1,33},{33,65},{65,97},{97,1},{2,34}... | collective-permute-start | bytes 1572872 | tf_op jit(solution)/shard_map/ppermute | solution.py:60
  95.5 21.5 %collective-permute-start.11 = (bf16[128,2048]{1,0:T(8,128)(2,1)}, bf16[128,2048]{1,0:T(8,128)(2,1)}, u32[]{:S(2)}, u32[]{:S(2)}) collective-permute-start(bf16[128,2048]{1,0:T(8,128)(2,1)} %copy.175), channel_id=1, source_target_pairs={{0,96},{32,0},{64,32},{96,64},{1,97},{33,1},{65,33},{97,65},{2,98}... | collective-permute-start | bytes 1572872 | tf_op jit(solution)/shard_map/ppermute | solution.py:60
  97.9 24.8 %collective-permute-start.23 = (bf16[128,2048]{1,0:T(8,128)(2,1)}, bf16[128,2048]{1,0:T(8,128)(2,1)}, u32[]{:S(2)}, u32[]{:S(2)}) collective-permute-start(bf16[128,2048]{1,0:T(8,128)(2,1)} %copy.175), channel_id=1, source_target_pairs={{0,1},{1,0},{2,3},{3,2},{4,5},{5,4},{6,7},{7,6},{8,9},{9,8},{10,11... | collective-permute-start | bytes 1572872 | tf_op jit(solution)/shard_map/ppermute | solution.py:60
  117.0 17.1 %collective-permute-start.24 = (bf16[128,2048]{1,0:T(8,128)(2,1)}, bf16[128,2048]{1,0:T(8,128)(2,1)S(1)}, u32[]{:S(2)}, u32[]{:S(2)}) collective-permute-start(bf16[128,2048]{1,0:T(8,128)(2,1)} %collective-permute-done.11), channel_id=1, source_target_pairs={{0,1},{1,0},{2,3},{3,2},{4,5},{5,4},{6,7},{7,6},{8,9},{9,8},{10,11... | collective-permute-start | bytes 1572872 | tf_op jit(solution)/shard_map/ppermute | solution.py:60
  119.5 22.2 %collective-permute-start.27 = (bf16[128,2048]{1,0:T(8,128)(2,1)}, bf16[128,2048]{1,0:T(8,128)(2,1)S(1)}, u32[]{:S(2)}, u32[]{:S(2)}) collective-permute-start(bf16[128,2048]{1,0:T(8,128)(2,1)} %collective-permute-done.10), channel_id=1, source_target_pairs={{0,1},{1,0},{2,3},{3,2},{4,5},{5,4},{6,7},{7,6},{8,9},{9,8},{10,11... | collective-permute-start | bytes 1572872 | tf_op jit(solution)/shard_map/ppermute | solution.py:60
  120.0 11.2 %collective-permute-start.12 = (bf16[64,2048]{1,0:T(8,128)(2,1)S(1)}, bf16[64,2048]{1,0:T(8,128)(2,1)S(1)}, u32[]{:S(2)}, u32[]{:S(2)}) collective-permute-start(bf16[64,2048]{1,0:T(8,128)(2,1)S(1)} %slice.212), channel_id=1, source_target_pairs={{0,32},{32,64},{64,96},{96,0},{1,33},{33,65},{65,97},{97,1},{2,34}... | collective-permute-start | bytes 786440 | tf_op jit(solution)/shard_map/ppermute | solution.py:60
  120.0 11.2 %collective-permute-start.13 = (bf16[64,2048]{1,0:T(8,128)(2,1)S(1)}, bf16[64,2048]{1,0:T(8,128)(2,1)S(1)}, u32[]{:S(2)}, u32[]{:S(2)}) collective-permute-start(bf16[64,2048]{1,0:T(8,128)(2,1)S(1)} %slice.213), channel_id=1, source_target_pairs={{0,96},{32,0},{64,32},{96,64},{1,97},{33,1},{65,33},{97,65},{2,98}... | collective-permute-start | bytes 786440 | tf_op jit(solution)/shard_map/ppermute | solution.py:60
  137.7 14.8 %collective-permute-start.20 = (bf16[128,2048]{1,0:T(8,128)(2,1)S(1)}, bf16[128,2048]{1,0:T(8,128)(2,1)S(1)}, u32[]{:S(2)}, u32[]{:S(2)}) collective-permute-start(bf16[128,2048]{1,0:T(8,128)(2,1)S(1)} %get-tuple-element.71), channel_id=1, source_target_pairs={{0,64},{32,96},{64,0},{96,32},{1,65},{33,97},{65,1},{97,33},{2,66}... | collective-permute-start | bytes 1572872 | tf_op jit(solution)/shard_map/ppermute | solution.py:60
  137.8 26.3 %collective-permute-start.21 = (bf16[128,2048]{1,0:T(8,128)(2,1)S(1)}, bf16[128,2048]{1,0:T(8,128)(2,1)S(1)}, u32[]{:S(2)}, u32[]{:S(2)}) collective-permute-start(bf16[128,2048]{1,0:T(8,128)(2,1)S(1)} %get-tuple-element.72), channel_id=1, source_target_pairs={{0,32},{32,64},{64,96},{96,0},{1,33},{33,65},{65,97},{97,1},{2,34}... | collective-permute-start | bytes 1572872 | tf_op jit(solution)/shard_map/ppermute | solution.py:60
  139.1 25.0 %collective-permute-start.22 = (bf16[128,2048]{1,0:T(8,128)(2,1)S(1)}, bf16[128,2048]{1,0:T(8,128)(2,1)S(1)}, u32[]{:S(2)}, u32[]{:S(2)}) collective-permute-start(bf16[128,2048]{1,0:T(8,128)(2,1)S(1)} %get-tuple-element.73), channel_id=1, source_target_pairs={{0,96},{32,0},{64,32},{96,64},{1,97},{33,1},{65,33},{97,65},{2,98}... | collective-permute-start | bytes 1572872 | tf_op jit(solution)/shard_map/ppermute | solution.py:60
  168.6 16.4 %collective-permute-start.31 = (bf16[128,2048]{1,0:T(8,128)(2,1)}, bf16[128,2048]{1,0:T(8,128)(2,1)}, u32[]{:S(2)}, u32[]{:S(2)}) collective-permute-start(bf16[128,2048]{1,0:T(8,128)(2,1)} %get-tuple-element.123), channel_id=1, source_target_pairs={{0,1},{1,0},{2,3},{3,2},{4,5},{5,4},{6,7},{7,6},{8,9},{9,8},{10,11... | collective-permute-start | bytes 1572872 | tf_op jit(solution)/shard_map/ppermute | solution.py:60
  169.2 15.0 %collective-permute-start.28 = (bf16[128,2048]{1,0:T(8,128)(2,1)}, bf16[128,2048]{1,0:T(8,128)(2,1)S(1)}, u32[]{:S(2)}, u32[]{:S(2)}) collective-permute-start(bf16[128,2048]{1,0:T(8,128)(2,1)} %get-tuple-element.123), channel_id=1, source_target_pairs={{0,32},{32,64},{64,96},{96,0},{1,33},{33,65},{65,97},{97,1},{2,34}... | collective-permute-start | bytes 1572872 | tf_op jit(solution)/shard_map/ppermute | solution.py:60
  169.2 15.0 %collective-permute-start.29 = (bf16[128,2048]{1,0:T(8,128)(2,1)}, bf16[128,2048]{1,0:T(8,128)(2,1)}, u32[]{:S(2)}, u32[]{:S(2)}) collective-permute-start(bf16[128,2048]{1,0:T(8,128)(2,1)} %get-tuple-element.123), channel_id=1, source_target_pairs={{0,96},{32,0},{64,32},{96,64},{1,97},{33,1},{65,33},{97,65},{2,98}... | collective-permute-start | bytes 1572872 | tf_op jit(solution)/shard_map/ppermute | solution.py:60
  184.2 13.3 %collective-permute-start.32 = (bf16[128,2048]{1,0:T(8,128)(2,1)}, bf16[128,2048]{1,0:T(8,128)(2,1)S(1)}, u32[]{:S(2)}, u32[]{:S(2)}) collective-permute-start(bf16[128,2048]{1,0:T(8,128)(2,1)} %collective-permute-done.29), channel_id=1, source_target_pairs={{0,1},{1,0},{2,3},{3,2},{4,5},{5,4},{6,7},{7,6},{8,9},{9,8},{10,11... | collective-permute-start | bytes 1572872 | tf_op jit(solution)/shard_map/ppermute | solution.py:60
  187.1 12.0 %collective-permute-start.37 = (bf16[128,2048]{1,0:T(8,128)(2,1)S(1)}, bf16[128,2048]{1,0:T(8,128)(2,1)S(1)}, u32[]{:S(2)}, u32[]{:S(2)}) collective-permute-start(bf16[128,2048]{1,0:T(8,128)(2,1)S(1)} %collective-permute-done.28), channel_id=1, source_target_pairs={{0,1},{1,0},{2,3},{3,2},{4,5},{5,4},{6,7},{7,6},{8,9},{9,8},{10,11... | collective-permute-start | bytes 1572872 | tf_op jit(solution)/shard_map/ppermute | solution.py:60
  227.7 29.0 %collective-permute-start.38 = (bf16[128,2048]{1,0:T(8,128)(2,1)S(1)}, bf16[128,2048]{1,0:T(8,128)(2,1)S(1)}, u32[]{:S(2)}, u32[]{:S(2)}) collective-permute-start(bf16[128,2048]{1,0:T(8,128)(2,1)S(1)} %get-tuple-element.148), channel_id=1, source_target_pairs={{0,1},{1,0},{2,3},{3,2},{4,5},{5,4},{6,7},{7,6},{8,9},{9,8},{10,11... | collective-permute-start | bytes 1572872 | tf_op jit(solution)/shard_map/ppermute | solution.py:60
  234.7 21.9 %collective-permute-start.42 = (bf16[128,2048]{1,0:T(8,128)(2,1)S(1)}, bf16[128,2048]{1,0:T(8,128)(2,1)S(1)}, u32[]{:S(2)}, u32[]{:S(2)}) collective-permute-start(bf16[128,2048]{1,0:T(8,128)(2,1)S(1)} %get-tuple-element.83), channel_id=1, source_target_pairs={{0,64},{32,96},{64,0},{96,32},{1,65},{33,97},{65,1},{97,33},{2,66}... | collective-permute-start | bytes 1572872 | tf_op jit(solution)/shard_map/ppermute | solution.py:60
  236.9 24.5 %collective-permute-start.43 = (bf16[128,2048]{1,0:T(8,128)(2,1)S(1)}, bf16[128,2048]{1,0:T(8,128)(2,1)S(1)}, u32[]{:S(2)}, u32[]{:S(2)}) collective-permute-start(bf16[128,2048]{1,0:T(8,128)(2,1)S(1)} %get-tuple-element.84), channel_id=1, source_target_pairs={{0,32},{32,64},{64,96},{96,0},{1,33},{33,65},{65,97},{97,1},{2,34}... | collective-permute-start | bytes 1572872 | tf_op jit(solution)/shard_map/ppermute | solution.py:60
  237.6 23.8 %collective-permute-start.44 = (bf16[128,2048]{1,0:T(8,128)(2,1)S(1)}, bf16[128,2048]{1,0:T(8,128)(2,1)S(1)}, u32[]{:S(2)}, u32[]{:S(2)}) collective-permute-start(bf16[128,2048]{1,0:T(8,128)(2,1)S(1)} %get-tuple-element.85), channel_id=1, source_target_pairs={{0,96},{32,0},{64,32},{96,64},{1,97},{33,1},{65,33},{97,65},{2,98}... | collective-permute-start | bytes 1572872 | tf_op jit(solution)/shard_map/ppermute | solution.py:60
  262.8 169.9 %reduce-scatter.5.cloned.1.call-start = ((), (), s32[]{:S(2)}) async-start(), calls=%async_computation.7 | async-start | bytes 5013504 | tf_op jit(solution)/shard_map/reduce_scatter | solution.py:468
  269.3 14.5 %collective-permute-start.46 = (bf16[128,2048]{1,0:T(8,128)(2,1)}, bf16[128,2048]{1,0:T(8,128)(2,1)}, u32[]{:S(2)}, u32[]{:S(2)}) collective-permute-start(bf16[128,2048]{1,0:T(8,128)(2,1)} %get-tuple-element.120), channel_id=1, source_target_pairs={{0,32},{32,64},{64,96},{96,0},{1,33},{33,65},{65,97},{97,1},{2,34}... | collective-permute-start | bytes 1572872 | tf_op jit(solution)/shard_map/ppermute | solution.py:60
  269.7 14.2 %collective-permute-start.47 = (bf16[128,2048]{1,0:T(8,128)(2,1)}, bf16[128,2048]{1,0:T(8,128)(2,1)}, u32[]{:S(2)}, u32[]{:S(2)}) collective-permute-start(bf16[128,2048]{1,0:T(8,128)(2,1)} %get-tuple-element.120), channel_id=1, source_target_pairs={{0,96},{32,0},{64,32},{96,64},{1,97},{33,1},{65,33},{97,65},{2,98}... | collective-permute-start | bytes 1572872 | tf_op jit(solution)/shard_map/ppermute | solution.py:60
  272.0 18.1 %collective-permute-start.45 = (bf16[128,2048]{1,0:T(8,128)(2,1)}, bf16[128,2048]{1,0:T(8,128)(2,1)}, u32[]{:S(2)}, u32[]{:S(2)}) collective-permute-start(bf16[128,2048]{1,0:T(8,128)(2,1)} %get-tuple-element.120), channel_id=1, source_target_pairs={{0,1},{1,0},{2,3},{3,2},{4,5},{5,4},{6,7},{7,6},{8,9},{9,8},{10,11... | collective-permute-start | bytes 1572872 | tf_op jit(solution)/shard_map/ppermute | solution.py:60
  283.9 13.4 %collective-permute-start.48 = (bf16[128,2048]{1,0:T(8,128)(2,1)}, bf16[128,2048]{1,0:T(8,128)(2,1)S(1)}, u32[]{:S(2)}, u32[]{:S(2)}) collective-permute-start(bf16[128,2048]{1,0:T(8,128)(2,1)} %collective-permute-done.47), channel_id=1, source_target_pairs={{0,1},{1,0},{2,3},{3,2},{4,5},{5,4},{6,7},{7,6},{8,9},{9,8},{10,11... | collective-permute-start | bytes 1572872 | tf_op jit(solution)/shard_map/ppermute | solution.py:60
  287.2 15.8 %collective-permute-start.53 = (bf16[128,2048]{1,0:T(8,128)(2,1)}, bf16[128,2048]{1,0:T(8,128)(2,1)S(1)}, u32[]{:S(2)}, u32[]{:S(2)}) collective-permute-start(bf16[128,2048]{1,0:T(8,128)(2,1)} %collective-permute-done.46), channel_id=1, source_target_pairs={{0,1},{1,0},{2,3},{3,2},{4,5},{5,4},{6,7},{7,6},{8,9},{9,8},{10,11... | collective-permute-start | bytes 1572872 | tf_op jit(solution)/shard_map/ppermute | solution.py:60
  355.6 22.8 %collective-permute-start.71 = (bf16[44,2048]{1,0:T(8,128)(2,1)}, bf16[44,2048]{1,0:T(8,128)(2,1)}, u32[]{:S(2)}, u32[]{:S(2)}) collective-permute-start(bf16[44,2048]{1,0:T(8,128)(2,1)} %pad_maximum_fusion.9), channel_id=1, source_target_pairs={{0,0},{1,16},{2,1},{3,17},{4,2},{5,18},{6,3},{7,19},{8,4},{9,20},{... | collective-permute-start | bytes 540680 | tf_op jit(solution)/shard_map/ppermute | solution.py:477
  364.2 17.9 %collective-permute-start.63 = (bf16[128,2048]{1,0:T(8,128)(2,1)}, bf16[128,2048]{1,0:T(8,128)(2,1)}, u32[]{:S(2)}, u32[]{:S(2)}) collective-permute-start(bf16[128,2048]{1,0:T(8,128)(2,1)} %get-tuple-element.137), channel_id=1, source_target_pairs={{0,1},{1,0},{2,3},{3,2},{4,5},{5,4},{6,7},{7,6},{8,9},{9,8},{10,11... | collective-permute-start | bytes 1572872 | tf_op jit(solution)/shard_map/ppermute | solution.py:60
  364.2 18.5 %collective-permute-start.64 = (bf16[128,2048]{1,0:T(8,128)(2,1)}, bf16[128,2048]{1,0:T(8,128)(2,1)}, u32[]{:S(2)}, u32[]{:S(2)}) collective-permute-start(bf16[128,2048]{1,0:T(8,128)(2,1)} %get-tuple-element.136), channel_id=1, source_target_pairs={{0,1},{1,0},{2,3},{3,2},{4,5},{5,4},{6,7},{7,6},{8,9},{9,8},{10,11... | collective-permute-start | bytes 1572872 | tf_op jit(solution)/shard_map/ppermute | solution.py:60
  364.8 18.1 %collective-permute-start.67 = (bf16[128,2048]{1,0:T(8,128)(2,1)}, bf16[128,2048]{1,0:T(8,128)(2,1)}, u32[]{:S(2)}, u32[]{:S(2)}) collective-permute-start(bf16[128,2048]{1,0:T(8,128)(2,1)} %get-tuple-element.135), channel_id=1, source_target_pairs={{0,1},{1,0},{2,3},{3,2},{4,5},{5,4},{6,7},{7,6},{8,9},{9,8},{10,11... | collective-permute-start | bytes 1572872 | tf_op jit(solution)/shard_map/ppermute | solution.py:60
  365.0 37.7 %collective-permute-start.62 = (bf16[128,2048]{1,0:T(8,128)(2,1)}, bf16[128,2048]{1,0:T(8,128)(2,1)}, u32[]{:S(2)}, u32[]{:S(2)}) collective-permute-start(bf16[128,2048]{1,0:T(8,128)(2,1)} %get-tuple-element.134), channel_id=1, source_target_pairs={{0,1},{1,0},{2,3},{3,2},{4,5},{5,4},{6,7},{7,6},{8,9},{9,8},{10,11... | collective-permute-start | bytes 1572872 | tf_op jit(solution)/shard_map/ppermute | solution.py:60
  365.5 16.2 %all-to-all-start.3 = ((bf16[8,16,1536]{2,1,0:T(8,128)(2,1)}), bf16[8,16,1536]{2,1,0:T(8,128)(2,1)S(1)}, u32[]{:S(2)}, u32[]{:S(2)}) async-start(bf16[8,16,1536]{2,1,0:T(8,128)(2,1)} %bitcast.408), calls=%async_computation.5 | async-start | bytes 786432 | tf_op jit(solution)/shard_map/all_to_all | solution.py:479
  382.8 32.1 %collective-permute-start.54 = (bf16[128,2048]{1,0:T(8,128)(2,1)}, bf16[128,2048]{1,0:T(8,128)(2,1)S(1)}, u32[]{:S(2)}, u32[]{:S(2)}) collective-permute-start(bf16[128,2048]{1,0:T(8,128)(2,1)} %get-tuple-element.141), channel_id=1, source_target_pairs={{0,1},{1,0},{2,3},{3,2},{4,5},{5,4},{6,7},{7,6},{8,9},{9,8},{10,11... | collective-permute-start | bytes 1572872 | tf_op jit(solution)/shard_map/ppermute | solution.py:60
  396.6 14.1 %collective-permute-start.66 = (bf16[128,2048]{1,0:T(8,128)(2,1)S(1)}, bf16[128,2048]{1,0:T(8,128)(2,1)S(1)}, u32[]{:S(2)}, u32[]{:S(2)}) collective-permute-start(bf16[128,2048]{1,0:T(8,128)(2,1)S(1)} %pad_maximum_fusion.4), channel_id=1, source_target_pairs={{0,32},{32,64},{64,96},{96,0},{1,33},{33,65},{65,97},{97,1},{2,34}... | collective-permute-start | bytes 1572872 | tf_op jit(solution)/shard_map/ppermute | solution.py:60
  400.9 12.0 %collective-permute-start.69 = (bf16[128,2048]{1,0:T(8,128)(2,1)S(1)}, bf16[128,2048]{1,0:T(8,128)(2,1)S(1)}, u32[]{:S(2)}, u32[]{:S(2)}) collective-permute-start(bf16[128,2048]{1,0:T(8,128)(2,1)S(1)} %pad_maximum_fusion.5), channel_id=1, source_target_pairs={{0,96},{32,0},{64,32},{96,64},{1,97},{33,1},{65,33},{97,65},{2,98}... | collective-permute-start | bytes 1572872 | tf_op jit(solution)/shard_map/ppermute | solution.py:60
  402.3 19.7 %collective-permute-start.58 = (bf16[128,2048]{1,0:T(8,128)(2,1)S(1)}, bf16[128,2048]{1,0:T(8,128)(2,1)S(1)}, u32[]{:S(2)}, u32[]{:S(2)}) collective-permute-start(bf16[128,2048]{1,0:T(8,128)(2,1)S(1)} %pad_maximum_fusion.2), channel_id=1, source_target_pairs={{0,32},{32,64},{64,96},{96,0},{1,33},{33,65},{65,97},{97,1},{2,34}... | collective-permute-start | bytes 1572872 | tf_op jit(solution)/shard_map/ppermute | solution.py:60
  402.6 21.5 %collective-permute-start.61 = (bf16[128,2048]{1,0:T(8,128)(2,1)S(1)}, bf16[128,2048]{1,0:T(8,128)(2,1)S(1)}, u32[]{:S(2)}, u32[]{:S(2)}) collective-permute-start(bf16[128,2048]{1,0:T(8,128)(2,1)S(1)} %pad_maximum_fusion.3), channel_id=1, source_target_pairs={{0,96},{32,0},{64,32},{96,64},{1,97},{33,1},{65,33},{97,65},{2,98}... | collective-permute-start | bytes 1572872 | tf_op jit(solution)/shard_map/ppermute | solution.py:60
  435.2 14.7 %all-to-all-start.2 = ((bf16[8,16,896]{2,1,0:T(8,128)(2,1)}), bf16[8,16,896]{2,1,0:T(8,128)(2,1)S(1)}, u32[]{:S(2)}, u32[]{:S(2)}) async-start(bf16[8,16,896]{2,1,0:T(8,128)(2,1)} %bitcast.151), calls=%async_computation.4 | async-start | bytes 458752 | tf_op jit(solution)/shard_map/all_to_all | solution.py:491
  (70 other events, 558.9 us)
Sparse Core Ops, SparseCore 0:
  28.5 60.9 all-gather.4
  91.7 75.7 all-gather.6
  262.9 89.1 reduce-scatter.2
  355.7 76.9 reduce-scatter.4
